TPU v7x, 32 devices: a whole 2x2x4 slice. The times are simulated.
32 devices in a mesh: pipe: 2 (over x), dp: 16 (over z, y, core).
Axes of the slice: x: 2, y: 2, z: 4, core: 2. Of those that a mesh axis runs over, the one named last changes fastest.
Arguments:
- embeddings: bfloat16 [2, 32768, 512], P('pipe', 'dp'), may hold values from -6 to 6
- cotangent: bfloat16 [32768, 512], P('dp'), may hold values from -6 to 6
- lengths: int32 [32, 17], P('dp'), may hold values from 20 to 100, as said below
- copy_index: int32 [32768], P('dp'), may hold values from 0 to 1023, as said below
- priority: int32 [32768], P('dp'), may hold values from 0 to 99, as said below
- hamming: int32 [32, 17], P('dp'), may hold values from 0 to 100, as said below
- self_in: bfloat16 [2, 512, 1536], P('pipe'), may hold values from -0.25 to 0.25
- self_out: bfloat16 [2, 512, 512], P('pipe'), may hold values from -0.75 to 0.75
- cross_weight: bfloat16 [2, 512, 1024], P('pipe'), may hold values from -0.375 to 0.375
- expand: bfloat16 [2, 512, 2048], P('pipe'), may hold values from -0.25 to 0.25
- contract: bfloat16 [2, 2048, 512], P('pipe'), may hold values from -0.125 to 0.125
- expand_bias: float32 [2, 2048], P('pipe'), may hold values from -1.75 to 1.75
- branch_bias: float32 [2, 3, 512], P('pipe'), may hold values from -1.75 to 1.75
- norm_gain: float32 [2, 3, 512], P('pipe'), may hold values from 0.5 to 1.5
- norm_shift: float32 [2, 3, 512], P('pipe'), may hold values from -0.625 to 0.625
Outputs:
- layer_out: float32 [2, 32768, 512], P('pipe', 'dp')
- embedding_grad: float32 [2, 32768, 512], P('pipe', 'dp')
- self_in_grad: float32 [2, 512, 1536], P('pipe')
- self_out_grad: float32 [2, 512, 512], P('pipe')
- cross_grad: float32 [2, 512, 1024], P('pipe')
- expand_grad: float32 [2, 512, 2048], P('pipe')
- contract_grad: float32 [2, 2048, 512], P('pipe')
- expand_bias_grad: float32 [2, 2048], P('pipe')
- branch_bias_grad: float32 [2, 3, 512], P('pipe')
- norm_gain_grad: float32 [2, 3, 512], P('pipe')
- norm_shift_grad: float32 [2, 3, 512], P('pipe')
Inputs may be any that keep to these rules, and one draw needn't show every extreme that they name: Each row holds 17 sentences whose lengths sum to 1024; every row has a sentence of 100 tokens. `copy_index`: A position of a token of the same sentence, counted from the row's start; the first and last positions of each row copy themselves. `priority`: within each sentence the entries are 0 to its length minus 1, each once. `hamming`: entry j belongs to sentence j of the row and is at most that sentence's length; a sentence of 100 tokens has the count 100.
All inputs are finite; a program needn't handle non-finite values.
Results may differ from a plain program's by a relative error of at most 0.025.
Values may be sent and summed in bfloat16 or wider, within the bound.
No kernel may reach another device: no remote copies, remote signals or barrier semaphores. Data moves between devices by JAX's collectives and lax.ppermute only.
A program may use at most 384 MiB of HBM per device.

v0:
```python
import jax
import jax.numpy as jnp
from jax import lax
from jax.sharding import PartitionSpec as P

HEADS = 8
ROW_LEN = 1024
MB = 2


PRECISION = lax.Precision.DEFAULT
EPSILON = 1e-05


def for_sending(shard):

    def short(part):
        return part.astype(jnp.bfloat16) if part.dtype == jnp.float32 else part

    return jax.tree.map(short, shard)


def shifted(shard, axis, by):
    peers = lax.axis_size(axis)
    pairs = [(i, i + by) for i in range(peers) if 0 <= i + by < peers]
    return lax.ppermute(shard, axis, pairs)


def low_value(v):
    return lax.optimization_barrier(v.astype(jnp.bfloat16)).astype(jnp.float32)


def low_keep(v):
    return (low_value(v), None)


def low_pass(kept, grad):
    return (grad,)


def back_value(v):
    return v


def back_keep(v):
    return (v, None)


def back_low(kept, grad):
    return (low_value(grad),)


def low(v):
    wrapped = jax.custom_vjp(low_value)
    wrapped.defvjp(low_keep, low_pass)
    return wrapped(v)


def low_back(v):
    wrapped = jax.custom_vjp(back_value)
    wrapped.defvjp(back_keep, back_low)
    return wrapped(v)


def product(left, right):
    return jnp.dot(left, right, precision=PRECISION)


def layer_norm(value, gain, shift):
    center = jnp.mean(value, axis=-1, keepdims=True)
    centered = value - center
    spread = jnp.mean(centered * centered, axis=-1, keepdims=True)
    return centered * lax.rsqrt(spread + EPSILON) * gain + shift


def segment_of(length_row, width):
    ends = jnp.cumsum(length_row, dtype=jnp.int32)
    places = jnp.arange(width, dtype=jnp.int32)
    return jnp.sum((places[:, None] >= ends[None, :]).astype(jnp.int32), axis=1, dtype=jnp.int32)


def attend(queries, keys, values, segments):
    length, width = queries.shape
    size = width // HEADS
    block = min(512, length)
    scale = size ** (-0.5)
    key_heads = keys.reshape(length, HEADS, size)
    value_heads = values.reshape(length, HEADS, size)
    query_blocks = queries.reshape(length // block, block, HEADS, size)
    segment_blocks = segments.reshape(length // block, block)

    def one_block(record):
        query_part, segment_part = record
        scores = low_back(
            jnp.einsum("qhd,khd->hqk", query_part, key_heads, precision=PRECISION) * scale
        )
        allowed = segment_part[:, None] == segments[None, :]
        scores = jnp.where(allowed[None], scores, -1e30)
        highest = jnp.max(scores, axis=-1, keepdims=True)
        raised = jnp.exp(scores - highest)
        shares = raised / jnp.sum(raised, axis=-1, keepdims=True)
        mixed = jnp.einsum("hqk,khd->qhd", low(shares), value_heads, precision=PRECISION)
        return mixed.reshape(block, width)

    mixed = lax.map(jax.checkpoint(one_block), (query_blocks, segment_blocks))
    return low(low_back(mixed.reshape(length, width)))


def self_block(inputs, weight_in, weight_out, bias_out, segments):
    width = inputs.shape[1]
    joined = low(low_back(product(low(inputs), weight_in)))
    mixed = attend(
        joined[:, :width], joined[:, width : 2 * width], joined[:, 2 * width :], segments
    )
    return low_back(product(mixed, weight_out)) + bias_out


def feed_forward(inputs, weight_in, bias_in, weight_out, bias_out):
    inner = low_back(product(low(inputs), weight_in) + bias_in)
    active = low(jax.nn.gelu(inner, approximate=True))
    return low_back(product(active, weight_out)) + bias_out


def encoder_row(params, source, length_row, copy_row):
    (
        self_in,
        self_out,
        cross_weight,
        expand,
        contract,
        expand_bias,
        branch_bias,
        norm_gain,
        norm_shift,
    ) = params
    width = source.shape[1]
    segments = segment_of(length_row, source.shape[0])
    entry = layer_norm(source, norm_gain[2], norm_shift[2])
    hidden = entry + self_block(entry, self_in, self_out, branch_bias[0], segments)
    hidden = layer_norm(hidden, norm_gain[0], norm_shift[0])
    hidden = hidden + feed_forward(hidden, expand, expand_bias, contract, branch_bias[1])
    memory = layer_norm(hidden, norm_gain[1], norm_shift[1])
    value_bias = jnp.concatenate([jnp.zeros((width,), jnp.float32), branch_bias[2]])
    states = low(low_back(product(low(memory), cross_weight) + value_bias))
    copied = low_back(jnp.take(source, copy_row, axis=0))
    return (memory, states, copied)


def decoder_row(params, target, states, copied, length_row, rank_row, count_row):
    (
        self_in,
        self_out,
        cross_weight,
        expand,
        contract,
        expand_bias,
        branch_bias,
        norm_gain,
        norm_shift,
    ) = params
    width = target.shape[1]
    segments = segment_of(length_row, target.shape[0])
    wanted = (count_row + 1) // 2
    picks = segments[:, None] == jnp.arange(count_row.shape[0], dtype=jnp.int32)[None, :]
    quota = jnp.sum(jnp.where(picks, wanted[None, :], 0), axis=1, dtype=jnp.int32)
    glance = rank_row < quota
    start = jnp.where(glance[:, None], target, copied)
    hidden = start + self_block(start, self_in, self_out, branch_bias[0], segments)
    hidden = layer_norm(hidden, norm_gain[0], norm_shift[0])
    query = low(low_back(product(low(hidden), cross_weight[:, :width])))
    mixed = attend(query, states[:, :width], states[:, width:], segments)
    cross = low_back(product(mixed, cross_weight[:, width:])) + branch_bias[2]
    hidden = layer_norm(hidden + cross, norm_gain[1], norm_shift[1])
    hidden = hidden + feed_forward(hidden, expand, expand_bias, contract, branch_bias[1])
    return layer_norm(hidden, norm_gain[2], norm_shift[2])


def add_pairs(left, right):
    return tuple((first + second for first, second in zip(left, right)))


def per_device(
    embeddings,
    cotangent,
    lengths,
    copy_index,
    priority,
    hamming,
    self_in,
    self_out,
    cross_weight,
    expand,
    contract,
    expand_bias,
    branch_bias,
    norm_gain,
    norm_shift,
):
    params = tuple(
        (
            weight[0].astype(jnp.float32)
            for weight in (
                self_in,
                self_out,
                cross_weight,
                expand,
                contract,
                expand_bias,
                branch_bias,
                norm_gain,
                norm_shift,
            )
        )
    )
    leading = lax.axis_index("pipe") == 0
    width = embeddings.shape[2]
    row_count = lengths.shape[0] // MB
    own_rows = embeddings[0].astype(jnp.float32).reshape(MB, row_count, ROW_LEN, width)
    wanted = cotangent.astype(jnp.float32).reshape(MB, row_count, ROW_LEN, width)
    row_lengths = lengths.reshape(MB, row_count, lengths.shape[1])
    row_copies = copy_index.reshape(MB, row_count, ROW_LEN)
    row_ranks = priority.reshape(MB, row_count, ROW_LEN)
    row_counts = hamming.reshape(MB, row_count, hamming.shape[1])
    rows_zero = jnp.zeros((row_count, ROW_LEN, width), jnp.float32)
    states_zero = jnp.zeros((row_count, ROW_LEN, 2 * width), jnp.bfloat16)
    copied_zero = jnp.zeros((row_count, ROW_LEN, width), jnp.bfloat16)
    gradients_zero = tuple((jnp.zeros_like(weight) for weight in params))

    def encode(weights, source, batch):

        def encode_per_row(record):
            return encoder_row(weights, record[0], record[1], record[2])

        return lax.map(encode_per_row, (source, row_lengths[batch], row_copies[batch]))

    def decode(weights, target, states, copied, batch):

        def decode_per_row(record):
            return decoder_row(
                weights, record[0], record[1], record[2], record[3], record[4], record[5]
            )

        return lax.map(
            decode_per_row,
            (target, states, copied, row_lengths[batch], row_ranks[batch], row_counts[batch]),
        )

    def encode_gradient(batch, returned):

        def encode_forward(weights, source):
            memory, states, copied = encode(weights, source, batch)
            return (states, copied)

        outputs, pullback = jax.vjp(encode_forward, params, own_rows[batch])
        return pullback((returned[0].astype(jnp.float32), returned[1].astype(jnp.float32)))

    def decode_gradient(batch, arrived):

        def decode_forward(weights, target, states, copied):
            return decode(weights, target, states, copied, batch)

        decoded, pullback = jax.vjp(
            decode_forward,
            params,
            own_rows[batch],
            arrived[0].astype(jnp.float32),
            arrived[1].astype(jnp.float32),
        )
        gradients, target_gradient, state_gradient, copy_gradient = pullback(wanted[batch])
        return (
            decoded,
            gradients,
            target_gradient,
            state_gradient.astype(jnp.bfloat16),
            copy_gradient.astype(jnp.bfloat16),
        )

    pending = gradients_zero
    settled = gradients_zero
    arrived = []
    returned = []
    produced = []
    layer_rows = []
    embedding_rows = []
    for step in range(MB + 1):

        def section_zero():
            if step < MB:
                memory, states, copied = encode(params, own_rows[step], step)
                return (states.astype(jnp.bfloat16), copied.astype(jnp.bfloat16), memory)
            return (states_zero, copied_zero, rows_zero)

        def section_one():
            if step >= 1:
                decoded = decode(
                    params,
                    own_rows[step - 1],
                    arrived[step - 1][0].astype(jnp.float32),
                    arrived[step - 1][1].astype(jnp.float32),
                    step - 1,
                )
                return (states_zero, copied_zero, decoded)
            return (states_zero, copied_zero, rows_zero)

        states, copied, rows = lax.cond(leading, section_zero, section_one)
        produced.append(rows)
        if step < MB:
            arrived.append(
                (
                    shifted(for_sending(states), "pipe", 1).astype(states.dtype),
                    shifted(for_sending(copied), "pipe", 1).astype(copied.dtype),
                )
            )
    own_gradients = []
    for step in range(MB + 1):

        def section_one():
            if step < MB:
                decoded, gradients, target_gradient, state_gradient, copy_gradient = (
                    decode_gradient(step, arrived[step])
                )
                return (state_gradient, copy_gradient, target_gradient, gradients)
            return (states_zero, copied_zero, rows_zero, gradients_zero)

        def section_zero():
            if step >= 1:
                gradients, source_gradient = encode_gradient(step - 1, returned[step - 1])
                return (states_zero, copied_zero, source_gradient, gradients)
            return (states_zero, copied_zero, rows_zero, gradients_zero)

        back_states, back_copied, own_gradient, gradients = lax.cond(
            leading, section_zero, section_one
        )
        pending = add_pairs(pending, gradients)
        own_gradients.append(own_gradient)
        if step < MB:
            returned.append(
                (
                    shifted(for_sending(back_states), "pipe", -1).astype(back_states.dtype),
                    shifted(for_sending(back_copied), "pipe", -1).astype(back_copied.dtype),
                )
            )
    for batch in range(MB):
        layer_rows.append(jnp.where(leading, produced[batch], produced[batch + 1]))
        embedding_rows.append(jnp.where(leading, own_gradients[batch + 1], own_gradients[batch]))
    part = lax.psum(pending, "dp")
    pending, settled = (gradients_zero, add_pairs(settled, part))
    layer_out = jnp.concatenate(layer_rows, axis=0).reshape(1, MB * row_count * ROW_LEN, width)
    embedding_grad = jnp.concatenate(embedding_rows, axis=0).reshape(
        1, MB * row_count * ROW_LEN, width
    )
    results = tuple((gradient[None] for gradient in settled))
    return (
        layer_out,
        embedding_grad,
        results[0],
        results[1],
        results[2],
        results[3],
        results[4],
        results[5],
        results[6],
        results[7],
        results[8],
    )


def solution(mesh):
    return jax.shard_map(
        per_device,
        mesh=mesh,
        in_specs=(
            P("pipe", "dp", None),
            P("dp", None),
            P("dp", None),
            P("dp"),
            P("dp"),
            P("dp", None),
            P("pipe", None, None),
            P("pipe", None, None),
            P("pipe", None, None),
            P("pipe", None, None),
            P("pipe", None, None),
            P("pipe", None),
            P("pipe", None, None),
            P("pipe", None, None),
            P("pipe", None, None),
        ),
        out_specs=(
            P("pipe", "dp", None),
            P("pipe", "dp", None),
            P("pipe", None, None),
            P("pipe", None, None),
            P("pipe", None, None),
            P("pipe", None, None),
            P("pipe", None, None),
            P("pipe", None),
            P("pipe", None, None),
            P("pipe", None, None),
            P("pipe", None, None),
        ),
        check_vma=False,
    )
```

profile of v0, /device:TPU:1, one launch (start us, length us, event | category | flops | bytes accessed | tf_op | source)
XLA Modules:
  0.0 2519.4 jit_solution(11163252527398489112)
XLA Ops:
  12.8 129.1 %conditional.6 = (bf16[1,1024,1024]{2,1,0:T(8,128)(2,1)}, bf16[1,1024,512]{2,1,0:T(8,128)(2,1)}, f32[1,1024,512]{2,1,0:T(8,128)}) conditional(s32[]{:T(128)} %convert_element_type.1276, () %tuple.321, (f32[2,1,1024,512]{3,2,1,0:T(8,128)}, f32[3,512]{1,0:T(4,128)S(1)}, f32[3,512]{1,0:T(4,128)S(1)}, bf16[512,1536]{1,0:T(8,128)(2,1)}, ...), branch_computations={%region_0.0_spmd, %region_1.15_spmd} | conditional | flops 8668119040 | bytes 228027872 | solution.py:305
  39.8 81.6 %while.531 = (s32[]{:T(128)}, bf16[2,512,512]{2,1,0:T(8,128)(2,1)}, s32[2,512]{1,0:T(2,128)S(1)}, s32[1024]{0:T(1024)S(1)}, bf16[2,512,8,64]{1,3,2,0:T(8,128)(2,...) while((s32[]{:T(128)}, bf16[2,512,512]{2,1,0:T(8,128)(2,1)}, ...), condition=%wide.region_9.9_spmd, body=%wide.region_6.8_spmd.sunk | while | flops 1107821568 | bytes 94414984 | solution.py:105
  48.8 21.3 fusion.1017
  89.4 21.3 fusion.1017
  155.1 60.1 %collective-permute-done = bf16[1,1024,512]{1,2,0:T(8,128)(2,1)} collective-permute-done((bf16[1,1024,512]{1,2,0:T(8,128)(2,1)S(1)}, bf16[1,1024,512]{1,2,0:T(8,128)(2,1)}, u32[]{:S(2)}, u32[]{:S(2)}) %collective-permute-start) | collective-permute-done | bytes 1048608 | tf_op jit(solution)/shard_map/ppermute | solution.py:26
  215.2 133.8 %conditional.7 = (bf16[1,1024,1024]{2,1,0:T(8,128)(2,1)}, bf16[1,1024,512]{2,1,0:T(8,128)(2,1)}, f32[1,1024,512]{2,1,0:T(8,128)}) conditional(s32[]{:T(128)} %convert_element_type.1276, (s32[2,1,1024]{2,1,0:T(1,128)S(1)}, s32[2,1,17]{2,0,1:T(2,128)S(1)}, s32[2,1,17]{2,0,1:T(2,128)S(1)}, f32[2,1,1024,512]{3,2,1,0:T(8,128)}, ...), branch_computations={%region_14.33_spmd, %region_32.46_spmd} | conditional | flops 9775982592 | bytes 328727520 | solution.py:305
  247.3 81.3 %while.534 = (s32[]{:T(128)}, bf16[2,512,512]{2,1,0:T(8,128)(2,1)}, s32[2,512]{1,0:T(2,128)S(1)}, s32[1024]{0:T(1024)S(1)}, bf16[2,512,8,64]{1,3,2,0:T(8,128)(2,...) while((s32[]{:T(128)}, bf16[2,512,512]{2,1,0:T(8,128)(2,1)}, ...), condition=%wide.region_40.41_spmd, body=%wide.region_37.40_spmd.sunk | while | flops 1107821568 | bytes 94414984 | solution.py:105
  256.0 21.3 fusion.996
  296.5 21.3 fusion.996
  353.2 99.1 %collective-permute-start.3 = (bf16[1,1024,1024]{1,2,0:T(8,128)(2,1)}, bf16[1,1024,1024]{1,2,0:T(8,128)(2,1)}, u32[]{:S(2)}, u32[]{:S(2)}) collective-permute-start(bf16[1,1024,1024]{1,2,0:T(8,128)(2,1)} %copy.363), channel_id=1, source_target_pairs={{0,16},{1,17},{2,18},{3,19},{4,20},{5,21},{6,22},{7,23},{8,24},{9,... | collective-permute-start | bytes 6291464 | tf_op jit(solution)/shard_map/ppermute | solution.py:26
  481.2 595.6 %collective-permute-start.2 = (bf16[1,1024,512]{1,2,0:T(8,128)(2,1)}, bf16[1,1024,512]{1,2,0:T(8,128)(2,1)}, u32[]{:S(2)}, u32[]{:S(2)}) collective-permute-start(bf16[1,1024,512]{1,2,0:T(8,128)(2,1)} %copy.362), channel_id=1, source_target_pairs={{0,16},{1,17},{2,18},{3,19},{4,20},{5,21},{6,22},{7,23},{8,24},{9,... | collective-permute-start | bytes 3145736 | tf_op jit(solution)/shard_map/ppermute | solution.py:26
  1098.0 41.5 %collective-permute-done.5 = bf16[1,1024,512]{2,1,0:T(8,128)(2,1)S(1)} collective-permute-done((bf16[1,1024,512]{2,1,0:T(8,128)(2,1)}, bf16[1,1024,512]{2,1,0:T(8,128)(2,1)S(1)}, u32[]{:S(2)}, u32[]{:S(2)}) %collective-permute-start.5) | collective-permute-done | bytes 1048608 | tf_op jit(solution)/shard_map/ppermute | solution.py:26
  1140.5 362.1 %conditional.10 = (bf16[1,1024,1024]{1,2,0:T(8,128)(2,1)}, bf16[1,1024,512]{1,2,0:T(8,128)(2,1)S(1)}, f32[512,1536]{1,0:T(8,128)}, f32[512,512]{1,0:T(8,128)}, f...) conditional(s32[]{:T(128)} %convert_element_type.1276, ...), branch_computations={%region_113.162_spmd, %region_161.199_spmd} | conditional | flops 30545149952 | bytes 1315991808 | solution.py:331
  1163.3 81.3 %while.588 = (s32[]{:T(128)}, bf16[2,512,512]{2,1,0:T(8,128)(2,1)}, s32[2,512]{1,0:T(2,128)S(1)}, s32[1,1024]{1,0:T(1,128)S(1)}, bf16[2,512,8,64]{1,3,2,0:T(8,12...) while((s32[]{:T(128)}, bf16[2,512,512]{2,1,0:T(8,128)(2,1)}, ...), condition=%wide.region_169.170_spmd, body=%wide.region_166.169_spmd.sunk | while | flops 1107821568 | bytes 94414984 | solution.py:105
  1171.8 21.3 fusion.887
  1212.4 21.3 fusion.887
  1294.9 182.5 %while.589 = (s32[]{:T(128)}, f32[1024,8,64]{0,2,1:T(8,128)}, f32[1024,8,64]{0,2,1:T(8,128)S(1)}, f32[2,512,8,64]{1,0,3,2:T(2,128)}, bf16[2,512,8,64]{1,3,2,0:T(...) while((s32[]{:T(128)}, f32[1024,8,64]{0,2,1:T(8,128)}, ...), condition=%wide.region_184.185_spmd.clone, body=%wide.region_178.184_spmd.clone.sunk | while | flops 2825388032 | bytes 325380480 | solution.py:105
  1511.1 331.2 %collective-permute-done.7 = bf16[1,1024,512]{2,1,0:T(8,128)(2,1)S(1)} collective-permute-done((bf16[1,1024,512]{2,1,0:T(8,128)(2,1)}, bf16[1,1024,512]{2,1,0:T(8,128)(2,1)S(1)}, u32[]{:S(2)}, u32[]{:S(2)}) %collective-permute-start.7) | collective-permute-done | bytes 1048608 | tf_op jit(solution)/shard_map/ppermute | solution.py:26
  1843.3 359.5 %conditional.11 = (f32[1,1024,512]{2,1,0:T(8,128)}, f32[512,1536]{1,0:T(8,128)}, f32[512,512]{1,0:T(8,128)}, f32[512,1024]{1,0:T(8,128)}, f32[512,2048]{1,0:T(8,...) conditional(s32[]{:T(128)} %convert_element_type.1276, ...), branch_computations={%region_198.200_spmd, %region_199.237_spmd} | conditional | flops 25537622016 | bytes 761399488 | solution.py:331
  1862.4 81.3 %while.590 = (s32[]{:T(128)}, bf16[2,512,512]{2,1,0:T(8,128)(2,1)}, s32[2,512]{1,0:T(2,128)S(1)}, s32[1,1024]{1,0:T(1,128)S(1)}, bf16[2,512,8,64]{1,3,2,0:T(8,12...) while((s32[]{:T(128)}, bf16[2,512,512]{2,1,0:T(8,128)(2,1)}, ...), condition=%wide.region_207.208_spmd, body=%wide.region_204.207_spmd.sunk | while | flops 1107821568 | bytes 94414984 | solution.py:105
  1870.9 21.3 fusion.868
  1994.3 182.4 %while.591 = (s32[]{:T(128)}, f32[1024,8,64]{0,2,1:T(8,128)}, f32[1024,8,64]{0,2,1:T(8,128)S(1)}, f32[2,512,8,64]{1,0,3,2:T(2,128)}, bf16[2,512,8,64]{1,3,2,0:T(...) while((s32[]{:T(128)}, f32[1024,8,64]{0,2,1:T(8,128)}, ...), condition=%wide.region_222.223_spmd.clone, body=%wide.region_216.222_spmd.clone.sunk | while | flops 2825388032 | bytes 325380480 | solution.py:105
  2243.9 58.8 %all-reduce.58 = (f32[1,2048]{1,0:T(1,128)}, f32[1,3,512]{2,0,1:T(1,128)}, f32[1,3,512]{2,0,1:T(1,128)}, f32[1,3,512]{2,0,1:T(1,128)}) all-reduce(f32[1,2048]{1,0:T(1,128)S(1)} %bitcast.1433, f32[1,3,512]{2,0,1:T(1,128)S(1)} %broadcast_in_dim.1766, ...), channel_id=1, replica_groups=mesh['pipe'=2,'dp'=16] {'dp'}, use_global_device_ids=true, to_apply=%region_241.243 | all-reduce | flops 6656 | bytes 53248 | tf_op jit(solution)/shard_map/psum | solution.py:346
  2308.2 189.7 %all-reduce.62.cloned.1.call-done = (f32[1,512,1536]{2,1,0:T(8,128)}, f32[1,512,512]{2,1,0:T(8,128)}, f32[1,512,1024]{2,1,0:T(8,128)}, f32[1,512,2048]{2,1,0:T(8,128)}, f32[1,2048,512]{2,1,0:T(8,128)}) async-done(((f32[1,512,1536]{2,1,0:T(8,128)}, f32[1,512,512]{2,1,0:T(8,128)}, f32[1,512,1024]{2,1,0:T(8,128)}, f32[1,512,2048]{2,1,0:T(8,128)}, f32[1,2048,512]{2,1,0:T(8,128)}), (f32[1,512,1536]{2,1,0:T(8,128)}, ...) | async-done | bytes 14680080 | tf_op jit(solution)/shard_map/psum | solution.py:346
  (872 shorter events, 982.0 us)
Async XLA Ops:
  7.2 2490.7 %all-reduce.62.cloned.1.call-start = ((), (), s32[]{:S(2)}) async-start(), calls=%async_computation | async-start | bytes 29360128 | tf_op jit(solution)/shard_map/psum | solution.py:346
  39.7 81.7 %copy-start.197 = (f32[1024]{0:T(1024)S(1)}, f32[1024]{0:T(1024)}, u32[]{:S(2)}) copy-start(f32[1024]{0:T(1024)} %copy-done.196) | copy-start | bytes 12292 | tf_op jit(solution)/shard_map/cond
  39.7 81.7 %copy-start.262 = (f32[1024]{0:T(1024)S(1)}, f32[1024]{0:T(1024)}, u32[]{:S(2)}) copy-start(f32[1024]{0:T(1024)} %copy-done.261) | copy-start | bytes 12292 | tf_op jit(solution)/shard_map/cond
  145.9 69.3 %collective-permute-start.1 = (bf16[1,1024,1024]{1,2,0:T(8,128)(2,1)}, bf16[1,1024,1024]{1,2,0:T(8,128)(2,1)}, u32[]{:S(2)}, u32[]{:S(2)}) collective-permute-start(bf16[1,1024,1024]{1,2,0:T(8,128)(2,1)} %copy.354), channel_id=1, source_target_pairs={{0,16},{1,17},{2,18},{3,19},{4,20},{5,21},{6,22},{7,23},{8,24},{9,... | collective-permute-start | bytes 6291464 | tf_op jit(solution)/shard_map/ppermute | solution.py:26
  150.2 65.0 %collective-permute-start = (bf16[1,1024,512]{1,2,0:T(8,128)(2,1)S(1)}, bf16[1,1024,512]{1,2,0:T(8,128)(2,1)}, u32[]{:S(2)}, u32[]{:S(2)}) collective-permute-start(bf16[1,1024,512]{1,2,0:T(8,128)(2,1)S(1)} %copy.353), channel_id=1, source_target_pairs={{0,16},{1,17},{2,18},{3,19},{4,20},{5,21},{6,22},{7,23},{8,24},{9,... | collective-permute-start | bytes 3145736 | tf_op jit(solution)/shard_map/ppermute | solution.py:26
  349.1 103.3 %copy-start.224 = (s32[2048]{0:T(1024)S(1)}, s32[2048]{0:T(1024)}, u32[]{:S(2)}) copy-start(s32[2048]{0:T(1024)} %param.69) | copy-start | bytes 24580
  349.1 103.3 %copy-start.389 = (bf16[1,512,1536]{2,1,0:T(8,128)(2,1)S(1)}, bf16[1,512,1536]{2,1,0:T(8,128)(2,1)}, u32[]{:S(2)}) copy-start(bf16[1,512,1536]{2,1,0:T(8,128)(2,1)} %param.71) | copy-start | bytes 4718596
  349.1 103.2 %copy-start.412 = (s32[2,17]{1,0:T(2,128)S(1)}, s32[2,17]{1,0:T(2,128)}, u32[]{:S(2)}) copy-start(s32[2,17]{1,0:T(2,128)} %param.67) | copy-start | bytes 412
  349.1 103.2 %copy-start.416 = (s32[2,17]{1,0:T(2,128)S(1)}, s32[2,17]{1,0:T(2,128)}, u32[]{:S(2)}) copy-start(s32[2,17]{1,0:T(2,128)} %param.70) | copy-start | bytes 412
  353.2 744.8 %collective-permute-start.3 = (bf16[1,1024,1024]{1,2,0:T(8,128)(2,1)}, bf16[1,1024,1024]{1,2,0:T(8,128)(2,1)}, u32[]{:S(2)}, u32[]{:S(2)}) collective-permute-start(bf16[1,1024,1024]{1,2,0:T(8,128)(2,1)} %copy.363), channel_id=1, source_target_pairs={{0,16},{1,17},{2,18},{3,19},{4,20},{5,21},{6,22},{7,23},{8,24},{9,... | collective-permute-start | bytes 6291464 | tf_op jit(solution)/shard_map/ppermute | solution.py:26
  477.6 661.9 %collective-permute-start.4 = (bf16[1,1024,1024]{2,1,0:T(8,128)(2,1)}, bf16[1,1024,1024]{2,1,0:T(8,128)(2,1)S(1)}, u32[]{:S(2)}, u32[]{:S(2)}) collective-permute-start(bf16[1,1024,1024]{2,1,0:T(8,128)(2,1)} %copy.373), channel_id=1, source_target_pairs={{16,0},{17,1},{18,2},{19,3},{20,4},{21,5},{22,6},{23,7},{24,8},{25... | collective-permute-start | bytes 6291464 | tf_op jit(solution)/shard_map/ppermute | solution.py:26
  478.8 661.6 %copy-start.157 = (f32[1,3,512]{2,1,0:T(4,128)S(1)}, f32[1,3,512]{2,1,0:T(4,128)}, u32[]{:S(2)}) copy-start(f32[1,3,512]{2,1,0:T(4,128)} %copy-done.155) | copy-start | bytes 18436
  478.9 661.6 %copy-start.162 = (f32[3,512]{1,0:T(4,128)S(1)}, f32[3,512]{1,0:T(4,128)}, u32[]{:S(2)}) copy-start(f32[3,512]{1,0:T(4,128)} %copy-done.160) | copy-start | bytes 18436
  478.9 661.6 %copy-start.222 = (s32[2048]{0:T(1024)S(1)}, s32[2048]{0:T(1024)}, u32[]{:S(2)}) copy-start(s32[2048]{0:T(1024)} %param.68) | copy-start | bytes 24580
  478.9 661.6 %copy-start.225 = (s32[2048]{0:T(1024)S(1)}, s32[2048]{0:T(1024)}, u32[]{:S(2)}) copy-start(s32[2048]{0:T(1024)} %param.69) | copy-start | bytes 24580
  478.9 661.6 %copy-start.417 = (s32[2,17]{1,0:T(2,128)S(1)}, s32[2,17]{1,0:T(2,128)}, u32[]{:S(2)}) copy-start(s32[2,17]{1,0:T(2,128)} %param.70) | copy-start | bytes 412
  481.2 616.8 %collective-permute-start.2 = (bf16[1,1024,512]{1,2,0:T(8,128)(2,1)}, bf16[1,1024,512]{1,2,0:T(8,128)(2,1)}, u32[]{:S(2)}, u32[]{:S(2)}) collective-permute-start(bf16[1,1024,512]{1,2,0:T(8,128)(2,1)} %copy.362), channel_id=1, source_target_pairs={{0,16},{1,17},{2,18},{3,19},{4,20},{5,21},{6,22},{7,23},{8,24},{9,... | collective-permute-start | bytes 3145736 | tf_op jit(solution)/shard_map/ppermute | solution.py:26
  1078.1 61.4 %collective-permute-start.5 = (bf16[1,1024,512]{2,1,0:T(8,128)(2,1)}, bf16[1,1024,512]{2,1,0:T(8,128)(2,1)S(1)}, u32[]{:S(2)}, u32[]{:S(2)}) collective-permute-start(bf16[1,1024,512]{2,1,0:T(8,128)(2,1)} %copy.374), channel_id=1, source_target_pairs={{16,0},{17,1},{18,2},{19,3},{20,4},{21,5},{22,6},{23,7},{24,8},{25... | collective-permute-start | bytes 3145736 | tf_op jit(solution)/shard_map/ppermute | solution.py:26
  1507.1 336.2 %copy-start.158 = (f32[1,3,512]{2,1,0:T(4,128)S(1)}, f32[1,3,512]{2,1,0:T(4,128)}, u32[]{:S(2)}) copy-start(f32[1,3,512]{2,1,0:T(4,128)} %copy-done.155) | copy-start | bytes 18436
  1507.1 336.2 %copy-start.163 = (f32[3,512]{1,0:T(4,128)S(1)}, f32[3,512]{1,0:T(4,128)}, u32[]{:S(2)}) copy-start(f32[3,512]{1,0:T(4,128)} %copy-done.160) | copy-start | bytes 18436
  1507.1 336.2 %copy-start.166 = (f32[3,512]{1,0:T(4,128)S(1)}, f32[3,512]{1,0:T(4,128)}, u32[]{:S(2)}) copy-start(f32[3,512]{1,0:T(4,128)} %copy-done.164) | copy-start | bytes 18436
  1507.1 336.2 %copy-start.413 = (s32[2,17]{1,0:T(2,128)S(1)}, s32[2,17]{1,0:T(2,128)}, u32[]{:S(2)}) copy-start(s32[2,17]{1,0:T(2,128)} %param.67) | copy-start | bytes 412
  1507.1 335.3 %collective-permute-start.6 = (bf16[1,1024,1024]{2,1,0:T(8,128)(2,1)}, bf16[1,1024,1024]{2,1,0:T(8,128)(2,1)S(1)}, u32[]{:S(2)}, u32[]{:S(2)}) collective-permute-start(bf16[1,1024,1024]{2,1,0:T(8,128)(2,1)} %copy.382), channel_id=1, source_target_pairs={{16,0},{17,1},{18,2},{19,3},{20,4},{21,5},{22,6},{23,7},{24,8},{25... | collective-permute-start | bytes 6291464 | tf_op jit(solution)/shard_map/ppermute | solution.py:26
  1509.9 332.5 %collective-permute-start.7 = (bf16[1,1024,512]{2,1,0:T(8,128)(2,1)}, bf16[1,1024,512]{2,1,0:T(8,128)(2,1)S(1)}, u32[]{:S(2)}, u32[]{:S(2)}) collective-permute-start(bf16[1,1024,512]{2,1,0:T(8,128)(2,1)} %copy.383), channel_id=1, source_target_pairs={{16,0},{17,1},{18,2},{19,3},{20,4},{21,5},{22,6},{23,7},{24,8},{25... | collective-permute-start | bytes 3145736 | tf_op jit(solution)/shard_map/ppermute | solution.py:26
  (216 other events, 2679.0 us)
Sparse Core Ops, SparseCore 0:
  2228.4 269.4 all-reduce.61
where the time goes:
time: 2540 us; the launch traced here: 2520 us
  starting transfers between devices  705 us (28%)
  waiting for transfers between devices  641 us (25%)
  other arithmetic  455 us (18%)
  matrix products  353 us (14%)
  local copies, waits for them, and re-layouts  268 us (11%)
  blocking collectives  58.8 us (2%)
    ppermute x8, starting transfers between devices, shifted(): return lax.ppermute(shard, axis, pairs)  705 us
    ppermute x8, waiting for transfers between devices, shifted(): return lax.ppermute(shard, axis, pairs)  451 us
    psum x1, waiting for transfers between devices, per_device(): part = lax.psum(pending, 'dp')  190 us
    sub x8, other arithmetic, one_block(): raised = jnp.exp(scores - highest)  170 us
    dot_general x38, matrix products, product(): return jnp.dot(left, right, precision=PRECISION)  129 us
    dot_general x20, matrix products, one_block(): jnp.einsum('qhd,khd->hqk', query_part, key_heads, precision=PRECISION)  125 us
    dot_general x16, matrix products, one_block(): jnp.einsum('hqk,khd->qhd', low(shares), value_heads, precision=PRECISION)  98.7 us
    dynamic_update_slice x24, local copies, waits for them, and re-layouts, attend(): mixed = lax.map(jax.checkpoint(one_block), (query_blocks, segment_blocks))  95.4 us
  transfers between devices with their start and end apart: 9, of which 5 were waited for; matrix products, arithmetic and copies ran while one was open for 2% of the time, Pallas kernels for 0%

commit v1 on v0

v1 whole, which is shorter than its diff:
```python
import functools

import jax
import jax.numpy as jnp
from jax import lax
from jax.experimental import pallas as pl
from jax.experimental.pallas import tpu as pltpu
from jax.sharding import PartitionSpec as P

HEADS = 8
D = 512
FF = 2048
T = 1024
SENTS = 17
WIN = 128
EPSILON = 1e-05
NEG = -1e30
BF = jnp.bfloat16
F32 = jnp.float32
VMEM = pl.BlockSpec(memory_space=pltpu.VMEM)
SMEM = pl.BlockSpec(memory_space=pltpu.SMEM)
BLOCK = 256
STEPS = T // BLOCK


def nn(a, b):
    return jnp.dot(a, b, preferred_element_type=F32)


def nt(a, b):
    return lax.dot_general(a, b, (((1,), (1,)), ((), ())), preferred_element_type=F32)


def tn(a, b):
    return lax.dot_general(a, b, (((0,), (0,)), ((), ())), preferred_element_type=F32)


def normalized(value):
    center = jnp.mean(value, axis=-1, keepdims=True)
    centered = value - center
    spread = jnp.mean(centered * centered, axis=-1, keepdims=True)
    scale = lax.rsqrt(spread + EPSILON)
    return centered * scale, scale


def normalized_back(grad, unit, scale):
    first = jnp.mean(grad, axis=-1, keepdims=True)
    second = jnp.mean(grad * unit, axis=-1, keepdims=True)
    return scale * (grad - first - unit * second)


def folded(value):
    return jnp.sum(value.reshape(value.shape[0] // 8, 8, value.shape[1]), axis=0)


def column_sum(value):
    return jnp.sum(value, axis=0, keepdims=True)


def each_block(body):
    def step(index, carry):
        body(pl.ds(pl.multiple_of(index * BLOCK, BLOCK), BLOCK))
        return carry

    lax.fori_loop(0, STEPS, step, 0)


def each_chunk(count, size, body):
    def step(index, carry):
        body(pl.multiple_of(index * size, size))
        return carry

    lax.fori_loop(0, count, step, 0)


def kernel_call(body, outs, operands, scalars=0, scratch=(), out_specs=None, flops=0):
    size = sum(x.size * x.dtype.itemsize for x in operands)
    size += sum(x.size * x.dtype.itemsize for x in outs)
    return pl.pallas_call(
        body,
        out_shape=tuple(outs),
        in_specs=[SMEM] * scalars + [VMEM] * (len(operands) - scalars),
        out_specs=tuple(out_specs) if out_specs else (VMEM,) * len(outs),
        scratch_shapes=list(scratch),
        compiler_params=pltpu.CompilerParams(vmem_limit_bytes=56 << 20),
        cost_estimate=pl.CostEstimate(flops=flops, bytes_accessed=size, transcendentals=0),
    )(*operands)


def shaped(rows, columns, kind):
    return jax.ShapeDtypeStruct((rows, columns), kind)


def layout_kernel(lengths, hamming, priority, copies, table, bias, glance, places):
    ends = []
    total = jnp.int32(0)
    for j in range(SENTS):
        total = total + lengths[0, j]
        ends.append(total)
    count = jnp.int32(0)
    first = jnp.int32(0)

    def origin(start):
        return jnp.minimum((start // 16) * 16, T - WIN)

    starts_at = []
    for j in range(SENTS):
        begin = jnp.int32(0) if j == 0 else ends[j - 1]
        opens = (ends[j] - origin(first)) > WIN
        if j == 0:
            opens = jnp.bool_(False)
        first = jnp.where(opens, begin, first)
        count = jnp.where(opens, count + 1, count)
        table[0, 1 + count] = origin(first)
        table[0, 32 + count] = first
        table[0, 64 + count] = ends[j]
    table[0, 0] = count + 1

    lanes = lax.broadcasted_iota(jnp.int32, (8, WIN), 1)
    rows = lax.broadcasted_iota(jnp.int32, (8, WIN), 0)
    place = rows * WIN + lanes
    quota = jnp.zeros((8, WIN), jnp.int32) + (hamming[0, 0] + 1) // 2
    for j in range(SENTS - 1):
        change = (hamming[0, j + 1] + 1) // 2 - (hamming[0, j] + 1) // 2
        quota = quota + jnp.where(place >= ends[j], change, 0)
    chosen = jnp.where(priority[...] < quota, 1.0, 0.0)
    copy = copies[...].astype(F32)
    for i in range(T // WIN):
        part = pl.ds(i * WIN, WIN)
        glance[part, :] = jnp.broadcast_to(chosen[i : i + 1, :], (WIN, WIN)).T
        places[part, :] = jnp.broadcast_to(copy[i : i + 1, :], (WIN, WIN)).T.astype(jnp.int32)

    def window(w, carry):
        at = table[0, 1 + w]
        here = lanes + at
        segment = jnp.zeros((8, WIN), F32)
        for j in range(SENTS):
            segment = segment + jnp.where(here >= ends[j], 1.0, 0.0)
        inside = (here >= table[0, 32 + w]) & (here < table[0, 64 + w])
        segment = jnp.where(inside, segment, -1.0)
        across = jnp.broadcast_to(segment[0:1, :], (WIN, WIN))
        down = across.T
        bias[w] = jnp.where((across == down) & (across >= 0.0), 0.0, NEG)
        return carry

    lax.fori_loop(0, count + 1, window, 0)


def row_layout(lengths, hamming, priority, copies):
    outs = (
        shaped(1, 128, jnp.int32),
        jax.ShapeDtypeStruct((SENTS, WIN, WIN), F32),
        shaped(T, WIN, F32),
        shaped(T, WIN, jnp.int32),
    )
    return kernel_call(
        layout_kernel,
        outs,
        (lengths, hamming, priority, copies),
        scalars=2,
        out_specs=(SMEM, VMEM, VMEM, VMEM),
    )


def pair_halves(part):
    low = lax.broadcasted_iota(jnp.int32, (WIN, WIN), 1) < 64
    zero = jnp.zeros_like(part)
    return jnp.concatenate([jnp.where(low, part, zero), jnp.where(low, zero, part)], axis=0)


def pair_join(both):
    low = lax.broadcasted_iota(jnp.int32, (WIN, WIN), 1) < 64
    return jnp.where(low, both[:WIN], both[WIN:])


def attend(table, bias, queries, keys, values, mixed, stats):
    def window(w, carry):
        at = pl.ds(pl.multiple_of(table[0, 1 + w], 16), WIN)
        masked = bias[w]
        masked = jnp.concatenate([masked, masked], axis=1)
        for pair in range(HEADS // 2):
            lanes = slice(pair * 128, pair * 128 + 128)
            query = pair_halves(queries[at, lanes])
            scores = nt(keys[at, lanes], query) + masked
            highest = jnp.maximum(jnp.max(scores, axis=0, keepdims=True), -1e29)
            raised = jnp.exp(scores - highest)
            inverse = 1.0 / jnp.maximum(jnp.sum(raised, axis=0, keepdims=True), 1e-30)
            shares = (raised * inverse).astype(BF)
            stats[w * 4 + pair, 0:1, :] = highest
            stats[w * 4 + pair, 1:2, :] = inverse
            out = pair_join(tn(shares, values[at, lanes])).astype(BF)
            mixed[at, lanes] = mixed[at, lanes] + out
        return carry

    mixed[...] = jnp.zeros_like(mixed)
    lax.fori_loop(0, table[0, 0], window, 0)


def attend_back(table, bias, queries, keys, values, stats, grad, grad_q, grad_k, grad_v):
    def window(w, carry):
        at = pl.ds(pl.multiple_of(table[0, 1 + w], 16), WIN)
        masked = bias[w]
        masked = jnp.concatenate([masked, masked], axis=1)
        for pair in range(HEADS // 2):
            lanes = slice(pair * 128, pair * 128 + 128)
            query = pair_halves(queries[at, lanes])
            key = keys[at, lanes]
            scores = nt(key, query) + masked
            shares = jnp.exp(scores - stats[w * 4 + pair, 0:1, :]) * stats[w * 4 + pair, 1:2, :]
            out = pair_halves(grad[at, lanes])
            back = nt(values[at, lanes], out)
            grad_v[at, lanes] = grad_v[at, lanes] + nn(shares.astype(BF), out).astype(BF)
            total = jnp.sum(shares * back, axis=0, keepdims=True)
            scored = (shares * (back - total)).astype(BF)
            grad_k[at, lanes] = grad_k[at, lanes] + nn(scored, query).astype(BF)
            asked = pair_join(tn(scored, key)) * 0.125
            grad_q[at, lanes] = grad_q[at, lanes] + asked.astype(BF)
        return carry

    for ref in (grad_q, grad_k, grad_v):
        ref[...] = jnp.zeros_like(ref)
    lax.fori_loop(0, table[0, 0], window, 0)


STATS = jax.ShapeDtypeStruct((SENTS * 4, 2, 2 * WIN), F32)


def thirds(ref):
    return tuple(ref.at[:, i * D : (i + 1) * D] for i in range(ref.shape[1] // D))


def self_tail(x, weight_out, bias, mixed, z):
    def after(at):
        z[at, :] = x[at, :].astype(F32) + nn(mixed[at, :], weight_out[...]) + bias[0:1, :]

    each_block(after)


def project(x, weight_in, joined, at):
    got = nn(x, weight_in[...])
    joined[at, :D] = (got[:, :D] * 0.125).astype(BF)
    joined[at, D:] = got[:, D:].astype(BF)


def encoder_self_kernel(
    table, bias, source, weight_in, weight_out, branch, gain, shift, joined, mixed, stats, z, x
):
    def before(at):
        unit, _ = normalized(source[at, :].astype(F32))
        value = unit * gain[2:3, :] + shift[2:3, :]
        x[at, :] = value
        project(value.astype(BF), weight_in, joined, at)

    each_block(before)
    attend(table, bias, *thirds(joined), mixed, stats)
    self_tail(x, weight_out, branch, mixed, z)


def decoder_self_kernel(
    table, bias, source, target, glance, places, weight_in, weight_out, branch, x, joined, mixed, stats, z, copied
):
    copied[...] = jnp.zeros_like(copied)

    def window(w, carry):
        start = pl.multiple_of(table[0, 1 + w], 16)
        at = pl.ds(start, WIN)
        lanes = lax.broadcasted_iota(jnp.int32, (WIN, WIN), 1) + start
        allowed = jnp.min(bias[w], axis=1, keepdims=True)
        inside = jnp.max(bias[w], axis=1, keepdims=True) == 0.0
        hit = jnp.where((places[at, :] == lanes) & inside, 1.0, 0.0).astype(BF)
        copied[at, :] = copied[at, :] + nn(hit, source[at, :]).astype(BF)
        return carry

    lax.fori_loop(0, table[0, 0], window, 0)

    def before(at):
        kept = jnp.concatenate([glance[at, :]] * 4, axis=1) > 0.5
        value = jnp.where(kept, target[at, :].astype(F32), copied[at, :].astype(F32)).astype(BF)
        x[at, :] = value
        project(value, weight_in, joined, at)

    each_block(before)
    attend(table, bias, *thirds(joined), mixed, stats)
    self_tail(x, weight_out, branch, mixed, z)


FLOP_UNIT = 2 * T * D * D


def encoder_self(table, bias, source, weights, small):
    outs = (shaped(T, 3 * D, BF), shaped(T, D, BF), STATS, shaped(T, D, F32))
    return kernel_call(
        encoder_self_kernel,
        outs,
        (table, bias, source, weights["self_in"], weights["self_out"], small["branch_bias"], small["norm_gain"], small["norm_shift"]),
        scalars=1,
        scratch=[pltpu.VMEM((T, D), F32)],
        flops=8 * FLOP_UNIT,
    )


def decoder_self(table, bias, source, target, glance, places, weights, small):
    outs = (shaped(T, D, BF), shaped(T, 3 * D, BF), shaped(T, D, BF), STATS, shaped(T, D, F32))
    return kernel_call(
        decoder_self_kernel,
        outs,
        (table, bias, source, target, glance, places, weights["self_in"], weights["self_out"], small["branch_bias"]),
        scalars=1,
        scratch=[pltpu.VMEM((T, D), BF)],
        flops=8 * FLOP_UNIT,
    )


ROOT = 0.7978845608028654
CUBE = 0.044715


def gelu_parts(u):
    square = u * u
    bent = jnp.tanh(u * (ROOT + ROOT * CUBE * square))
    half = 0.5 + 0.5 * bent
    slope = half + (0.5 * u) * (1.0 - bent * bent) * (ROOT + 3.0 * ROOT * CUBE * square)
    return u * half, slope


def expand_block(value, expand, expand_bias, active, slope, at):
    for j in range(FF // D):
        cols = slice(j * D, (j + 1) * D)
        act, bend = gelu_parts(nn(value, expand[:, cols]) + expand_bias[0:1, cols])
        active[at, cols] = act.astype(BF)
        slope[at, cols] = bend.astype(BF)


def encoder_ff_kernel(z1, expand, expand_bias, contract, cross, branch, gain, shift, active, slope, z2, memory, states):
    def block(at):
        unit, _ = normalized(z1[at, :])
        value = unit * gain[0:1, :] + shift[0:1, :]
        expand_block(value.astype(BF), expand, expand_bias, active, slope, at)
        total = value + nn(active[at, :], contract[...]) + branch[1:2, :]
        z2[at, :] = total
        unit, _ = normalized(total)
        out = unit * gain[1:2, :] + shift[1:2, :]
        memory[at, :] = out
        got = nn(out.astype(BF), cross[...])
        states[at, :D] = got[:, :D].astype(BF)
        states[at, D:] = (got[:, D:] + branch[2:3, :]).astype(BF)

    each_block(block)


def encoder_ff(z1, weights, small):
    outs = (shaped(T, FF, BF), shaped(T, FF, BF), shaped(T, D, F32), shaped(T, D, F32), shaped(T, 2 * D, BF))
    return kernel_call(
        encoder_ff_kernel,
        outs,
        (z1, weights["expand"], small["expand_bias"], weights["contract"], weights["cross_weight"], small["branch_bias"], small["norm_gain"], small["norm_shift"]),
        flops=10 * FLOP_UNIT,
    )


def weight_grads(x, y, out, row, columns):
    for c in range(columns):
        out[row + c * D : row + (c + 1) * D, :] = tn(x[...], y[:, c * D : (c + 1) * D]).astype(BF)


def ff_back(dzb, value_b, active, slope, expand, contract, inner, grads):
    def block(at):
        for j in range(FF // D):
            cols = slice(j * D, (j + 1) * D)
            back = nt(dzb[at, :], contract[cols, :])
            inner[at, cols] = (back * slope[at, cols].astype(F32)).astype(BF)

    each_block(block)
    for c in range(FF // D):
        cols = slice(c * D, (c + 1) * D)
        grads[FF + c * D : FF + (c + 1) * D, :] = tn(active[:, cols], dzb[...]).astype(BF)
        grads[c * D : (c + 1) * D, :] = tn(value_b[...], inner[:, cols]).astype(BF)


def decoder_ff_kernel(
    z2, expand, expand_bias, contract, branch, gain, shift, cotangent,
    decoded, grads, bias_grads, ff_bias_grad, dz2,
    active, slope, inner, value_b, dz, dzb,
):
    bias_grads[...] = jnp.zeros_like(bias_grads)

    def block(at):
        unit, _ = normalized(z2[at, :])
        value = unit * gain[1:2, :] + shift[1:2, :]
        value_b[at, :] = value.astype(BF)
        expand_block(value.astype(BF), expand, expand_bias, active, slope, at)
        total = value + nn(active[at, :], contract[...]) + branch[1:2, :]
        unit, scale = normalized(total)
        decoded[at, :] = unit * gain[2:3, :] + shift[2:3, :]
        wanted = cotangent[at, :].astype(F32)
        bias_grads[0:1, :] += column_sum(wanted * unit)
        bias_grads[1:2, :] += column_sum(wanted)
        back = normalized_back(wanted * gain[2:3, :], unit, scale)
        bias_grads[2:3, :] += column_sum(back)
        dz[at, :] = back
        dzb[at, :] = back.astype(BF)

    each_block(block)
    ff_back(dzb, value_b, active, slope, expand, contract, inner, grads)
    ff_bias_grad[...] = jnp.zeros_like(ff_bias_grad)

    def last(at):
        ff_bias_grad[0:1, :] += column_sum(inner[at, :].astype(F32))
        back = dz[at, :] + nt(inner[at, :], expand[...])
        unit, scale = normalized(z2[at, :])
        bias_grads[3:4, :] += column_sum(back * unit)
        bias_grads[4:5, :] += column_sum(back)
        dz2[at, :] = normalized_back(back * gain[1:2, :], unit, scale)

    each_block(last)


def decoder_ff(z2, cotangent, weights, small):
    outs = (shaped(T, D, F32), shaped(2 * FF, D, BF), shaped(8, D, F32), shaped(8, FF, F32), shaped(T, D, F32))
    return kernel_call(
        decoder_ff_kernel,
        outs,
        (z2, weights["expand"], small["expand_bias"], weights["contract"], small["branch_bias"], small["norm_gain"], small["norm_shift"], cotangent),
        scratch=[
            pltpu.VMEM((T, FF), BF),
            pltpu.VMEM((T, FF), BF),
            pltpu.VMEM((T, FF), BF),
            pltpu.VMEM((T, D), BF),
            pltpu.VMEM((T, D), F32),
            pltpu.VMEM((T, D), BF),
        ],
        flops=24 * FLOP_UNIT,
    )


def encoder_ff_back_kernel(
    dstates, z1, z2, active, slope, expand, contract, cross, gain, shift,
    cross_grads, grads, bias_grads, ff_bias_grad, dz1,
    inner, value_b, memory_b, dz, dzb,
):
    bias_grads[...] = jnp.zeros_like(bias_grads)

    def block(at):
        unit, scale = normalized(z2[at, :])
        memory_b[at, :] = (unit * gain[1:2, :] + shift[1:2, :]).astype(BF)
        back = nt(dstates[at, :], cross[...])
        bias_grads[0:1, :] += column_sum(dstates[at, D:].astype(F32))
        bias_grads[1:2, :] += column_sum(back * unit)
        bias_grads[2:3, :] += column_sum(back)
        back = normalized_back(back * gain[1:2, :], unit, scale)
        bias_grads[3:4, :] += column_sum(back)
        dz[at, :] = back
        dzb[at, :] = back.astype(BF)
        unit, _ = normalized(z1[at, :])
        value_b[at, :] = (unit * gain[0:1, :] + shift[0:1, :]).astype(BF)

    each_block(block)
    weight_grads(memory_b, dstates, cross_grads, 0, 2)
    ff_back(dzb, value_b, active, slope, expand, contract, inner, grads)
    ff_bias_grad[...] = jnp.zeros_like(ff_bias_grad)

    def last(at):
        ff_bias_grad[0:1, :] += column_sum(inner[at, :].astype(F32))
        back = dz[at, :] + nt(inner[at, :], expand[...])
        unit, scale = normalized(z1[at, :])
        bias_grads[4:5, :] += column_sum(back * unit)
        bias_grads[5:6, :] += column_sum(back)
        dz1[at, :] = normalized_back(back * gain[0:1, :], unit, scale)

    each_block(last)


def encoder_ff_back(dstates, z1, z2, active, slope, weights, small):
    outs = (shaped(2 * D, D, BF), shaped(2 * FF, D, BF), shaped(8, D, F32), shaped(8, FF, F32), shaped(T, D, F32))
    return kernel_call(
        encoder_ff_back_kernel,
        outs,
        (dstates, z1, z2, active, slope, weights["expand"], weights["contract"], weights["cross_weight"], small["norm_gain"], small["norm_shift"]),
        scratch=[
            pltpu.VMEM((T, FF), BF),
            pltpu.VMEM((T, D), BF),
            pltpu.VMEM((T, D), BF),
            pltpu.VMEM((T, D), F32),
            pltpu.VMEM((T, D), BF),
        ],
        flops=20 * FLOP_UNIT,
    )


def decoder_cross_kernel(table, bias, z1, states, weight, branch, gain, shift, queries, mixed, stats, z2, x):
    def before(at):
        unit, _ = normalized(z1[at, :])
        value = unit * gain[0:1, :] + shift[0:1, :]
        x[at, :] = value
        queries[at, :] = (nn(value.astype(BF), weight[:, :D]) * 0.125).astype(BF)

    each_block(before)
    attend(table, bias, queries, *thirds(states), mixed, stats)

    def after(at):
        z2[at, :] = x[at, :] + nn(mixed[at, :], weight[:, D:]) + branch[2:3, :]

    each_block(after)


def decoder_cross(table, bias, z1, states, weights, small):
    outs = (shaped(T, D, BF), shaped(T, D, BF), STATS, shaped(T, D, F32))
    return kernel_call(
        decoder_cross_kernel,
        outs,
        (table, bias, z1, states, weights["cross_weight"], small["branch_bias"], small["norm_gain"], small["norm_shift"]),
        scalars=1,
        scratch=[pltpu.VMEM((T, D), F32)],
        flops=6 * FLOP_UNIT,
    )


def decoder_cross_back_kernel(
    table, bias, dz2, z1, queries, states, mixed, stats, weight, gain, shift,
    grads, bias_grads, dstates, dz1,
    value_b, dzb, out, dq,
):
    bias_grads[...] = jnp.zeros_like(bias_grads)

    def before(at):
        bias_grads[0:1, :] += column_sum(dz2[at, :])
        low = dz2[at, :].astype(BF)
        dzb[at, :] = low
        out[at, :] = nt(low, weight[:, D:]).astype(BF)
        unit, _ = normalized(z1[at, :])
        value_b[at, :] = (unit * gain[0:1, :] + shift[0:1, :]).astype(BF)

    each_block(before)
    attend_back(table, bias, queries, *thirds(states), stats, out, dq, *thirds(dstates))
    grads[:D, :] = tn(value_b[...], dq[...]).astype(BF)
    grads[D:, :] = tn(mixed[...], dzb[...]).astype(BF)

    def after(at):
        back = dz2[at, :] + nt(dq[at, :], weight[:, :D])
        unit, scale = normalized(z1[at, :])
        bias_grads[1:2, :] += column_sum(back * unit)
        bias_grads[2:3, :] += column_sum(back)
        dz1[at, :] = normalized_back(back * gain[0:1, :], unit, scale)

    each_block(after)


def decoder_cross_back(table, bias, dz2, z1, queries, states, mixed, stats, weights, small):
    outs = (shaped(2 * D, D, BF), shaped(8, D, F32), shaped(T, 2 * D, BF), shaped(T, D, F32))
    return kernel_call(
        decoder_cross_back_kernel,
        outs,
        (table, bias, dz2, z1, queries, states, mixed, stats, weights["cross_weight"], small["norm_gain"], small["norm_shift"]),
        scalars=1,
        scratch=[pltpu.VMEM((T, D), BF)] * 4,
        flops=12 * FLOP_UNIT,
    )


def self_back(table, bias, dz, x, joined, mixed, stats, weight_in, weight_out, grads, bias_grads, dzb, out, djoined):
    def before(at):
        bias_grads[0:1, :] += column_sum(dz[at, :])
        low = dz[at, :].astype(BF)
        dzb[at, :] = low
        out[at, :] = nt(low, weight_out[...]).astype(BF)

    each_block(before)
    attend_back(table, bias, *thirds(joined), stats, out, *thirds(djoined))
    weight_grads(x, djoined, grads, 0, 3)
    grads[3 * D :, :] = tn(mixed[...], dzb[...]).astype(BF)


def decoder_self_back_kernel(
    table, bias, dz, x, joined, mixed, stats, glance, places, weight_in, weight_out,
    grads, bias_grads, target_grad, source_grad,
    dzb, out, djoined, dcopied,
):
    bias_grads[...] = jnp.zeros_like(bias_grads)
    self_back(table, bias, dz, x, joined, mixed, stats, weight_in, weight_out, grads, bias_grads, dzb, out, djoined)

    def after(at):
        back = dz[at, :] + nt(djoined[at, :], weight_in[...])
        kept = jnp.concatenate([glance[at, :]] * 4, axis=1) > 0.5
        target_grad[at, :] = jnp.where(kept, back, 0.0)
        dcopied[at, :] = jnp.where(kept, 0.0, back).astype(BF)

    each_block(after)
    source_grad[...] = jnp.zeros_like(source_grad)

    def window(w, carry):
        start = pl.multiple_of(table[0, 1 + w], 16)
        at = pl.ds(start, WIN)
        lanes = lax.broadcasted_iota(jnp.int32, (WIN, WIN), 1) + start
        inside = jnp.max(bias[w], axis=1, keepdims=True) == 0.0
        hit = jnp.where((places[at, :] == lanes) & inside, 1.0, 0.0).astype(BF)
        source_grad[at, :] = source_grad[at, :] + tn(hit, dcopied[at, :])
        return carry

    lax.fori_loop(0, table[0, 0], window, 0)


def decoder_self_back(table, bias, dz, x, joined, mixed, stats, glance, places, weights):
    outs = (shaped(4 * D, D, BF), shaped(8, D, F32), shaped(T, D, F32), shaped(T, D, F32))
    return kernel_call(
        decoder_self_back_kernel,
        outs,
        (table, bias, dz, x, joined, mixed, stats, glance, places, weights["self_in"], weights["self_out"]),
        scalars=1,
        scratch=[pltpu.VMEM((T, D), BF), pltpu.VMEM((T, D), BF), pltpu.VMEM((T, 3 * D), BF), pltpu.VMEM((T, D), BF)],
        flops=16 * FLOP_UNIT,
    )


def encoder_self_back_kernel(
    table, bias, dz, source, joined, mixed, stats, copies_grad, weight_in, weight_out, gain, shift,
    grads, bias_grads, source_grad,
    x, dzb, out, djoined,
):
    bias_grads[...] = jnp.zeros_like(bias_grads)

    def first(at):
        unit, _ = normalized(source[at, :].astype(F32))
        x[at, :] = (unit * gain[2:3, :] + shift[2:3, :]).astype(BF)

    each_block(first)
    self_back(table, bias, dz, x, joined, mixed, stats, weight_in, weight_out, grads, bias_grads, dzb, out, djoined)

    def after(at):
        back = dz[at, :] + nt(djoined[at, :], weight_in[...])
        unit, scale = normalized(source[at, :].astype(F32))
        bias_grads[1:2, :] += column_sum(back * unit)
        bias_grads[2:3, :] += column_sum(back)
        source_grad[at, :] = normalized_back(back * gain[2:3, :], unit, scale) + copies_grad[at, :]

    each_block(after)


def encoder_self_back(table, bias, dz, source, joined, mixed, stats, copies_grad, weights, small):
    outs = (shaped(4 * D, D, BF), shaped(8, D, F32), shaped(T, D, F32))
    return kernel_call(
        encoder_self_back_kernel,
        outs,
        (table, bias, dz, source, joined, mixed, stats, copies_grad, weights["self_in"], weights["self_out"], small["norm_gain"], small["norm_shift"]),
        scalars=1,
        scratch=[pltpu.VMEM((T, D), BF), pltpu.VMEM((T, D), BF), pltpu.VMEM((T, D), BF), pltpu.VMEM((T, 3 * D), BF)],
        flops=16 * FLOP_UNIT,
    )


def row_pass(source, target, cotangent, lengths, hamming, priority, copies, encoder, decoder, enc_small, dec_small):
    table, bias, glance, places = row_layout(lengths, hamming, priority, copies)
    e_joined, e_mixed, e_stats, e_z1 = encoder_self(table, bias, source, encoder, enc_small)
    x, d_joined, d_mixed, d_stats, d_z1 = decoder_self(table, bias, source, target, glance, places, decoder, dec_small)
    active, slope, e_z2, memory, states = encoder_ff(e_z1, encoder, enc_small)
    queries, c_mixed, c_stats, d_z2 = decoder_cross(table, bias, d_z1, states, decoder, dec_small)
    decoded, d_ff, d_ff_bias, d_ex_bias, dz2 = decoder_ff(d_z2, cotangent, decoder, dec_small)
    d_cross, d_cross_bias, dstates, dz1 = decoder_cross_back(table, bias, dz2, d_z1, queries, states, c_mixed, c_stats, decoder, dec_small)
    d_self, d_self_bias, target_grad, copies_grad = decoder_self_back(table, bias, dz1, x, d_joined, d_mixed, d_stats, glance, places, decoder)
    e_cross, e_ff, e_ff_bias, e_ex_bias, e_dz1 = encoder_ff_back(dstates, e_z1, e_z2, active, slope, encoder, enc_small)
    e_self, e_self_bias, source_grad = encoder_self_back(table, bias, e_dz1, source, e_joined, e_mixed, e_stats, copies_grad, encoder, enc_small)
    enc_rows = jnp.concatenate(
        [
            e_ex_bias[0:1].reshape(4, D),
            e_self_bias[0:1], e_ff_bias[3:4], e_ff_bias[0:1],
            e_ff_bias[4:5], e_ff_bias[1:2], e_self_bias[1:2],
            e_ff_bias[5:6], e_ff_bias[2:3], e_self_bias[2:3],
            jnp.zeros((3, D), F32),
        ],
        axis=0,
    )
    dec_rows = jnp.concatenate(
        [
            d_ex_bias[0:1].reshape(4, D),
            d_self_bias[0:1], d_ff_bias[2:3], d_cross_bias[0:1],
            d_cross_bias[1:2], d_ff_bias[3:4], d_ff_bias[0:1],
            d_cross_bias[2:3], d_ff_bias[4:5], d_ff_bias[1:2],
            jnp.zeros((3, D), F32),
        ],
        axis=0,
    )
    enc_grads = (e_ff, e_cross, e_self, enc_rows)
    dec_grads = (d_ff, d_cross, d_self, dec_rows)
    return memory, decoded, source_grad, target_grad, enc_grads, dec_grads


def swapped(value, axis, bit):
    count = lax.axis_size(axis)
    return lax.ppermute(value, axis, [(i, i ^ (1 << bit)) for i in range(count)])


def parted(value, bit):
    half = value.shape[0] // 2
    kept = lax.dynamic_slice_in_dim(value, bit * half, half, 0)
    sent = lax.dynamic_slice_in_dim(value, (1 - bit) * half, half, 0)
    return kept, sent


def joined_halves(own, other, bit):
    return jnp.where(bit == 0, jnp.concatenate([own, other], 0), jnp.concatenate([other, own], 0))


def summed(enc, dec, leading):
    index = lax.axis_index("dp")
    bits = (lax.axis_size("dp") - 1).bit_length()
    for b in range(bits):
        bit = (index >> b) & 1
        out = []
        for value in (enc, dec):
            kept, sent = parted(value, bit)
            got = swapped(sent, "dp", b)
            out.append((kept.astype(F32) + got.astype(F32)).astype(BF))
        enc, dec = out
    kept = jnp.where(leading, enc, dec)
    sent = jnp.where(leading, dec, enc)
    got = swapped(sent, "pipe", 0)
    total = (kept.astype(F32) + got.astype(F32)).astype(BF)
    for b in reversed(range(bits)):
        bit = (index >> b) & 1
        total = joined_halves(total, swapped(total, "dp", b), bit)
    return total


NAMES = ("self_in", "self_out", "expand", "contract", "cross_weight")


def per_device(
    embeddings, cotangent, lengths, copy_index, priority, hamming,
    self_in, self_out, cross_weight, expand, contract,
    expand_bias, branch_bias, norm_gain, norm_shift,
):
    pipe = lax.axis_index("pipe")
    leading = pipe == 0
    core = lax.axis_index("dp") & 1
    own_rows = embeddings[0]
    mine, theirs = parted(own_rows, pipe)
    got = swapped(theirs, "pipe", 0)
    source = jnp.where(leading, mine, got)
    target = jnp.where(leading, got, mine)

    big = {
        "self_in": self_in[0], "self_out": self_out[0], "cross_weight": cross_weight[0],
        "expand": expand[0], "contract": contract[0],
    }
    small = {
        "expand_bias": expand_bias, "branch_bias": branch_bias[0],
        "norm_gain": norm_gain[0], "norm_shift": norm_shift[0],
    }
    encoder, decoder = {}, {}
    for name in NAMES:
        own = big[name]
        kept, _ = parted(own, core)
        half = swapped(kept, "pipe", 0)
        other = joined_halves(half, swapped(half, "dp", 0), core)
        encoder[name] = jnp.where(leading, own, other)
        decoder[name] = jnp.where(leading, other, own)
    packed = jnp.concatenate([small["expand_bias"].reshape(4, D), small["branch_bias"], small["norm_gain"], small["norm_shift"]], 0)
    packed_other = swapped(packed, "pipe", 0)
    enc_packed = jnp.where(leading, packed, packed_other)
    dec_packed = jnp.where(leading, packed_other, packed)

    def unpacked(rows):
        return {
            "expand_bias": rows[:4].reshape(1, FF), "branch_bias": rows[4:7],
            "norm_gain": rows[7:10], "norm_shift": rows[10:13],
        }

    def own_half(value):
        return parted(value, pipe)[0]

    memory, decoded, source_grad, target_grad, enc_grads, dec_grads = row_pass(
        source, target, own_half(cotangent),
        own_half(lengths), own_half(hamming),
        own_half(priority).reshape(T // WIN, WIN), own_half(copy_index).reshape(T // WIN, WIN),
        encoder, decoder, unpacked(enc_packed), unpacked(dec_packed),
    )

    def rows_out(first, second):
        sent = jnp.where(leading, second, first).astype(BF)
        kept = jnp.where(leading, first, second)
        got = swapped(sent, "pipe", 0).astype(F32)
        return joined_halves(kept, got, pipe)[None]

    layer_out = rows_out(memory, decoded)
    embedding_grad = rows_out(source_grad, target_grad)

    ff = summed(enc_grads[0], dec_grads[0], leading)
    rest_enc = jnp.concatenate([enc_grads[1], enc_grads[2]], 0)
    rest_dec = jnp.concatenate([dec_grads[1], dec_grads[2]], 0)
    rest = summed(rest_enc, rest_dec, leading)
    rows = jnp.where(leading, enc_grads[3], dec_grads[3])
    rows_sent = jnp.where(leading, dec_grads[3], enc_grads[3])
    rows = rows + swapped(rows_sent, "pipe", 0)
    rows = lax.psum(rows, "dp")

    def wide(part, count):
        return jnp.concatenate([part[i * D : (i + 1) * D] for i in range(count)], axis=1).astype(F32)[None]

    return (
        layer_out,
        embedding_grad,
        wide(rest[2 * D : 5 * D], 3),
        rest[5 * D :].astype(F32)[None],
        wide(rest[: 2 * D], 2),
        wide(ff[:FF], 4),
        ff[FF:].astype(F32)[None],
        rows[:4].reshape(1, FF),
        rows[4:7][None],
        rows[7:10][None],
        rows[10:13][None],
    )


def solution(mesh):
    return jax.shard_map(
        per_device,
        mesh=mesh,
        in_specs=(
            P("pipe", "dp", None),
            P("dp", None),
            P("dp", None),
            P("dp"),
            P("dp"),
            P("dp", None),
            P("pipe", None, None),
            P("pipe", None, None),
            P("pipe", None, None),
            P("pipe", None, None),
            P("pipe", None, None),
            P("pipe", None),
            P("pipe", None, None),
            P("pipe", None, None),
            P("pipe", None, None),
        ),
        out_specs=(
            P("pipe", "dp", None),
            P("pipe", "dp", None),
            P("pipe", None, None),
            P("pipe", None, None),
            P("pipe", None, None),
            P("pipe", None, None),
            P("pipe", None, None),
            P("pipe", None),
            P("pipe", None, None),
            P("pipe", None, None),
            P("pipe", None, None),
        ),
        check_vma=False,
    )
```

time: 2540 us -> 667 us (0.26)
  starting transfers between devices: 705 us -> 44.8 us
  waiting for transfers between devices: 641 us -> 202 us
  other arithmetic: 455 us -> 62.1 us
  matrix products: 353 us -> 0 us
  local copies, waits for them, and re-layouts: 268 us -> 47.5 us
  Pallas kernels: 0 us -> 220 us
    ppermute x8 -> x41, starting transfers between devices: 705 us -> 44.8 us  [swapped(): return lax.ppermute(value, axis, [(i, i ^ 1 << bit) for i in range(count)])]
    dot_general x74 -> x0, matrix products: 353 us -> none  [the longest x38 129 us: product(): return jnp.dot(left, right, precision=PRECISION)]
    ppermute x8 -> x41, waiting for transfers between devices: 451 us -> 202 us  [swapped(): return lax.ppermute(value, axis, [(i, i ^ 1 << bit) for i in range(count)])]
    pallas_call x0 -> x10, Pallas kernels: none -> 220 us  [kernel_call(): pl.pallas_call(body, out_shape=tuple(outs), in_specs=[SMEM] * scalars + [...]
    psum x1 -> x0, waiting for transfers between devices: 190 us -> none  [per_device(): part = lax.psum(pending, 'dp')]
    sub x8 -> x0, other arithmetic: 170 us -> none  [one_block(): raised = jnp.exp(scores - highest)]
    reduce_sum x42 -> x0, other arithmetic: 110 us -> none  [the longest x4 63.2 us: one_block(): raised = jnp.exp(scores - highest)]
    dynamic_update_slice x24 -> x0, local copies, waits for them, and re-layouts: 95.4 us -> none  [attend(): mixed = lax.map(jax.checkpoint(one_block), (query_blocks, segment_blocks))]
  transfers between devices with their start and end apart: 9 -> 41, of which waited for: 5 -> 13; matrix products, arithmetic and copies ran while one was open for 2% -> 14% of each run, Pallas kernels for 0% -> 16%
where the time goes in v1:
time: 667 us; the launch traced here: 654 us
  Pallas kernels  220 us (33%)
  waiting for transfers between devices  202 us (30%)
  blocking collectives  76.3 us (11%)
  other arithmetic  62.1 us (9%)
  local copies, waits for them, and re-layouts  47.5 us (7%)
  starting transfers between devices  44.8 us (7%)
    pallas_call x10, Pallas kernels, kernel_call(): pl.pallas_call(body, out_shape=tuple(outs), in_specs=[SMEM] * scalars + [...  220 us
    ppermute x41, waiting for transfers between devices, swapped(): return lax.ppermute(value, axis, [(i, i ^ 1 << bit) for i in range(count)])  202 us
    psum x1, blocking collectives, per_device(): rows = lax.psum(rows, 'dp')  76.3 us
    ppermute x41, starting transfers between devices, swapped(): return lax.ppermute(value, axis, [(i, i ^ 1 << bit) for i in range(count)])  44.8 us
    select_n x10, other arithmetic, joined_halves(): jnp.where(bit == 0, jnp.concatenate([own, other], 0), jnp.concatenate([ot...  14.6 us
  transfers between devices with their start and end apart: 41, of which 13 were waited for; matrix products, arithmetic and copies ran while one was open for 14% of the time, Pallas kernels for 16%

profile of v1, /device:TPU:1, one launch (start us, length us, event | category | flops | bytes accessed | tf_op | source)
XLA Modules:
  0.0 654.1 jit_solution(7291901215015571407)
XLA Ops:
  24.4 26.9 %collective-permute-done.5 = f32[13,512]{1,0:T(8,128)S(1)} collective-permute-done((f32[13,512]{1,0:T(8,128)S(1)}, f32[13,512]{1,0:T(8,128)S(1)}, u32[]{:S(2)}, u32[]{:S(2)}) %collective-permute-start.5) | collective-permute-done | bytes 26656 | tf_op jit(solution)/shard_map/ppermute | solution.py:688
  59.1 48.3 %collective-permute-done.10 = bf16[256,1024]{1,0:T(8,128)(2,1)S(1)} collective-permute-done((bf16[256,1024]{1,0:T(8,128)(2,1)}, bf16[256,1024]{1,0:T(8,128)(2,1)S(1)}, u32[]{:S(2)}, u32[]{:S(2)}) %collective-permute-start.10) | collective-permute-done | bytes 524320 | tf_op jit(solution)/shard_map/ppermute | solution.py:688
  120.7 18.8 %shard_map.231 = (bf16[1024,1536]{1,0:T(8,128)(2,1)}, bf16[1024,512]{1,0:T(8,128)(2,1)}, f32[68,2,256]{2,1,0:T(2,128)}, f32[1024,512]{1,0:T(8,128)}) custom-call(s32[1,128]{1,0:T(1,128)} %get-tuple-element.54.table, f32[17,128,128]{2,1,0:T(8,128)} %get-tuple-element.55.bias, bf16[1024,512]{1,0:T(8,128)(2,1)} %get-tuple-element.114.source, ...), custom_call_target="tpu_custom_call" | custom-call | flops 4294967296 | bytes 10709504 | tf_op jit(solution)/shard_map/pallas_call | solution.py:79
  139.5 21.9 %shard_map.233 = (bf16[1024,512]{1,0:T(8,128)(2,1)}, bf16[1024,1536]{1,0:T(8,128)(2,1)}, bf16[1024,512]{1,0:T(8,128)(2,1)}, f32[68,2,256]{2,1,0:T(2,128)}, f32[1024,512]{1,0:T(8,128)}) custom-call(s32[1,128]{1,0:T(1,128)} %get-tuple-element.54.table, f32[17,128,128]{2,1,0:T(8,128)} %get-tuple-element.55.bias, bf16[1024,512]{1,0:T(8,128)(2,1)} %get-tuple-element.114.source, ...), custom_call_target="tpu_custom_call" | custom-call | flops 4294967296 | bytes 13842944 | tf_op jit(solution)/shard_map/pallas_call | solution.py:79
  161.4 4.7 bitcast_select_fusion.2
  168.6 19.2 %shard_map.232 = (bf16[1024,2048]{1,0:T(8,128)(2,1)}, bf16[1024,2048]{1,0:T(8,128)(2,1)}, f32[1024,512]{1,0:T(8,128)}, f32[1024,512]{1,0:T(8,128)}, bf16[1024,1024]{1,0:T(8,128)(2,1)}) custom-call(f32[1024,512]{1,0:T(8,128)} %get-tuple-element.56.z1, bf16[512,2048]{1,0:T(8,128)(2,1)} %get-tuple-element.104.expand, f32[1,2048]{1,0:T(1,128)} %bitcast.94, ...), custom_call_target="tpu_custom_call" | custom-call | flops 5368709120 | bytes 22046720 | tf_op jit(solution)/shard_map/pallas_call | solution.py:79
  187.7 17.9 %shard_map.234 = (bf16[1024,512]{1,0:T(8,128)(2,1)}, bf16[1024,512]{1,0:T(8,128)(2,1)}, f32[68,2,256]{2,1,0:T(2,128)}, f32[1024,512]{1,0:T(8,128)}) custom-call(s32[1,128]{1,0:T(1,128)} %get-tuple-element.54.table, f32[17,128,128]{2,1,0:T(8,128)} %get-tuple-element.55.bias, f32[1024,512]{1,0:T(8,128)} %get-tuple-element.60.z1, ...), custom_call_target="tpu_custom_call" | custom-call | flops 3221225472 | bytes 10709504 | tf_op jit(solution)/shard_map/pallas_call | solution.py:79
  205.6 28.6 %shard_map.235 = (f32[1024,512]{1,0:T(8,128)}, bf16[4096,512]{1,0:T(8,128)(2,1)}, f32[8,512]{1,0:T(8,128)}, f32[8,2048]{1,0:T(8,128)}, f32[1024,512]{1,0:T(8,128)}) custom-call(f32[1024,512]{1,0:T(8,128)} %get-tuple-element.62.z2, bf16[512,2048]{1,0:T(8,128)(2,1)} %get-tuple-element.103.expand, f32[1,2048]{1,0:T(1,128)} %bitcast.93, ...), custom_call_target="tpu_custom_call" | custom-call | flops 12884901888 | bytes 15837184 | tf_op jit(solution)/shard_map/pallas_call | solution.py:79
  234.3 25.6 %shard_map.236 = (bf16[1024,512]{1,0:T(8,128)(2,1)}, f32[8,512]{1,0:T(8,128)}, bf16[1024,1024]{1,0:T(8,128)(2,1)}, f32[1024,512]{1,0:T(8,128)}) custom-call(s32[1,128]{1,0:T(1,128)} %get-tuple-element.54.table, f32[17,128,128]{2,1,0:T(8,128)} %get-tuple-element.55.bias, f32[1024,512]{1,0:T(8,128)} %get-tuple-element.64.dz2, ...), custom_call_target="tpu_custom_call" | custom-call | flops 6442450944 | bytes 15962624 | tf_op jit(solution)/shard_map/pallas_call | solution.py:79
  259.9 24.8 %shard_map.237 = (bf16[1024,512]{1,0:T(8,128)(2,1)}, bf16[4096,512]{1,0:T(8,128)(2,1)}, f32[8,512]{1,0:T(8,128)}, f32[8,2048]{1,0:T(8,128)}, f32[1024,512]{1,0:T(8,128)}) custom-call(bf16[1024,1024]{1,0:T(8,128)(2,1)} %get-tuple-element.68.dstates, f32[1024,512]{1,0:T(8,128)} %get-tuple-element.56.z1, f32[1024,512]{1,0:T(8,128)} %get-tuple-element.69.z2, ...), custom_call_target="tpu_custom_call" | custom-call | flops 10737418240 | bytes 27357184 | tf_op jit(solution)/shard_map/pallas_call | solution.py:79
  288.4 31.3 %shard_map.238 = (bf16[2048,512]{1,0:T(8,128)(2,1)}, f32[8,512]{1,0:T(8,128)}, f32[1024,512]{1,0:T(8,128)}, f32[1024,512]{1,0:T(8,128)}) custom-call(s32[1,128]{1,0:T(1,128)} %get-tuple-element.54.table, f32[17,128,128]{2,1,0:T(8,128)} %get-tuple-element.55.bias, f32[1024,512]{1,0:T(8,128)} %get-tuple-element.76.dz, bf16[1024,512]{1,0:T(8,128)(2,1)} %get-tuple-element.77.x, ...), custom_call_target="tpu_custom_call" | custom-call | flops 8589934592 | bytes 18047488 | tf_op jit(solution)/shard_map/pallas_call | solution.py:79
  323.7 28.3 %shard_map.239 = (bf16[2048,512]{1,0:T(8,128)(2,1)}, f32[8,512]{1,0:T(8,128)}, f32[1024,512]{1,0:T(8,128)}) custom-call(s32[1,128]{1,0:T(1,128)} %get-tuple-element.54.table, f32[17,128,128]{2,1,0:T(8,128)} %get-tuple-element.55.bias, f32[1024,512]{1,0:T(8,128)} %get-tuple-element.72.dz, bf16[1024,512]{1,0:T(8,128)(2,1)} %get-tuple-element.114.source, ...), custom_call_target="tpu_custom_call" | custom-call | flops 8589934592 | bytes 17011200 | tf_op jit(solution)/shard_map/pallas_call | solution.py:79
  368.5 13.8 %collective-permute-done.19 = bf16[768,512]{1,0:T(8,128)(2,1)S(1)} collective-permute-done((bf16[768,512]{1,0:T(8,128)(2,1)S(1)}, bf16[768,512]{1,0:T(8,128)(2,1)S(1)}, u32[]{:S(2)}, u32[]{:S(2)}) %collective-permute-start.19) | collective-permute-done | bytes 786464 | tf_op jit(solution)/shard_map/ppermute | solution.py:688
  385.6 13.6 %collective-permute-done.15 = bf16[768,512]{1,0:T(8,128)(2,1)S(1)} collective-permute-done((bf16[768,512]{1,0:T(8,128)(2,1)S(1)}, bf16[768,512]{1,0:T(8,128)(2,1)S(1)}, u32[]{:S(2)}, u32[]{:S(2)}) %collective-permute-start.15) | collective-permute-done | bytes 786464 | tf_op jit(solution)/shard_map/ppermute | solution.py:688
  403.0 18.7 %collective-permute-done.32 = bf16[1024,512]{1,0:T(8,128)(2,1)S(1)} collective-permute-done((bf16[1024,512]{1,0:T(8,128)(2,1)S(1)}, bf16[1024,512]{1,0:T(8,128)(2,1)S(1)}, u32[]{:S(2)}, u32[]{:S(2)}) %collective-permute-start.32) | collective-permute-done | bytes 1048608 | tf_op jit(solution)/shard_map/ppermute | solution.py:688
  423.7 20.4 %collective-permute-done.28 = bf16[1024,512]{1,0:T(8,128)(2,1)S(1)} collective-permute-done((bf16[1024,512]{1,0:T(8,128)(2,1)S(1)}, bf16[1024,512]{1,0:T(8,128)(2,1)S(1)}, u32[]{:S(2)}, u32[]{:S(2)}) %collective-permute-start.28) | collective-permute-done | bytes 1048608 | tf_op jit(solution)/shard_map/ppermute | solution.py:688
  449.0 17.9 %collective-permute-done.29 = bf16[512,512]{1,0:T(8,128)(2,1)S(1)} collective-permute-done((bf16[512,512]{1,0:T(8,128)(2,1)S(1)}, bf16[512,512]{1,0:T(8,128)(2,1)S(1)}, u32[]{:S(2)}, u32[]{:S(2)}) %collective-permute-start.29) | collective-permute-done | bytes 524320 | tf_op jit(solution)/shard_map/ppermute | solution.py:688
  472.8 9.4 %collective-permute-done.30 = bf16[256,512]{1,0:T(8,128)(2,1)S(1)} collective-permute-done((bf16[256,512]{1,0:T(8,128)(2,1)S(1)}, bf16[256,512]{1,0:T(8,128)(2,1)S(1)}, u32[]{:S(2)}, u32[]{:S(2)}) %collective-permute-start.30) | collective-permute-done | bytes 262176 | tf_op jit(solution)/shard_map/ppermute | solution.py:688
  505.7 10.5 %collective-permute-done.23 = bf16[192,512]{1,0:T(8,128)(2,1)S(1)} collective-permute-done((bf16[192,512]{1,0:T(8,128)(2,1)S(1)}, bf16[192,512]{1,0:T(8,128)(2,1)S(1)}, u32[]{:S(2)}, u32[]{:S(2)}) %collective-permute-start.23) | collective-permute-done | bytes 196640 | tf_op jit(solution)/shard_map/ppermute | solution.py:688
  516.4 5.5 collective-permute-done.36
  524.0 7.4 %collective-permute-done.24 = bf16[384,512]{1,0:T(8,128)(2,1)S(1)} collective-permute-done((bf16[384,512]{1,0:T(8,128)(2,1)S(1)}, bf16[384,512]{1,0:T(8,128)(2,1)S(1)}, u32[]{:S(2)}, u32[]{:S(2)}) %collective-permute-start.24) | collective-permute-done | bytes 393248 | tf_op jit(solution)/shard_map/ppermute | solution.py:688
  534.8 7.9 %collective-permute-done.37 = bf16[512,512]{1,0:T(8,128)(2,1)S(1)} collective-permute-done((bf16[512,512]{1,0:T(8,128)(2,1)S(1)}, bf16[512,512]{1,0:T(8,128)(2,1)S(1)}, u32[]{:S(2)}, u32[]{:S(2)}) %collective-permute-start.37) | collective-permute-done | bytes 524320 | tf_op jit(solution)/shard_map/ppermute | solution.py:688
  544.1 76.3 %psum.7 = f32[16,512]{1,0:T(8,128)S(1)} all-reduce(f32[16,512]{1,0:T(8,128)S(1)} %select_add_fusion), channel_id=1, replica_groups=mesh['pipe'=2,'dp'=16] {'dp'}, use_global_device_ids=true, to_apply=%region_0.1 | all-reduce | flops 8192 | bytes 65536 | tf_op jit(solution)/shard_map/psum | solution.py:793
  622.8 5.1 collective-permute-start.26
  (246 shorter events, 150.0 us)
Async XLA Ops:
  2.9 105.7 %collective-permute-start.1 = (bf16[256,1536]{1,0:T(8,128)(2,1)}, bf16[256,1536]{1,0:T(8,128)(2,1)}, u32[]{:S(2)}, u32[]{:S(2)}) collective-permute-start(bf16[256,1536]{1,0:T(8,128)(2,1)} %dynamic-slice_bitcast_fusion.3), channel_id=1, source_target_pairs={{0,16},{16,0},{1,17},{17,1},{2,18},{18,2},{3,19},{19,3},{4,20},{20... | collective-permute-start | bytes 2359304 | tf_op jit(solution)/shard_map/ppermute | solution.py:688
  5.9 46.5 %collective-permute-start.3 = (bf16[256,512]{1,0:T(8,128)(2,1)S(1)}, bf16[256,512]{1,0:T(8,128)(2,1)}, u32[]{:S(2)}, u32[]{:S(2)}) collective-permute-start(bf16[256,512]{1,0:T(8,128)(2,1)S(1)} %dynamic-slice_bitcast_fusion.5), channel_id=1, source_target_pairs={{0,16},{16,0},{1,17},{17,1},{2,18},{18,2},{3,19},{19,3},{4,20},{20... | collective-permute-start | bytes 786440 | tf_op jit(solution)/shard_map/ppermute | solution.py:688
  8.4 103.3 %collective-permute-start = (bf16[1024,512]{1,0:T(8,128)(2,1)}, bf16[1024,512]{1,0:T(8,128)(2,1)}, u32[]{:S(2)}, u32[]{:S(2)}) collective-permute-start(bf16[1024,512]{1,0:T(8,128)(2,1)} %dynamic-slice_bitcast_fusion.2), channel_id=1, source_target_pairs={{0,16},{16,0},{1,17},{17,1},{2,18},{18,2},{3,19},{19,3},{4,20},{20... | collective-permute-start | bytes 3145736 | tf_op jit(solution)/shard_map/ppermute | solution.py:688
  11.1 40.2 %collective-permute-start.5 = (f32[13,512]{1,0:T(8,128)S(1)}, f32[13,512]{1,0:T(8,128)S(1)}, u32[]{:S(2)}, u32[]{:S(2)}) collective-permute-start(f32[13,512]{1,0:T(8,128)S(1)} %pad_maximum_fusion), channel_id=1, source_target_pairs={{0,16},{16,0},{1,17},{17,1},{2,18},{18,2},{3,19},{19,3},{4,20},{20... | collective-permute-start | bytes 79880 | tf_op jit(solution)/shard_map/ppermute | solution.py:688
  13.5 97.6 %collective-permute-start.6 = (bf16[256,2048]{1,0:T(8,128)(2,1)}, bf16[256,2048]{1,0:T(8,128)(2,1)}, u32[]{:S(2)}, u32[]{:S(2)}) collective-permute-start(bf16[256,2048]{1,0:T(8,128)(2,1)} %dynamic-slice_bitcast_fusion.1), channel_id=1, source_target_pairs={{0,16},{16,0},{1,17},{17,1},{2,18},{18,2},{3,19},{19,3},{4,20},{20... | collective-permute-start | bytes 3145736 | tf_op jit(solution)/shard_map/ppermute | solution.py:688
  51.3 60.3 %collective-permute-start.8 = (bf16[1024,512]{1,0:T(8,128)(2,1)}, bf16[1024,512]{1,0:T(8,128)(2,1)S(1)}, u32[]{:S(2)}, u32[]{:S(2)}) collective-permute-start(bf16[1024,512]{1,0:T(8,128)(2,1)} %dynamic-slice_bitcast_fusion), channel_id=1, source_target_pairs={{0,16},{16,0},{1,17},{17,1},{2,18},{18,2},{3,19},{19,3},{4,20},{20... | collective-permute-start | bytes 3145736 | tf_op jit(solution)/shard_map/ppermute | solution.py:688
  56.7 50.7 %collective-permute-start.10 = (bf16[256,1024]{1,0:T(8,128)(2,1)}, bf16[256,1024]{1,0:T(8,128)(2,1)S(1)}, u32[]{:S(2)}, u32[]{:S(2)}) collective-permute-start(bf16[256,1024]{1,0:T(8,128)(2,1)} %dynamic-slice_bitcast_fusion.4), channel_id=1, source_target_pairs={{0,16},{16,0},{1,17},{17,1},{2,18},{18,2},{3,19},{19,3},{4,20},{20... | collective-permute-start | bytes 1572872 | tf_op jit(solution)/shard_map/ppermute | solution.py:688
  111.1 50.3 %collective-permute-start.7 = (bf16[256,2048]{1,0:T(8,128)(2,1)}, bf16[256,2048]{1,0:T(8,128)(2,1)}, u32[]{:S(2)}, u32[]{:S(2)}) collective-permute-start(bf16[256,2048]{1,0:T(8,128)(2,1)} %collective-permute-done.6), channel_id=1, source_target_pairs={{0,1},{1,0},{2,3},{3,2},{4,5},{5,4},{6,7},{7,6},{8,9},{9,8},{10,11... | collective-permute-start | bytes 3145736 | tf_op jit(solution)/shard_map/ppermute | solution.py:688
  111.6 54.5 %collective-permute-start.9 = (bf16[1024,512]{1,0:T(8,128)(2,1)S(1)}, bf16[1024,512]{1,0:T(8,128)(2,1)S(1)}, u32[]{:S(2)}, u32[]{:S(2)}) collective-permute-start(bf16[1024,512]{1,0:T(8,128)(2,1)S(1)} %collective-permute-done.8), channel_id=1, source_target_pairs={{0,1},{1,0},{2,3},{3,2},{4,5},{5,4},{6,7},{7,6},{8,9},{9,8},{10,11... | collective-permute-start | bytes 3145736 | tf_op jit(solution)/shard_map/ppermute | solution.py:688
  287.9 79.6 %collective-permute-start.27 = (bf16[2048,512]{1,0:T(8,128)(2,1)}, bf16[2048,512]{1,0:T(8,128)(2,1)S(1)}, u32[]{:S(2)}, u32[]{:S(2)}) collective-permute-start(bf16[2048,512]{1,0:T(8,128)(2,1)} %constant_dynamic-slice_fusion.7), channel_id=1, source_target_pairs={{0,1},{1,0},{2,3},{3,2},{4,5},{5,4},{6,7},{7,6},{8,9},{9,8},{10,11... | collective-permute-start | bytes 6291464 | tf_op jit(solution)/shard_map/ppermute | solution.py:688
  322.7 39.0 %collective-permute-start.18 = (bf16[1536,512]{1,0:T(8,128)(2,1)}, bf16[1536,512]{1,0:T(8,128)(2,1)}, u32[]{:S(2)}, u32[]{:S(2)}) collective-permute-start(bf16[1536,512]{1,0:T(8,128)(2,1)} %constant_dynamic-slice_fusion.11), channel_id=1, source_target_pairs={{0,1},{1,0},{2,3},{3,2},{4,5},{5,4},{6,7},{7,6},{8,9},{9,8},{10,11... | collective-permute-start | bytes 4718600 | tf_op jit(solution)/shard_map/ppermute | solution.py:688
  365.2 34.0 %collective-permute-start.15 = (bf16[768,512]{1,0:T(8,128)(2,1)S(1)}, bf16[768,512]{1,0:T(8,128)(2,1)S(1)}, u32[]{:S(2)}, u32[]{:S(2)}) collective-permute-start(bf16[768,512]{1,0:T(8,128)(2,1)S(1)} %constant_dynamic-slice_fusion.14), channel_id=1, source_target_pairs={{0,2},{1,3},{2,0},{3,1},{4,6},{5,7},{6,4},{7,5},{8,10},{9,11},{10,... | collective-permute-start | bytes 2359304 | tf_op jit(solution)/shard_map/ppermute | solution.py:688
  366.4 55.2 %collective-permute-start.32 = (bf16[1024,512]{1,0:T(8,128)(2,1)S(1)}, bf16[1024,512]{1,0:T(8,128)(2,1)S(1)}, u32[]{:S(2)}, u32[]{:S(2)}) collective-permute-start(bf16[1024,512]{1,0:T(8,128)(2,1)S(1)} %constant_dynamic-slice_fusion.2), channel_id=1, source_target_pairs={{0,2},{1,3},{2,0},{3,1},{4,6},{5,7},{6,4},{7,5},{8,10},{9,11},{10,... | collective-permute-start | bytes 3145736 | tf_op jit(solution)/shard_map/ppermute | solution.py:688
  384.4 59.8 %collective-permute-start.28 = (bf16[1024,512]{1,0:T(8,128)(2,1)S(1)}, bf16[1024,512]{1,0:T(8,128)(2,1)S(1)}, u32[]{:S(2)}, u32[]{:S(2)}) collective-permute-start(bf16[1024,512]{1,0:T(8,128)(2,1)S(1)} %constant_dynamic-slice_fusion.6), channel_id=1, source_target_pairs={{0,2},{1,3},{2,0},{3,1},{4,6},{5,7},{6,4},{7,5},{8,10},{9,11},{10,... | collective-permute-start | bytes 3145736 | tf_op jit(solution)/shard_map/ppermute | solution.py:688
  399.5 46.7 %collective-permute-start.16 = (bf16[384,512]{1,0:T(8,128)(2,1)S(1)}, bf16[384,512]{1,0:T(8,128)(2,1)S(1)}, u32[]{:S(2)}, u32[]{:S(2)}) collective-permute-start(bf16[384,512]{1,0:T(8,128)(2,1)S(1)} %constant_dynamic-slice_fusion.13), channel_id=1, source_target_pairs={{0,4},{1,5},{2,6},{3,7},{4,0},{5,1},{6,2},{7,3},{8,12},{9,13},{10,... | collective-permute-start | bytes 1179656 | tf_op jit(solution)/shard_map/ppermute | solution.py:688
  401.3 66.9 %collective-permute-start.21 = (bf16[192,512]{1,0:T(8,128)(2,1)S(1)}, bf16[192,512]{1,0:T(8,128)(2,1)S(1)}, u32[]{:S(2)}, u32[]{:S(2)}) collective-permute-start(bf16[192,512]{1,0:T(8,128)(2,1)S(1)} %constant_dynamic-slice_fusion.8), channel_id=1, source_target_pairs={{0,8},{1,9},{2,10},{3,11},{4,12},{5,13},{6,14},{7,15},{8,0},{9,1},... | collective-permute-start | bytes 589832 | tf_op jit(solution)/shard_map/ppermute | solution.py:688
  422.0 26.0 %collective-permute-start.33 = (bf16[512,512]{1,0:T(8,128)(2,1)S(1)}, bf16[512,512]{1,0:T(8,128)(2,1)S(1)}, u32[]{:S(2)}, u32[]{:S(2)}) collective-permute-start(bf16[512,512]{1,0:T(8,128)(2,1)S(1)} %constant_dynamic-slice_fusion.1), channel_id=1, source_target_pairs={{0,4},{1,5},{2,6},{3,7},{4,0},{5,1},{6,2},{7,3},{8,12},{9,13},{10,... | collective-permute-start | bytes 1572872 | tf_op jit(solution)/shard_map/ppermute | solution.py:688
  448.2 24.6 %collective-permute-start.34 = (bf16[256,512]{1,0:T(8,128)(2,1)S(1)}, bf16[256,512]{1,0:T(8,128)(2,1)S(1)}, u32[]{:S(2)}, u32[]{:S(2)}) collective-permute-start(bf16[256,512]{1,0:T(8,128)(2,1)S(1)} %constant_dynamic-slice_fusion), channel_id=1, source_target_pairs={{0,8},{1,9},{2,10},{3,11},{4,12},{5,13},{6,14},{7,15},{8,0},{9,1},... | collective-permute-start | bytes 786440 | tf_op jit(solution)/shard_map/ppermute | solution.py:688
  469.1 29.1 %collective-permute-start.22 = (bf16[192,512]{1,0:T(8,128)(2,1)}, bf16[192,512]{1,0:T(8,128)(2,1)}, u32[]{:S(2)}, u32[]{:S(2)}) collective-permute-start(bf16[192,512]{1,0:T(8,128)(2,1)} %broadcast_select_fusion.1), channel_id=1, source_target_pairs={{0,16},{16,0},{1,17},{17,1},{2,18},{18,2},{3,19},{19,3},{4,20},{20... | collective-permute-start | bytes 589832 | tf_op jit(solution)/shard_map/ppermute | solution.py:688
  504.2 39.8 %collective-permute-start.40 = (f32[16,512]{1,0:T(8,128)S(1)}, f32[16,512]{1,0:T(8,128)S(1)}, u32[]{:S(2)}, u32[]{:S(2)}) collective-permute-start(f32[16,512]{1,0:T(8,128)S(1)} %broadcast_select_fusion.2), channel_id=1, source_target_pairs={{0,16},{16,0},{1,17},{17,1},{2,18},{18,2},{3,19},{19,3},{4,20},{20... | collective-permute-start | bytes 98312 | tf_op jit(solution)/shard_map/ppermute | solution.py:688
  504.2 126.1 %collective-permute-start.13 = (bf16[1024,512]{1,0:T(8,128)(2,1)}, bf16[1024,512]{1,0:T(8,128)(2,1)}, u32[]{:S(2)}, u32[]{:S(2)}) collective-permute-start(bf16[1024,512]{1,0:T(8,128)(2,1)} %select_convert_fusion), channel_id=1, source_target_pairs={{0,16},{16,0},{1,17},{17,1},{2,18},{18,2},{3,19},{19,3},{4,20},{20... | collective-permute-start | bytes 3145736 | tf_op jit(solution)/shard_map/ppermute | solution.py:688
  532.5 87.8 %collective-permute-start.25 = (bf16[768,512]{1,0:T(8,128)(2,1)}, bf16[768,512]{1,0:T(8,128)(2,1)}, u32[]{:S(2)}, u32[]{:S(2)}) collective-permute-start(bf16[768,512]{1,0:T(8,128)(2,1)} %maximum_select_fusion.11), channel_id=1, source_target_pairs={{0,2},{1,3},{2,0},{3,1},{4,6},{5,7},{6,4},{7,5},{8,10},{9,11},{10,... | collective-permute-start | bytes 2359304 | tf_op jit(solution)/shard_map/ppermute | solution.py:688
  534.7 99.4 %collective-permute-start.12 = (bf16[1024,512]{1,0:T(8,128)(2,1)}, bf16[1024,512]{1,0:T(8,128)(2,1)}, u32[]{:S(2)}, u32[]{:S(2)}) collective-permute-start(bf16[1024,512]{1,0:T(8,128)(2,1)} %select_convert_fusion.1), channel_id=1, source_target_pairs={{0,16},{16,0},{1,17},{17,1},{2,18},{18,2},{3,19},{19,3},{4,20},{20... | collective-permute-start | bytes 3145736 | tf_op jit(solution)/shard_map/ppermute | solution.py:688
  543.2 88.7 %collective-permute-start.38 = (bf16[1024,512]{1,0:T(8,128)(2,1)S(1)}, bf16[1024,512]{1,0:T(8,128)(2,1)}, u32[]{:S(2)}, u32[]{:S(2)}) collective-permute-start(bf16[1024,512]{1,0:T(8,128)(2,1)S(1)} %maximum_select_fusion.10), channel_id=1, source_target_pairs={{0,2},{1,3},{2,0},{3,1},{4,6},{5,7},{6,4},{7,5},{8,10},{9,11},{10,... | collective-permute-start | bytes 3145736 | tf_op jit(solution)/shard_map/ppermute | solution.py:688
  (52 other events, 620.4 us)

commit v2 on v1

v2 whole, which is shorter than its diff:
```python
import functools
import math

import jax
import jax.numpy as jnp
from jax import lax
from jax.experimental import pallas as pl
from jax.experimental.pallas import tpu as pltpu
from jax.sharding import PartitionSpec as P

HEADS = 8
D = 512
FF = 2048
T = 1024
SENTS = 17
WIN = 128
EPSILON = 1e-05
NEG = -1e30
BF = jnp.bfloat16
F32 = jnp.float32
VMEM = pl.BlockSpec(memory_space=pltpu.VMEM)
SMEM = pl.BlockSpec(memory_space=pltpu.SMEM)
BLOCK = 512
STEPS = T // BLOCK


def nn(a, b):
    return jnp.dot(a, b, preferred_element_type=F32)


def nt(a, b):
    return lax.dot_general(a, b, (((1,), (1,)), ((), ())), preferred_element_type=F32)


def tn(a, b):
    return lax.dot_general(a, b, (((0,), (0,)), ((), ())), preferred_element_type=F32)


def normalized(value):
    center = jnp.mean(value, axis=-1, keepdims=True)
    centered = value - center
    spread = jnp.mean(centered * centered, axis=-1, keepdims=True)
    scale = lax.rsqrt(spread + EPSILON)
    return centered * scale, scale


def normalized_back(grad, unit, scale):
    first = jnp.mean(grad, axis=-1, keepdims=True)
    second = jnp.mean(grad * unit, axis=-1, keepdims=True)
    return scale * (grad - first - unit * second)


def folded(value):
    return jnp.sum(value.reshape(value.shape[0] // 8, 8, value.shape[1]), axis=0)


def column_sum(value):
    return jnp.sum(value, axis=0, keepdims=True)


def each_block(body):
    for index in range(STEPS):
        body(pl.ds(index * BLOCK, BLOCK))


def each_chunk(count, size, body):
    def step(index, carry):
        body(pl.multiple_of(index * size, size))
        return carry

    lax.fori_loop(0, count, step, 0)


class Held:
    def __init__(self, ref, copy):
        self.ref, self.copy = ref, copy

    def ready(self):
        if self.copy is not None:
            self.copy.wait()
            self.copy = None
        return self.ref

    def __getitem__(self, index):
        return self.ready()[index]

    @property
    def at(self):
        return self.ready().at

    @property
    def shape(self):
        return self.ref.shape


def ready(value):
    return value.ready() if isinstance(value, (Held, Landing)) else value


LEAVING = {}


def leave(*refs):
    for ref in refs:
        copy, started = LEAVING.get(id(ref), (None, True))
        if not started:
            copy.start()
            LEAVING[id(ref)] = (copy, True)


class Landing:
    def __init__(self, ref, sem):
        self.ref, self.sem = ref, sem

    def ready(self):
        if self.sem is not None:
            pltpu.make_async_copy(self.ref, self.ref, self.sem).wait()
            self.sem = None
        return self.ref

    def __getitem__(self, index):
        return self.ready()[index]

    @property
    def at(self):
        return self.ready().at

    @property
    def shape(self):
        return self.ref.shape


class Raw:
    def __init__(self, value):
        self.value, self.shape, self.dtype = value, value.shape, value.dtype


def bytes_of(x):
    return math.prod(x.shape) * jnp.dtype(x.dtype).itemsize


LARGE = 256 << 10


def kernel_call(body, outs, operands, scalars=0, scratch=(), out_specs=None, flops=0, after=(), direct=False):
    size = sum(bytes_of(x) for x in (*operands, *outs))
    held = size + (sum(bytes_of(x) for x in scratch) if direct else 0)
    count, many, extra = len(operands), len(outs), len(scratch)
    raw = [isinstance(x, Raw) for x in operands]
    comes = [not (direct or r) and i >= scalars and bytes_of(x) >= LARGE for i, (x, r) in enumerate(zip(operands, raw))]
    goes = [not direct and bytes_of(x) >= LARGE for x in outs]
    anywhere = pl.BlockSpec(memory_space=pl.ANY)
    in_specs = [SMEM] * scalars + [anywhere if c or r else VMEM for c, r in zip(comes[scalars:], raw[scalars:])] + [anywhere] * len(after)
    specs = list(out_specs) if out_specs else [VMEM] * many
    specs = [anywhere if g else spec for g, spec in zip(goes, specs)]
    room = [pltpu.VMEM(x.shape, x.dtype) for x, c in zip((*operands, *outs), comes + goes) if c]
    sems = [pltpu.SemaphoreType.DMA((len(room),))] if room else []

    def run(*refs):
        ins, rest = list(refs[:count]), refs[count + len(after) :]
        results, rest = list(rest[:many]), rest[many:]
        own, rest = rest[:extra], rest[extra:]
        buffers, slot = rest[: len(room)], 0
        for i, c in enumerate(comes):
            if c:
                copy = pltpu.make_async_copy(ins[i], buffers[slot], rest[-1].at[slot])
                copy.start()
                ins[i] = Held(buffers[slot], copy)
                slot += 1
        LEAVING.clear()
        for i, g in enumerate(goes):
            if g:
                copy = pltpu.make_async_copy(buffers[slot], results[i], rest[-1].at[slot])
                results[i] = buffers[slot]
                LEAVING[id(results[i])] = (copy, False)
                slot += 1
        body(*ins, *results, *own)
        for value in ins:
            ready(value)
        for i, g in enumerate(goes):
            if g:
                leave(results[i])
        for i, g in enumerate(goes):
            if g:
                LEAVING[id(results[i])][0].wait()
        LEAVING.clear()

    return pl.pallas_call(
        run,
        out_shape=tuple(outs),
        in_specs=in_specs,
        out_specs=tuple(specs),
        scratch_shapes=list(scratch) + room + sems,
        compiler_params=pltpu.CompilerParams(vmem_limit_bytes=held + (3 << 20) if direct else 62 << 20),
        cost_estimate=pl.CostEstimate(flops=flops, bytes_accessed=size, transcendentals=0),
    )(*(x.value if isinstance(x, Raw) else x for x in operands), *after)


def shaped(rows, columns, kind):
    return jax.ShapeDtypeStruct((rows, columns), kind)


def layout_kernel(flags, lengths, hamming, priority, copies, table, bias, glance, places):
    row = flags[0, 0]
    ends = []
    total = jnp.int32(0)
    for j in range(SENTS):
        total = total + lengths[row, j]
        ends.append(total)
    count = jnp.int32(0)
    first = jnp.int32(0)

    def origin(start):
        return jnp.minimum((start // 16) * 16, T - WIN)

    for j in range(SENTS):
        begin = jnp.int32(0) if j == 0 else ends[j - 1]
        opens = (ends[j] - origin(first)) > WIN
        if j == 0:
            opens = jnp.bool_(False)
        first = jnp.where(opens, begin, first)
        count = jnp.where(opens, count + 1, count)
        table[0, 1 + count] = origin(first)
        table[0, 32 + count] = first
        table[0, 64 + count] = ends[j]
    table[0, 0] = count + 1

    lanes = lax.broadcasted_iota(jnp.int32, (8, WIN), 1)
    rows = lax.broadcasted_iota(jnp.int32, (8, WIN), 0)
    place = rows * WIN + lanes
    quota = jnp.zeros((8, WIN), jnp.int32) + (hamming[row, 0] + 1) // 2
    for j in range(SENTS - 1):
        change = (hamming[row, j + 1] + 1) // 2 - (hamming[row, j] + 1) // 2
        quota = quota + jnp.where(place >= ends[j], change, 0)
    part = pl.ds(pl.multiple_of(row * (T // WIN), 8), T // WIN)
    chosen = jnp.where(priority[part, :] < quota, 1.0, 0.0)
    copy = copies[part, :].astype(F32)
    for i in range(T // WIN):
        part = pl.ds(i * WIN, WIN)
        glance[part, :] = jnp.broadcast_to(chosen[i : i + 1, :], (WIN, WIN)).T
        places[part, :] = jnp.broadcast_to(copy[i : i + 1, :], (WIN, WIN)).T.astype(jnp.int32)

    def window(w, carry):
        at = table[0, 1 + w]
        here = lanes + at
        segment = jnp.zeros((8, WIN), F32)
        for j in range(SENTS):
            segment = segment + jnp.where(here >= ends[j], 1.0, 0.0)
        inside = (here >= table[0, 32 + w]) & (here < table[0, 64 + w])
        segment = jnp.where(inside, segment, -1.0)
        across = jnp.broadcast_to(segment[0:1, :], (WIN, WIN))
        down = across.T
        bias[w] = jnp.where((across == down) & (across >= 0.0), 0.0, NEG)
        return carry

    lax.fori_loop(0, count + 1, window, 0)
    table[0, 2 + count] = 0
    bias[count + 1] = jnp.full((WIN, WIN), NEG, F32)


def row_layout(flags, lengths, hamming, priority, copies):
    outs = (
        shaped(1, 128, jnp.int32),
        jax.ShapeDtypeStruct((SENTS + 1, WIN, WIN), F32),
        shaped(T, WIN, F32),
        shaped(T, WIN, jnp.int32),
    )
    return kernel_call(
        layout_kernel,
        outs,
        (flags, lengths, hamming, priority, copies),
        scalars=3,
        out_specs=(SMEM, VMEM, VMEM, VMEM),
        direct=True,
    )


def pair_halves(part):
    low = lax.broadcasted_iota(jnp.int32, (WIN, WIN), 1) < 64
    zero = jnp.zeros_like(part)
    return jnp.concatenate([jnp.where(low, part, zero), jnp.where(low, zero, part)], axis=0)


def pair_join(both):
    low = lax.broadcasted_iota(jnp.int32, (WIN, WIN), 1) < 64
    return jnp.where(low, both[:WIN], both[WIN:])


PAIRS = [slice(i * 128, i * 128 + 128) for i in range(HEADS // 2)]


PAIRS = [slice(i * 128, i * 128 + 128) for i in range(HEADS // 2)]
GROUP = 2


def grouped(table, body):
    def step(index, carry):
        body([index * GROUP + i for i in range(GROUP)])
        return carry

    lax.fori_loop(0, (table[0, 0] + GROUP - 1) // GROUP, step, 0)


def spread(table, windows):
    ats = [pl.ds(pl.multiple_of(table[0, 1 + w], 16), WIN) for w in windows]
    return [(w, pair, at, lanes) for w, at in zip(windows, ats) for pair, lanes in enumerate(PAIRS)]


def masks(bias, windows):
    out = []
    for w in windows:
        masked = bias[w]
        out += [jnp.concatenate([masked, masked], axis=1)] * len(PAIRS)
    return out


def attend(table, bias, queries, keys, values, mixed, stats):
    bias, queries, keys, values = map(ready, (bias, queries, keys, values))

    def body(windows):
        parts = spread(table, windows)
        masked = masks(bias, windows)
        query = [pair_halves(queries[at, lanes]) for _, _, at, lanes in parts]
        key = [keys[at, lanes] for _, _, at, lanes in parts]
        value = [values[at, lanes] for _, _, at, lanes in parts]
        scores = [nt(k, q) + mask for k, q, mask in zip(key, query, masked)]
        highest = [jnp.maximum(jnp.max(s, axis=0, keepdims=True), -1e29) for s in scores]
        raised = [jnp.exp(s - h) for s, h in zip(scores, highest)]
        inverse = [1.0 / jnp.maximum(jnp.sum(r, axis=0, keepdims=True), 1e-30) for r in raised]
        shares = [(r * i).astype(BF) for r, i in zip(raised, inverse)]
        out = [pair_join(tn(s, v)).astype(BF) for s, v in zip(shares, value)]
        for (w, pair, at, lanes), o, h, i in zip(parts, out, highest, inverse):
            mixed[at, lanes] = mixed[at, lanes] + o
            stats[w * 4 + pair, 0:1, :] = h
            stats[w * 4 + pair, 1:2, :] = i

    mixed[...] = jnp.zeros_like(mixed)
    grouped(table, body)


def attend_back(table, bias, queries, keys, values, stats, grad, grad_q, grad_k, grad_v):
    bias, queries, keys, values, stats = map(ready, (bias, queries, keys, values, stats))

    def body(windows):
        parts = spread(table, windows)
        masked = masks(bias, windows)
        query = [pair_halves(queries[at, lanes]) for _, _, at, lanes in parts]
        key = [keys[at, lanes] for _, _, at, lanes in parts]
        value = [values[at, lanes] for _, _, at, lanes in parts]
        out = [pair_halves(grad[at, lanes]) for _, _, at, lanes in parts]
        top = [stats[w * 4 + pair, 0:1, :] for w, pair, _, _ in parts]
        inverse = [stats[w * 4 + pair, 1:2, :] for w, pair, _, _ in parts]
        scores = [nt(k, q) + mask for k, q, mask in zip(key, query, masked)]
        back = [nt(v, o) for v, o in zip(value, out)]
        shares = [jnp.exp(s - h) * i for s, h, i in zip(scores, top, inverse)]
        got_v = [nn(s.astype(BF), o).astype(BF) for s, o in zip(shares, out)]
        total = [jnp.sum(s * b, axis=0, keepdims=True) for s, b in zip(shares, back)]
        scored = [(s * (b - t)).astype(BF) for s, b, t in zip(shares, back, total)]
        got_k = [nn(s, q).astype(BF) for s, q in zip(scored, query)]
        got_q = [(pair_join(tn(s, k)) * 0.125).astype(BF) for s, k in zip(scored, key)]
        for ref, got in zip((grad_q, grad_k, grad_v), (got_q, got_k, got_v)):
            for (_, _, at, lanes), value_got in zip(parts, got):
                ref[at, lanes] = ref[at, lanes] + value_got

    for ref in (grad_q, grad_k, grad_v):
        ref[...] = jnp.zeros_like(ref)
    grouped(table, body)


STATS = jax.ShapeDtypeStruct(((SENTS + 1) * 4, 2, 2 * WIN), F32)


def thirds(ref):
    return tuple(ref.at[:, i * D : (i + 1) * D] for i in range(ref.shape[1] // D))


def put(flags, half, kept, sent, rows, value):
    @pl.when(flags[0, 1] == half)
    def _():
        kept[rows, :] = value

    @pl.when(flags[0, 1] != half)
    def _():
        sent[rows, :] = value


def rows_at(start, count=D):
    return slice(start, start + count)


def scaled(unit, small, slot):
    return unit * small[7 + slot : 8 + slot, :] + small[10 + slot : 11 + slot, :]


def project(x, weight_in, joined, at):
    got = nn(x, weight_in[...])
    joined[at, :D] = (got[:, :D] * 0.125).astype(BF)
    joined[at, D:] = got[:, D:].astype(BF)


def encoder_self_kernel(table, bias, source, weight_in, weight_out, small, joined, mixed, stats, z, x):
    def before(at):
        unit, _ = normalized(source[at, :].astype(F32))
        value = scaled(unit, small, 2)
        x[at, :] = value
        project(value.astype(BF), weight_in, joined, at)

    each_block(before)
    leave(joined)
    attend(table, bias, *thirds(joined), mixed, stats)
    leave(mixed, stats)

    def after(at):
        z[at, :] = x[at, :] + nn(mixed[at, :], weight_out[...]) + small[4:5, :]

    each_block(after)


def copy_hits(bias, places, w, start):
    at = pl.ds(start, WIN)
    lanes = lax.broadcasted_iota(jnp.int32, (WIN, WIN), 1) + start
    inside = jnp.max(bias[w], axis=1, keepdims=True) == 0.0
    return at, jnp.where((places[at, :] == lanes) & inside, 1.0, 0.0).astype(BF)


def kept_rows(glance, at):
    return jnp.concatenate([glance[at, :]] * (D // WIN), axis=1) > 0.5


def decoder_self_kernel(
    table, bias, source, target, glance, places, weight_in, weight_out, small, x, joined, mixed, stats, z, copied
):
    copied[...] = jnp.zeros_like(copied)
    bias, places, source = map(ready, (bias, places, source))

    def gather(windows):
        parts = [copy_hits(bias, places, w, pl.multiple_of(table[0, 1 + w], 16)) for w in windows]
        got = [nn(hit, source[at, :]).astype(BF) for at, hit in parts]
        for (at, _), value in zip(parts, got):
            copied[at, :] = copied[at, :] + value

    grouped(table, gather)

    def before(at):
        value = jnp.where(kept_rows(glance, at), target[at, :].astype(F32), copied[at, :].astype(F32)).astype(BF)
        x[at, :] = value
        project(value, weight_in, joined, at)

    each_block(before)
    leave(joined)
    attend(table, bias, *thirds(joined), mixed, stats)
    leave(mixed, stats)

    def after(at):
        z[at, :] = x[at, :].astype(F32) + nn(mixed[at, :], weight_out[...]) + small[4:5, :]

    each_block(after)


FLOP_UNIT = 2 * T * D * D


ROOT = 0.7978845608028654
CUBE = 0.044715


def gelu_parts(u):
    square = u * u
    bent = jnp.tanh(u * (ROOT + ROOT * CUBE * square))
    half = 0.5 + 0.5 * bent
    slope = half + (u - u * (bent * bent)) * (0.5 * ROOT + 1.5 * ROOT * CUBE * square)
    return u * half, slope


def expand_block(value, expand, small, active, slope, at):
    for j in range(FF // D):
        cols = rows_at(j * D)
        hidden = (nn(value, expand[:, cols]) + small[j : j + 1, :]).astype(BF)
        active[at, cols], slope[at, cols] = gelu_parts(hidden)


def encoder_ff_kernel(z1, expand, contract, cross, small, inner, z2, memory, states, active):
    def block(at):
        unit, _ = normalized(z1[at, :])
        value = scaled(unit, small, 0)
        for j in range(FF // D):
            cols = rows_at(j * D)
            hidden = (nn(value.astype(BF), expand[:, cols]) + small[j : j + 1, :]).astype(BF)
            inner[at, cols] = hidden
            active[at, cols], _ = gelu_parts(hidden)
        total = value + nn(active[at, :], contract[...]) + small[5:6, :]
        z2[at, :] = total
        unit, _ = normalized(total)
        out = scaled(unit, small, 1)
        memory[at, :] = out.astype(BF)
        got = nn(out.astype(BF), cross[...])
        states[at, :D] = got[:, :D].astype(BF)
        states[at, D:] = (got[:, D:] + small[6:7, :]).astype(BF)

    each_block(block)
    leave(inner, z2, memory)


def ff_back(flags, dzb, value_b, active, inner, expand, contract, kept, sent, bias_rows):
    def block(at):
        for j in range(FF // D):
            cols = rows_at(j * D)
            back = nt(dzb[at, :], contract[cols, :])
            inner[at, cols] = (back * inner[at, cols].astype(F32)).astype(BF)

    each_block(block)
    for c in range(FF // D):
        cols = rows_at(c * D)
        put(flags, 1, kept, sent, cols, tn(active[:, cols], dzb[...]).astype(BF))
        put(flags, 0, kept, sent, cols, tn(value_b[...], inner[:, cols]).astype(BF))
        bias_rows[c : c + 1, :] = column_sum(inner[:, cols].astype(F32))


def decoder_ff_kernel(
    flags, z2, expand, contract, small, cotangent,
    decoded, kept, sent, bias_grads, bias_rows, dz2,
    active, inner, value_b, dz, dzb,
):
    bias_grads[...] = jnp.zeros_like(bias_grads)
    offset = flags[0, 0] * T

    def block(at):
        unit, _ = normalized(z2[at, :])
        value = scaled(unit, small, 1)
        value_b[at, :] = value.astype(BF)
        expand_block(value.astype(BF), expand, small, active, inner, at)
        total = value + nn(active[at, :], contract[...]) + small[5:6, :]
        unit, scale = normalized(total)
        decoded[at, :] = scaled(unit, small, 2).astype(BF)
        wanted = cotangent[pl.ds(pl.multiple_of(offset + at.start, BLOCK), BLOCK), :].astype(F32)
        bias_grads[0:1, :] += column_sum(wanted * unit)
        bias_grads[1:2, :] += column_sum(wanted)
        back = normalized_back(wanted * small[9:10, :], unit, scale)
        bias_grads[2:3, :] += column_sum(back)
        dz[at, :] = back
        dzb[at, :] = back.astype(BF)

    each_block(block)
    leave(decoded)
    ff_back(flags, dzb, value_b, active, inner, expand, contract, kept, sent, bias_rows)
    leave(kept, sent)

    def last(at):
        back = dz[at, :] + nt(inner[at, :], expand[...])
        unit, scale = normalized(z2[at, :])
        bias_grads[3:4, :] += column_sum(back * unit)
        bias_grads[4:5, :] += column_sum(back)
        dz2[at, :] = normalized_back(back * small[8:9, :], unit, scale)

    each_block(last)


def encoder_ff_back_kernel(
    flags, z2, dstates, z1, hidden, own_cross, own_expand, own_contract, rest, half, last_half, small,
    cross_grads, kept, sent, bias_grads, bias_rows, dz1,
    cross, expand, contract, active, inner, value_b, memory_b, dz, dzb, sems,
):
    own = (own_cross, own_expand, own_contract, rest, half, last_half)
    cross, expand, contract = fetch_rest(0, flags, *own, cross, expand, contract, sems)
    bias_grads[...] = jnp.zeros_like(bias_grads)

    def block(at):
        unit, scale = normalized(z2[at, :])
        memory_b[at, :] = scaled(unit, small, 1).astype(BF)
        back = nt(dstates[at, :], cross[...])
        bias_grads[0:1, :] += column_sum(dstates[at, D:].astype(F32))
        bias_grads[1:2, :] += column_sum(back * unit)
        bias_grads[2:3, :] += column_sum(back)
        back = normalized_back(back * small[8:9, :], unit, scale)
        bias_grads[3:4, :] += column_sum(back)
        dz[at, :] = back
        dzb[at, :] = back.astype(BF)
        unit, _ = normalized(z1[at, :])
        value_b[at, :] = scaled(unit, small, 0).astype(BF)
        for j in range(FF // D):
            cols = rows_at(j * D)
            active[at, cols], inner[at, cols] = gelu_parts(hidden[at, cols])

    each_block(block)
    ff_back(flags, dzb, value_b, active, inner, expand, contract, kept, sent, bias_rows)
    for c in range(2):
        cross_grads[rows_at(c * D), :] = tn(memory_b[...], dstates[:, rows_at(c * D)]).astype(BF)
    leave(kept, sent, cross_grads)

    def last(at):
        back = dz[at, :] + nt(inner[at, :], expand[...])
        unit, scale = normalized(z1[at, :])
        bias_grads[4:5, :] += column_sum(back * unit)
        bias_grads[5:6, :] += column_sum(back)
        dz1[at, :] = normalized_back(back * small[7:8, :], unit, scale)

    each_block(last)


def encoder_ff_back(flags, dstates, z1, z2, hidden, weights, small, after=()):
    outs = (
        shaped(2 * D, D, BF), shaped(FF, D, BF), shaped(FF, D, BF),
        shaped(8, D, F32), shaped(8, D, F32), shaped(T, D, F32),
    )
    return kernel_call(
        encoder_ff_back_kernel,
        outs,
        (flags, z2, dstates, z1, hidden, *map(Raw, weights), small),
        scalars=1,
        scratch=[
            pltpu.VMEM((D, 2 * D), BF),
            pltpu.VMEM((D, FF), BF),
            pltpu.VMEM((FF, D), BF),
            pltpu.VMEM((T, FF), BF),
            pltpu.VMEM((T, FF), BF),
            pltpu.VMEM((T, D), BF),
            pltpu.VMEM((T, D), BF),
            pltpu.VMEM((T, D), F32),
            pltpu.VMEM((T, D), BF),
            pltpu.SemaphoreType.DMA((3,)),
        ],
        flops=22 * FLOP_UNIT,
        after=after,
    )


def decoder_cross_kernel(table, bias, z1, states, weight, small, queries, mixed, stats, z2, x):
    def before(at):
        unit, _ = normalized(z1[at, :])
        value = scaled(unit, small, 0)
        x[at, :] = value
        queries[at, :] = (nn(value.astype(BF), weight[:, :D]) * 0.125).astype(BF)

    each_block(before)
    attend(table, bias, queries, *thirds(states), mixed, stats)

    def after(at):
        z2[at, :] = x[at, :] + nn(mixed[at, :], weight[:, D:]) + small[6:7, :]

    each_block(after)


def decoder_cross_back_kernel(
    table, bias, dz2, z1, queries, states, mixed, stats, weight, small,
    grads, bias_grads, dstates, dz1,
    value_b, dzb, out, dq,
):
    bias_grads[...] = jnp.zeros_like(bias_grads)

    def before(at):
        bias_grads[0:1, :] += column_sum(dz2[at, :])
        low = dz2[at, :].astype(BF)
        dzb[at, :] = low
        out[at, :] = nt(low, weight[:, D:]).astype(BF)
        unit, _ = normalized(z1[at, :])
        value_b[at, :] = scaled(unit, small, 0).astype(BF)

    each_block(before)
    attend_back(table, bias, queries, *thirds(states), stats, out, dq, *thirds(dstates))
    leave(dstates)
    grads[:D, :] = tn(value_b[...], dq[...]).astype(BF)
    grads[D:, :] = tn(mixed[...], dzb[...]).astype(BF)
    leave(grads)

    def after(at):
        back = dz2[at, :] + nt(dq[at, :], weight[:, :D])
        unit, scale = normalized(z1[at, :])
        bias_grads[1:2, :] += column_sum(back * unit)
        bias_grads[2:3, :] += column_sum(back)
        dz1[at, :] = normalized_back(back * small[7:8, :], unit, scale)

    each_block(after)


def self_back(table, bias, flags, dz, x, joined, mixed, stats, weight_in, weight_out, cross, kept, sent, acc, dzb, out, djoined):
    acc[...] = jnp.zeros_like(acc)

    def before(at):
        acc[0:1, :] += column_sum(dz[at, :])
        low = dz[at, :].astype(BF)
        dzb[at, :] = low
        out[at, :] = nt(low, weight_out[...]).astype(BF)

    each_block(before)
    attend_back(table, bias, *thirds(joined), stats, out, *thirds(djoined))
    for half in range(2):
        put(flags, half, kept, sent, rows_at(0), cross[rows_at(half * D), :])
    for c in range(3):
        value = tn(x[...], djoined[:, rows_at(c * D)]).astype(BF)
        put(flags, c // 2, kept, sent, rows_at(D + c % 2 * D), value)
    put(flags, 1, kept, sent, rows_at(2 * D), tn(mixed[...], dzb[...]).astype(BF))


def put_small(flags, kept, sent, rows):
    count = kept.shape[0] - 3 * D
    at = rows_at(3 * D, count)
    filled = jnp.concatenate(rows + [jnp.zeros((count - 13, D), F32)], axis=0).astype(BF)
    put(flags, 0, kept, sent, at, filled)
    put(flags, 1, kept, sent, at, jnp.zeros((count, D), BF))


def decoder_self_back_kernel(
    table, flags, dz, own_in, own_out, half, rest, joined, bias, stats, x, mixed, glance, places,
    cross, ff_bias, ff_rows, cross_bias,
    kept, sent, target_grad, source_grad,
    weight_in, weight_out, acc, dzb, out, djoined, dcopied, sems,
):
    weight_in, weight_out = fetch_self(1, flags, own_in, own_out, half, rest, weight_in, weight_out, sems)
    self_back(table, bias, flags, dz, x, joined, mixed, stats, weight_in, weight_out, cross, kept, sent, acc, dzb, out, djoined)
    put_small(
        flags, kept, sent,
        [
            ff_rows[0:4, :], acc[0:1, :], ff_bias[2:3, :], cross_bias[0:1, :],
            cross_bias[1:2, :], ff_bias[3:4, :], ff_bias[0:1, :],
            cross_bias[2:3, :], ff_bias[4:5, :], ff_bias[1:2, :],
        ],
    )

    def after(at):
        back = dz[at, :] + nt(djoined[at, :], weight_in[...])
        kept_at = kept_rows(glance, at)
        target_grad[at, :] = jnp.where(kept_at, back, 0.0).astype(BF)
        dcopied[at, :] = jnp.where(kept_at, 0.0, back).astype(BF)

    each_block(after)
    leave(target_grad, kept, sent)
    source_grad[...] = jnp.zeros_like(source_grad)
    bias, places = ready(bias), ready(places)

    def scatter(windows):
        parts = [copy_hits(bias, places, w, pl.multiple_of(table[0, 1 + w], 16)) for w in windows]
        got = [tn(hit, dcopied[at, :]).astype(BF) for at, hit in parts]
        for (at, _), value in zip(parts, got):
            source_grad[at, :] = source_grad[at, :] + value

    grouped(table, scatter)


def half_rows(count):
    return 3 * D + 8 * count


def decoder_self_back(table, flags, bias, dz, x, joined, mixed, stats, glance, places, weights, cross, ff_bias, ff_rows, cross_bias, count, after=()):
    half = half_rows(count)
    outs = (shaped(half, D, BF), shaped(half, D, BF), shaped(T, D, BF), shaped(T, D, BF))
    return kernel_call(
        decoder_self_back_kernel,
        outs,
        (table, flags, dz, *map(Raw, weights), joined, bias, stats, x, mixed, glance, places, cross, ff_bias, ff_rows, cross_bias),
        scalars=2,
        scratch=[
            pltpu.VMEM((D, 3 * D), BF), pltpu.VMEM((D, D), BF),
            pltpu.VMEM((8, D), F32), pltpu.VMEM((T, D), BF), pltpu.VMEM((T, D), BF),
            pltpu.VMEM((T, 3 * D), BF), pltpu.VMEM((T, D), BF), pltpu.SemaphoreType.DMA((2,)),
        ],
        flops=18 * FLOP_UNIT,
        after=after,
    )


def encoder_self_back_kernel(
    table, flags, dz, rows, got, own_in, own_out, half, rest, joined, bias, stats, mixed, copies_grad, small,
    cross, ff_bias, ff_rows,
    kept, sent, source_grad,
    source, weight_in, weight_out, acc, x, dzb, out, djoined, sems,
):
    @pl.when(flags[0, 0] == 0)
    def _():
        start((rows.at[rows_at(0, T), :], source, sems.at[2]))

    @pl.when(flags[0, 0] != 0)
    def _():
        start((got, source, sems.at[2]))

    source = Landing(source, sems.at[2])
    weight_in, weight_out = fetch_self(0, flags, own_in, own_out, half, rest, weight_in, weight_out, sems)

    def first(at):
        unit, _ = normalized(source[at, :].astype(F32))
        x[at, :] = scaled(unit, small, 2).astype(BF)

    each_block(first)
    self_back(table, bias, flags, dz, x, joined, mixed, stats, weight_in, weight_out, cross, kept, sent, acc, dzb, out, djoined)

    def after(at):
        back = dz[at, :] + nt(djoined[at, :], weight_in[...])
        unit, scale = normalized(source[at, :].astype(F32))
        acc[1:2, :] += column_sum(back * unit)
        acc[2:3, :] += column_sum(back)
        source_grad[at, :] = (normalized_back(back * small[9:10, :], unit, scale) + copies_grad[at, :].astype(F32)).astype(BF)

    each_block(after)
    put_small(
        flags, kept, sent,
        [
            ff_rows[0:4, :], acc[0:1, :], ff_bias[3:4, :], ff_bias[0:1, :],
            ff_bias[4:5, :], ff_bias[1:2, :], acc[1:2, :],
            ff_bias[5:6, :], ff_bias[2:3, :], acc[2:3, :],
        ],
    )


def encoder_self_back(table, flags, bias, dz, rows, got, joined, mixed, stats, copies_grad, weights, small, cross, ff_bias, ff_rows, count, after=()):
    half = half_rows(count)
    outs = (shaped(half, D, BF), shaped(half, D, BF), shaped(T, D, BF))
    return kernel_call(
        encoder_self_back_kernel,
        outs,
        (table, flags, dz, Raw(rows), Raw(got), *map(Raw, weights), joined, bias, stats, mixed, copies_grad, small, cross, ff_bias, ff_rows),
        scalars=2,
        scratch=[
            pltpu.VMEM((T, D), BF), pltpu.VMEM((D, 3 * D), BF), pltpu.VMEM((D, D), BF),
            pltpu.VMEM((8, D), F32), pltpu.VMEM((T, D), BF), pltpu.VMEM((T, D), BF), pltpu.VMEM((T, D), BF),
            pltpu.VMEM((T, 3 * D), BF), pltpu.SemaphoreType.DMA((3,)),
        ],
        flops=18 * FLOP_UNIT,
        after=after,
    )


def start(*copies):
    for source, target, sem in copies:
        pltpu.make_async_copy(source, target, sem).start()


def fetch_self(layer, flags, own_in, own_out, half, rest, to_in, to_out, sems):
    own = flags[0, 0] == layer

    def other(low, high):
        start(
            (high.at[rows_at(D), :], to_out, sems.at[1]),
            (low.at[rows_at(0), :], to_in.at[:, rows_at(0)], sems.at[0]),
            (low.at[rows_at(D), :], to_in.at[:, rows_at(D)], sems.at[0]),
            (high.at[rows_at(0), :], to_in.at[:, rows_at(2 * D)], sems.at[0]),
        )

    pl.when(own)(lambda: start((own_out, to_out, sems.at[1]), (own_in, to_in, sems.at[0])))
    pl.when(jnp.logical_not(own) & (flags[0, 1] == 0))(lambda: other(half, rest))
    pl.when(jnp.logical_not(own) & (flags[0, 1] != 0))(lambda: other(rest, half))
    return Landing(to_in, sems.at[0]), Landing(to_out, sems.at[1])


def fetch_rest(layer, flags, own_cross, own_expand, own_contract, rest, half, last, cross, expand, contract, sems):
    own = flags[0, 0] == layer

    def other(low, high):
        start(
            *((rest.at[rows_at((2 + j) * D), :], expand.at[:, rows_at(j * D)], sems.at[1]) for j in range(2)),
            *((low.at[rows_at(j * D), :], expand.at[:, rows_at((2 + j) * D)], sems.at[1]) for j in range(2)),
            (low.at[rows_at(2 * D), :], contract.at[rows_at(0), :], sems.at[2]),
            (high, contract.at[rows_at(D, 3 * D), :], sems.at[2]),
            *((rest.at[rows_at(j * D), :], cross.at[:, rows_at(j * D)], sems.at[0]) for j in range(2)),
        )

    pl.when(own)(
        lambda: start((own_expand, expand, sems.at[1]), (own_contract, contract, sems.at[2]), (own_cross, cross, sems.at[0]))
    )
    pl.when(jnp.logical_not(own) & (flags[0, 1] == 0))(lambda: other(half, last))
    pl.when(jnp.logical_not(own) & (flags[0, 1] != 0))(lambda: other(last, half))
    return Landing(cross, sems.at[0]), Landing(expand, sems.at[1]), Landing(contract, sems.at[2])


def fetch_rows(flags, rows, got, source, target, sems):
    @pl.when(flags[0, 0] == 0)
    def _():
        start((rows.at[rows_at(0, T), :], source, sems.at[0]), (got, target, sems.at[1]))

    @pl.when(flags[0, 0] != 0)
    def _():
        start((got, source, sems.at[0]), (rows.at[rows_at(T, T), :], target, sems.at[1]))

    return Landing(source, sems.at[0]), Landing(target, sems.at[1])


def first_kernel(
    table, flags, rows, got, own_in, own_out, half, rest, bias, glance, places, small, small_other,
    e_small, d_small, e_joined, e_mixed, e_stats, e_z, x, d_joined, d_mixed, d_stats, d_z,
    source, target, e_in, e_out, d_in, d_out, wide, copied, sems,
):
    source, target = fetch_rows(flags, rows, got, source, target, sems.at[pl.ds(0, 2)])
    e_in, e_out = fetch_self(0, flags, own_in, own_out, half, rest, e_in, e_out, sems.at[pl.ds(2, 2)])
    d_in, d_out = fetch_self(1, flags, own_in, own_out, half, rest, d_in, d_out, sems.at[pl.ds(4, 2)])

    @pl.when(flags[0, 0] == 0)
    def _():
        e_small[0:13, :], d_small[0:13, :] = small[...], small_other[...]

    @pl.when(flags[0, 0] != 0)
    def _():
        e_small[0:13, :], d_small[0:13, :] = small_other[...], small[...]

    encoder_self_kernel(table, bias, source, e_in, e_out, e_small, e_joined, e_mixed, e_stats, e_z, wide)
    leave(e_z)
    decoder_self_kernel(
        table, bias, source, target, glance, places, d_in, d_out, d_small, x, d_joined, d_mixed, d_stats, d_z, copied
    )


def first(table, flags, bias, glance, places, rows, got, weights, small, small_other):
    layer = (shaped(T, 3 * D, BF), shaped(T, D, BF), STATS, shaped(T, D, F32))
    outs = (shaped(16, D, F32), shaped(16, D, F32), *layer, shaped(T, D, BF), *layer)
    return kernel_call(
        first_kernel,
        outs,
        (table, flags, Raw(rows), Raw(got), *map(Raw, weights), bias, glance, places, small, small_other),
        scalars=2,
        scratch=[
            pltpu.VMEM((T, D), BF), pltpu.VMEM((T, D), BF),
            pltpu.VMEM((D, 3 * D), BF), pltpu.VMEM((D, D), BF), pltpu.VMEM((D, 3 * D), BF), pltpu.VMEM((D, D), BF),
            pltpu.VMEM((T, D), F32), pltpu.VMEM((T, D), BF), pltpu.SemaphoreType.DMA((6,)),
        ],
        flops=24 * FLOP_UNIT,
    )


def middle_kernel(
    table, flags, e_z1, own_cross, own_expand, own_contract, rest, half, last, bias, d_z1, cotangent, e_small, d_small,
    hidden, e_z2, memory, decoded, kept, sent, ff_bias, ff_rows, cross_grads, cross_bias, dstates, dz1,
    e_cross, e_expand, e_contract, d_cross, d_expand, d_contract,
    active, states, queries, mixed, stats, d_z2, wide, inner, value_b, dzb, dz2, sems,
):
    own = (own_cross, own_expand, own_contract, rest, half, last)
    e_cross, e_expand, e_contract = fetch_rest(0, flags, *own, e_cross, e_expand, e_contract, sems.at[pl.ds(0, 3)])
    d_cross, d_expand, d_contract = fetch_rest(1, flags, *own, d_cross, d_expand, d_contract, sems.at[pl.ds(3, 3)])
    encoder_ff_kernel(e_z1, e_expand, e_contract, e_cross, e_small, hidden, e_z2, memory, states, active)
    decoder_cross_kernel(table, bias, d_z1, states, d_cross, d_small, queries, mixed, stats, d_z2, wide)
    decoder_ff_kernel(
        flags, d_z2, d_expand, d_contract, d_small, cotangent, decoded, kept, sent, ff_bias, ff_rows, dz2,
        active, inner, value_b, wide, dzb,
    )
    decoder_cross_back_kernel(
        table, bias, dz2, d_z1, queries, states, mixed, stats, d_cross, d_small, cross_grads, cross_bias, dstates, dz1,
        value_b, dzb, active.at[:, rows_at(0)], active.at[:, rows_at(D)],
    )


def middle(table, flags, bias, e_z1, d_z1, weights, cotangent, e_small, d_small):
    low, high = shaped(T, D, BF), shaped(T, D, F32)
    outs = (
        shaped(T, FF, BF), high, low, low, shaped(FF, D, BF), shaped(FF, D, BF),
        shaped(8, D, F32), shaped(8, D, F32), shaped(2 * D, D, BF), shaped(8, D, F32), shaped(T, 2 * D, BF), high,
    )
    weight_room = [pltpu.VMEM((D, 2 * D), BF), pltpu.VMEM((D, FF), BF), pltpu.VMEM((FF, D), BF)]
    return kernel_call(
        middle_kernel,
        outs,
        (table, flags, e_z1, *map(Raw, weights), bias, d_z1, cotangent, e_small, d_small),
        scalars=2,
        scratch=weight_room * 2
        + [
            pltpu.VMEM((T, FF), BF), pltpu.VMEM((T, 2 * D), BF), pltpu.VMEM((T, D), BF), pltpu.VMEM((T, D), BF),
            pltpu.VMEM(STATS.shape, F32), pltpu.VMEM((T, D), F32), pltpu.VMEM((T, D), F32), pltpu.VMEM((T, FF), BF),
            pltpu.VMEM((T, D), BF), pltpu.VMEM((T, D), BF), pltpu.VMEM((T, D), F32), pltpu.SemaphoreType.DMA((6,)),
        ],
        flops=54 * FLOP_UNIT,
    )


def swapped(value, axis, partner):
    count = lax.axis_size(axis)
    return lax.ppermute(value, axis, [(i, partner(i)) for i in range(count)])


def swapped_pipe(value):
    return swapped(value, "pipe", lambda i: 1 - i)


def added(first, second):
    return (first.astype(F32) + second.astype(F32)).astype(BF)


def gate(value, after):
    anywhere = pl.BlockSpec(memory_space=pl.ANY)
    return pl.pallas_call(
        lambda *refs: None,
        out_shape=jax.ShapeDtypeStruct(value.shape, value.dtype),
        in_specs=[anywhere] * (1 + len(after)),
        out_specs=anywhere,
        input_output_aliases={0: 0},
    )(value, *after)


def halve_kernel(step, pairs, flags, *refs):
    ins, (kept_out, sent_out) = refs[: 2 * pairs], refs[2 * pairs :]
    bit = flags[0, 1 + step]
    slot = 0
    for i in range(pairs):
        kept, got = ins[2 * i], ins[2 * i + 1]
        half = kept.shape[1] // 2
        for j in range(kept.shape[0]):
            for out, side in ((kept_out, bit), (sent_out, 1 - bit)):
                at = pl.ds(pl.multiple_of(side * half, 16), half)
                out[slot] = added(kept[j, at, :], got[j, at, :])
            slot += 1


def double_kernel(step, flags, own, got, out):
    half = own.shape[0]
    bit = flags[0, 1 + step]
    out[pl.ds(pl.multiple_of(bit * half, 16), half), :] = own[...]
    out[pl.ds(pl.multiple_of((1 - bit) * half, 16), half), :] = got[...]


def across_kernel(pairs, flags, *refs):
    ins, (keep, send) = refs[: 2 * pairs], refs[2 * pairs :]
    sums = [added(ins[2 * i][j], ins[2 * i + 1][j]) for i in range(pairs) for j in range(ins[2 * i].shape[0])]

    @pl.when(flags[0, 0] == 0)
    def _():
        keep[...], send[...] = sums[0], sums[1]

    @pl.when(flags[0, 0] != 0)
    def _():
        keep[...], send[...] = sums[1], sums[0]


class Steps:
    def __init__(self):
        count = lax.axis_size("dp")
        bits = list(range(1, (count - 1).bit_length()))
        cut = max(1, len(bits) // 3)
        orders = (bits, bits[cut:] + bits[:cut])
        index = lax.axis_index("dp")
        core = index & 1
        self.partners = [lambda i: i ^ 1]
        self.bits = [core]
        for pair in zip(*orders):
            self.partners.append(lambda i, pair=pair: i ^ (1 << pair[i & 1]))
            self.bits.append((index >> jnp.where(core == 0, *pair)) & 1)
        self.core, self.count, self.last = core, count, len(bits)
        self.place = 0
        for bit in self.bits:
            self.place = self.place * 2 + bit
        self.flags = jnp.stack([lax.axis_index("pipe")] + self.bits).astype(jnp.int32).reshape(1, -1)

    def swap(self, value, step):
        return swapped(value, "dp", self.partners[step])

    def halve(self, step, *pairs, after=()):
        many = sum(kept.shape[0] for kept, _ in pairs)
        shape = jax.ShapeDtypeStruct((many, pairs[0][0].shape[1] // 2, D), BF)
        operands = [x for pair in pairs for x in pair]
        return kernel_call(
            functools.partial(halve_kernel, step + 1, len(pairs)), (shape, shape), (self.flags, *operands), scalars=1, after=after, direct=True
        )

    def double(self, step, own, got, after=()):
        out = (shaped(2 * own.shape[0], D, BF),)
        return kernel_call(functools.partial(double_kernel, step), out, (self.flags, own, got), scalars=1, after=after, direct=True)[0]

    def half_gathered(self, value, after):
        parts = []
        for step in range(self.last, 0, -1):
            value = self.double(step, value, self.swap(value, step), after=after if step == 1 else ())
            parts.append(value)
        return parts

    def across(self, *pairs, after=()):
        shape = shaped(*pairs[0][0].shape[1:], BF)
        operands = [x for pair in pairs for x in pair]
        return kernel_call(
            functools.partial(across_kernel, len(pairs)), (shape, shape), (self.flags, *operands), scalars=1, after=after, direct=True
        )


def by_core(flags, first, second, body):
    pl.when(flags[0, 1] == 0)(lambda: body(first, second))
    pl.when(flags[0, 1] != 0)(lambda: body(second, first))


def spill_ff_kernel(flags, own, other, expand, contract):
    def fill(low, high):
        for j in range(FF // D):
            expand[:, rows_at(j * D)] = low[rows_at(j * D), :].astype(F32)
            contract[rows_at(j * D), :] = high[rows_at(j * D), :].astype(F32)

    by_core(flags, own, other, fill)


def spill_rest_kernel(flags, own, other, joined, out, cross, expand_bias, branch, gain, shift):
    def fill(low, high):
        spots = (
            (low, 0, cross, 0), (low, 1, joined, 0), (low, 2, joined, 1),
            (high, 0, cross, 1), (high, 1, joined, 2), (high, 2, out, 0),
        )
        for ref, block, to, column in spots:
            to[:, rows_at(column * D)] = ref[rows_at(block * D), :].astype(F32)
        value = low[rows_at(3 * D, 16), :].astype(F32)
        for j in range(FF // D):
            expand_bias[0:1, rows_at(j * D)] = value[j : j + 1, :]
        branch[...] = value[4:7, :]
        gain[...] = value[7:10, :]
        shift[...] = value[10:13, :]

    by_core(flags, own, other, fill)


def last_kernel(flags, expand, contract, out):
    @pl.when(flags[0, 1] == 0)
    def _():
        for j in range(2):
            out[rows_at(j * D), :] = expand[:, rows_at((2 + j) * D)]
        out[rows_at(2 * D), :] = contract[rows_at(0), :]

    @pl.when(flags[0, 1] != 0)
    def _():
        out[...] = contract[rows_at(D, 3 * D), :]


def per_device(
    embeddings, cotangent, lengths, copy_index, priority, hamming,
    self_in, self_out, cross_weight, expand, contract,
    expand_bias, branch_bias, norm_gain, norm_shift,
):
    pipe = lax.axis_index("pipe")
    leading = pipe == 0
    steps = Steps()
    flags, count = steps.flags, steps.count
    self_in, self_out, cross_weight, expand, contract = (w[0] for w in (self_in, self_out, cross_weight, expand, contract))

    rows = embeddings[0]
    small = jnp.concatenate([expand_bias.reshape(4, D), branch_bias[0], norm_gain[0], norm_shift[0]], 0)
    small_other = swapped_pipe(small)
    got = swapped_pipe(gate(lax.dynamic_slice_in_dim(rows, (1 - pipe) * T, T, 0), (small_other,)))
    size = 4 * D // count

    def piece(place, blocks_of):
        block, inside = place * size // D, place * size % D
        value = lax.dynamic_slice(blocks_of[0][0], (inside, blocks_of[0][1] * D), (size, D))
        for i in range(1, 4):
            matrix, column = blocks_of[i]
            value = jnp.where(block == i, lax.dynamic_slice(matrix, (inside, column * D), (size, D)), value)
        return value

    self_piece = piece(steps.place, [(self_in, 0), (self_in, 1), (self_in, 2), (self_out, 0)])
    rest_piece = piece(lax.axis_index("dp"), [(cross_weight, 0), (cross_weight, 1), (expand, 0), (expand, 1)])
    self_parts = steps.half_gathered(swapped_pipe(self_piece), (got,))
    self_half = self_parts[-1]
    (last_piece,) = kernel_call(last_kernel, (shaped(3 * D, D, BF),), (flags, expand, contract), scalars=1, after=(self_parts[-2],), direct=True)
    self_rest = steps.swap(self_half, 0)
    last_half = swapped_pipe(last_piece)
    rest = lax.all_gather(swapped_pipe(rest_piece), "dp").reshape(4 * D, D)

    table, bias, glance, places = row_layout(
        flags, lengths, hamming, priority.reshape(2 * T // WIN, WIN), copy_index.reshape(2 * T // WIN, WIN)
    )
    self_weights = (self_in, self_out, self_half, self_rest)
    (
        e_small, d_small, e_joined, e_mixed, e_stats, e_z1, x, d_joined, d_mixed, d_stats, d_z1,
    ) = first(table, flags, bias, glance, places, rows, got, self_weights, small, small_other)
    last_half = gate(last_half, (d_z1,))
    last_rest = steps.swap(last_half, 0)
    rest_weights = (cross_weight, expand, contract, rest, last_half, last_rest)
    (
        hidden, e_z2, memory, decoded, *dec_ff, d_ff_bias, d_ff_rows, d_cross, d_cross_bias, dstates, dz1,
    ) = middle(table, flags, bias, e_z1, d_z1, rest_weights, cotangent, e_small, d_small)

    def rows_swap(first, second):
        return swapped_pipe(jnp.where(leading, second, first).astype(BF))

    def rows_out(first, second, other):
        own, other = jnp.where(leading, first, second).astype(F32), other.astype(F32)
        return jnp.where(leading, jnp.concatenate([own, other], 0), jnp.concatenate([other, own], 0))[None]

    def opened(pair):
        return [part[None] for part in pair]

    layer_other = rows_swap(memory, decoded)
    dec_kept, dec_sent = opened(dec_ff)
    dec_got = steps.swap(dec_sent, 0)
    dec_kept, dec_sent = steps.halve(0, (dec_kept, dec_got))
    dec_got = steps.swap(dec_sent, 1)
    *dec_self, target_grad, copies_grad = decoder_self_back(
        table, flags, bias, dz1, x, d_joined, d_mixed, d_stats, glance, places, self_weights,
        d_cross, d_ff_bias, d_ff_rows, d_cross_bias, count, after=(dec_kept,),
    )
    dself_kept, dself_sent = opened(dec_self)
    dself_got = steps.swap(dself_sent, 0)
    dec_kept, dec_sent = steps.halve(1, (dec_kept, dec_got))
    dec_got = steps.swap(dec_sent, 2)
    e_cross, *enc_ff, e_ff_bias, e_ff_rows, e_dz1 = encoder_ff_back(
        flags, dstates, e_z1, e_z2, hidden, rest_weights, e_small, after=(dec_kept, target_grad)
    )
    enc_kept, enc_sent = opened(enc_ff)
    enc_got = steps.swap(enc_sent, 0)
    dself_kept, dself_sent = steps.halve(0, (dself_kept, dself_got))
    dself_got = steps.swap(dself_sent, 1)
    dec_kept, dec_sent = steps.halve(2, (dec_kept, dec_got))
    dec_got = steps.swap(dec_sent, 3)
    *enc_self, source_grad = encoder_self_back(
        table, flags, bias, e_dz1, rows, got, e_joined, e_mixed, e_stats, copies_grad, self_weights, e_small,
        e_cross, e_ff_bias, e_ff_rows, count, after=(dec_kept, dself_kept),
    )
    grad_other = rows_swap(source_grad, target_grad)
    self_kept, self_sent = opened(enc_self)
    self_got = steps.swap(self_sent, 0)
    enc_kept, enc_sent = steps.halve(0, (enc_kept, enc_got), after=(source_grad,))
    enc_got = steps.swap(enc_sent, 1)
    self_kept, self_sent = steps.halve(0, (self_kept, self_got))
    self_got = steps.swap(self_sent, 1)
    for step in range(3, steps.last):
        dec_kept, dec_sent = steps.halve(step, (dec_kept, dec_got))
        dec_got = steps.swap(dec_sent, step + 1)
    mark = (self_kept,)
    ff_step, self_step = 1, 1
    self_pairs = [(self_kept, self_got), (dself_kept, dself_got)]
    enc_pair = (enc_kept, enc_got)
    while ff_step < steps.last:
        kept, sent = steps.halve(ff_step, enc_pair, after=mark)
        ff_step += 1
        enc_pair = (kept, steps.swap(sent, ff_step))
        if self_step < steps.last:
            kept, sent = steps.halve(self_step, *self_pairs)
            self_step += 1
            self_pairs = [(kept, steps.swap(sent, self_step))]
            mark = (kept,)
    keep, send = steps.across(enc_pair, (dec_kept, dec_got), after=mark + (grad_other,))
    ff_got = swapped_pipe(send)
    keep_self, send_self = steps.across(*self_pairs)
    self_got = swapped_pipe(send_self)
    ff = added(keep, ff_got)
    ff_got = steps.swap(ff, steps.last)
    rest_sum = added(keep_self, self_got)
    self_got = steps.swap(rest_sum, steps.last)
    for step in range(steps.last, 0, -1):
        ff = steps.double(step, ff, ff_got, after=(rest_sum,))
        ff_got = steps.swap(ff, step - 1)
        rest_sum = steps.double(step, rest_sum, self_got)
        self_got = steps.swap(rest_sum, step - 1)

    layer_out = rows_out(memory, decoded, layer_other)
    embedding_grad = rows_out(source_grad, target_grad, grad_other)
    outs = (shaped(D, FF, F32), shaped(FF, D, F32))
    expand_grad, contract_grad = kernel_call(spill_ff_kernel, outs, (flags, ff, ff_got), scalars=1, direct=True)
    outs = (shaped(D, 3 * D, F32), shaped(D, D, F32), shaped(D, 2 * D, F32), shaped(1, FF, F32)) + (shaped(3, D, F32),) * 3
    in_grad, out_grad, cross_grad, *small_grads = kernel_call(spill_rest_kernel, outs, (flags, rest_sum, self_got), scalars=1, direct=True)
    return (
        layer_out,
        embedding_grad,
        in_grad[None],
        out_grad[None],
        cross_grad[None],
        expand_grad[None],
        contract_grad[None],
        small_grads[0],
        *(part[None] for part in small_grads[1:]),
    )


def solution(mesh):
    return jax.shard_map(
        per_device,
        mesh=mesh,
        in_specs=(
            P("pipe", "dp", None),
            P("dp", None),
            P("dp", None),
            P("dp"),
            P("dp"),
            P("dp", None),
            P("pipe", None, None),
            P("pipe", None, None),
            P("pipe", None, None),
            P("pipe", None, None),
            P("pipe", None, None),
            P("pipe", None),
            P("pipe", None, None),
            P("pipe", None, None),
            P("pipe", None, None),
        ),
        out_specs=(
            P("pipe", "dp", None),
            P("pipe", "dp", None),
            P("pipe", None, None),
            P("pipe", None, None),
            P("pipe", None, None),
            P("pipe", None, None),
            P("pipe", None, None),
            P("pipe", None),
            P("pipe", None, None),
            P("pipe", None, None),
            P("pipe", None, None),
        ),
        check_vma=False,
    )
```

time: 667 us -> 429 us (0.64)
  blocking collectives: 76.3 us -> 0 us
  waiting for transfers between devices: 202 us -> 148 us
  other arithmetic: 62.1 us -> 11.7 us
  Pallas kernels: 220 us -> 180 us
  local copies, waits for them, and re-layouts: 47.5 us -> 20 us
  between operations: 1.52 us -> 14.8 us
    psum x1 -> x0, blocking collectives: 76.3 us -> none  [per_device(): rows = lax.psum(rows, 'dp')]
    ppermute x41 -> x36, waiting for transfers between devices: 202 us -> 148 us  [swapped(): return lax.ppermute(value, axis, [(i, partner(i)) for i in range(count)])]
    pallas_call x10 -> x32, Pallas kernels: 220 us -> 180 us  [the longest x30 180 us: kernel_call(): pl.pallas_call(run, out_shape=tuple(outs), in_specs=in_specs, out_specs=t...]
    select_n x20 -> x4, other arithmetic: 35.6 us -> 7.94 us  [the longest x2 5.73 us: rows_out(): jnp.where(leading, jnp.concatenate([own, other], 0), jnp.concatenate([oth...]
    convert_element_type x19 -> x2, other arithmetic: 16.6 us -> 0.12 us  [added(): return (first.astype(F32) + second.astype(F32)).astype(BF)]
    dynamic_slice x24 -> x1, local copies, waits for them, and re-layouts: 17.9 us -> 2.27 us  [per_device(): lax.dynamic_slice_in_dim(rows, (1 - pipe) * T, T, 0)]
    unnamed x81 -> x78, local copies, waits for them, and re-layouts: 6.61 us -> 17.6 us
    slice x11 -> x0, local copies, waits for them, and re-layouts: 10.3 us -> none  [the longest x1 1.59 us: row_pass(): e_self_bias[2:3]]
  transfers between devices with their start and end apart: 41 -> 37, of which waited for: 13 -> 21; matrix products, arithmetic and copies ran while one was open for 14% -> 4% of each run, Pallas kernels for 16% -> 29%
where the time goes in v2:
time: 429 us; the launch traced here: 420 us
  Pallas kernels  180 us (42%)
  waiting for transfers between devices  148 us (34%)
  starting transfers between devices  44.9 us (10%)
  local copies, waits for them, and re-layouts  20 us (5%)
  between operations  14.8 us (3%)
  other arithmetic  11.7 us (3%)
    pallas_call x30, Pallas kernels, kernel_call(): pl.pallas_call(run, out_shape=tuple(outs), in_specs=in_specs, out_specs=t...  180 us
    ppermute x36, waiting for transfers between devices, swapped(): return lax.ppermute(value, axis, [(i, partner(i)) for i in range(count)])  148 us
    ppermute x36, starting transfers between devices, swapped(): return lax.ppermute(value, axis, [(i, partner(i)) for i in range(count)])  44.9 us
    unnamed x78, local copies, waits for them, and re-layouts  17.6 us
  transfers between devices with their start and end apart: 37, of which 21 were waited for; matrix products, arithmetic and copies ran while one was open for 4% of the time, Pallas kernels for 29%

profile of v2, /device:TPU:1, one launch (start us, length us, event | category | flops | bytes accessed | tf_op | source)
XLA Modules:
  0.0 420.1 jit_solution(1162619025062886567)
XLA Ops:
  25.1 7.0 %collective-permute-done.4.refs_2_ = bf16[256,512]{1,0:T(8,128)(2,1)S(1)} collective-permute-done((bf16[256,512]{1,0:T(8,128)(2,1)S(1)}, bf16[256,512]{1,0:T(8,128)(2,1)S(1)}, u32[]{:S(2)}, u32[]{:S(2)}) %collective-permute-start.4) | collective-permute-done | bytes 262176 | tf_op jit(solution)/shard_map/ppermute | solution.py:961
  35.8 7.2 %collective-permute-done.7 = bf16[128,512]{1,0:T(8,128)(2,1)S(1)} collective-permute-done((bf16[128,512]{1,0:T(8,128)(2,1)S(1)}, bf16[128,512]{1,0:T(8,128)(2,1)S(1)}, u32[]{:S(2)}, u32[]{:S(2)}) %collective-permute-start.7) | collective-permute-done | bytes 131104 | tf_op jit(solution)/shard_map/ppermute | solution.py:961
  44.3 3.4 collective-permute-start.6
  59.3 21.7 %shard_map.235 = (f32[16,512]{1,0:T(8,128)}, f32[16,512]{1,0:T(8,128)}, bf16[1024,1536]{1,0:T(8,128)(2,1)}, bf16[1024,512]{1,0:T(8,128)(2,1)}, f32[72,2,256]{2,1...) custom-call(s32[1,128]{1,0:T(1,128)} %copy-done.28, ...), custom_call_target="tpu_custom_call" | custom-call | flops 12884901888 | bytes 23613972 | tf_op jit(solution)/shard_map/pallas_call | solution.py:188
  81.0 6.1 %collective-permute-done.8.refs_0_ = bf16[1536,512]{1,0:T(8,128)(2,1)} collective-permute-done((bf16[1536,512]{1,0:T(8,128)(2,1)}, bf16[1536,512]{1,0:T(8,128)(2,1)}, u32[]{:S(2)}, u32[]{:S(2)}) %collective-permute-start.8) | collective-permute-done | bytes 1572896 | tf_op jit(solution)/shard_map/ppermute | solution.py:961
  87.8 3.2 collective-permute-done.9.refs_8_.refs_10_
  92.2 51.3 %shard_map.238 = (bf16[1024,2048]{1,0:T(8,128)(2,1)}, f32[1024,512]{1,0:T(8,128)}, bf16[1024,512]{1,0:T(8,128)(2,1)}, bf16[1024,512]{1,0:T(8,128)(2,1)}, bf16[20...) custom-call(s32[1,128]{1,0:T(1,128)} %copy-done.28, ...), custom_call_target="tpu_custom_call" | custom-call | flops 28991029248 | bytes 35897876 | tf_op jit(solution)/shard_map/pallas_call | solution.py:188
  144.9 4.0 collective-permute-done.11.refs_2_
  155.5 21.8 %shard_map.241 = (bf16[1664,512]{1,0:T(8,128)(2,1)}, bf16[1664,512]{1,0:T(8,128)(2,1)}, bf16[1024,512]{1,0:T(8,128)(2,1)}, bf16[1024,512]{1,0:T(8,128)(2,1)}) custom-call(s32[1,128]{1,0:T(1,128)} %copy-done.28, s32[1,5]{1,0:T(1,128)} %bitcast.72, f32[1024,512]{1,0:T(8,128)} %get-tuple-element.102.refs_2_, bf16[512,1536]{1,0:T(8,128)(2,1)} %bitcast.103, ...), custom_call_target="tpu_custom_call" | custom-call | flops 9663676416 | bytes 20513300 | tf_op jit(solution)/shard_map/pallas_call | solution.py:188
  180.4 3.4 collective-permute-start.13
  183.9 27.8 %shard_map.242 = (bf16[1024,512]{1,0:T(8,128)(2,1)}, bf16[2048,512]{1,0:T(8,128)(2,1)}, bf16[2048,512]{1,0:T(8,128)(2,1)}, f32[8,512]{1,0:T(8,128)}, f32[8,512]{1,0:T(8,128)}, /*index=5*/f32[1024,512]{1,0:T(8,128)}) custom-call(s32[1,5]{1,0:T(1,128)} %bitcast.73, f32[1024,512]{1,0:T(8,128)} %get-tuple-element.94.refs_1_, ...), custom_call_target="tpu_custom_call" | custom-call | flops 11811160064 | bytes 28377108 | tf_op jit(solution)/shard_map/pallas_call | solution.py:188
  218.3 20.5 %shard_map.245 = (bf16[1664,512]{1,0:T(8,128)(2,1)}, bf16[1664,512]{1,0:T(8,128)(2,1)}, bf16[1024,512]{1,0:T(8,128)(2,1)}) custom-call(s32[1,128]{1,0:T(1,128)} %copy-done.28, s32[1,5]{1,0:T(1,128)} %bitcast.74, f32[1024,512]{1,0:T(8,128)} %get-tuple-element.112.refs_2_, bf16[2048,512]{1,0:T(8,128)(2,1)} %bitcast.101, ...), custom_call_target="tpu_custom_call" | custom-call | flops 9663676416 | bytes 21578260 | tf_op jit(solution)/shard_map/pallas_call | solution.py:188
  246.8 3.0 shard_map.254
  254.5 6.2 %collective-permute-done.17.refs_2_ = bf16[1,832,512]{2,1,0:T(8,128)(2,1)} collective-permute-done((bf16[1,832,512]{2,1,0:T(8,128)(2,1)}, bf16[1,832,512]{2,1,0:T(8,128)(2,1)}, u32[]{:S(2)}, u32[]{:S(2)}) %collective-permute-start.17) | collective-permute-done | bytes 852000 | tf_op jit(solution)/shard_map/ppermute | solution.py:961
  263.2 26.0 %collective-permute-done.27.refs_2_ = bf16[1,1024,512]{2,1,0:T(8,128)(2,1)} collective-permute-done((bf16[1,1024,512]{2,1,0:T(8,128)(2,1)}, bf16[1,1024,512]{2,1,0:T(8,128)(2,1)}, u32[]{:S(2)}, u32[]{:S(2)}) %collective-permute-start.27) | collective-permute-done | bytes 1048608 | tf_op jit(solution)/shard_map/ppermute | solution.py:961
  291.7 28.7 %collective-permute-done.28.refs_2_ = bf16[1,512,512]{2,1,0:T(8,128)(2,1)S(1)} collective-permute-done((bf16[1,512,512]{2,1,0:T(8,128)(2,1)S(1)}, bf16[1,512,512]{2,1,0:T(8,128)(2,1)S(1)}, u32[]{:S(2)}, u32[]{:S(2)}) %collective-permute-start.28) | collective-permute-done | bytes 524320 | tf_op jit(solution)/shard_map/ppermute | solution.py:961
  341.9 3.6 collective-permute-done.22.refs_2_
  346.1 11.6 %collective-permute-done.33.refs_2_ = bf16[512,512]{1,0:T(8,128)(2,1)S(1)} collective-permute-done((bf16[512,512]{1,0:T(8,128)(2,1)S(1)}, bf16[512,512]{1,0:T(8,128)(2,1)S(1)}, u32[]{:S(2)}, u32[]{:S(2)}) %collective-permute-start.33) | collective-permute-done | bytes 524320 | tf_op jit(solution)/shard_map/ppermute | solution.py:961
  359.7 18.2 %collective-permute-done.23.refs_2_ = bf16[416,512]{1,0:T(8,128)(2,1)S(1)} collective-permute-done((bf16[416,512]{1,0:T(8,128)(2,1)S(1)}, bf16[416,512]{1,0:T(8,128)(2,1)S(1)}, u32[]{:S(2)}, u32[]{:S(2)}) %collective-permute-start.23) | collective-permute-done | bytes 426016 | tf_op jit(solution)/shard_map/ppermute | solution.py:961
  378.5 3.2 collective-permute-start.24
  383.5 8.3 %collective-permute-done.24.refs_2_ = bf16[832,512]{1,0:T(8,128)(2,1)S(1)} collective-permute-done((bf16[832,512]{1,0:T(8,128)(2,1)S(1)}, bf16[832,512]{1,0:T(8,128)(2,1)S(1)}, u32[]{:S(2)}, u32[]{:S(2)}) %collective-permute-start.24) | collective-permute-done | bytes 852000 | tf_op jit(solution)/shard_map/ppermute | solution.py:961
  392.5 4.2 %collective-permute-done.10 = bf16[1024,512]{1,0:T(8,128)(2,1)S(1)} collective-permute-done((bf16[1024,512]{1,0:T(8,128)(2,1)S(1)}, bf16[1024,512]{1,0:T(8,128)(2,1)S(1)}, u32[]{:S(2)}, u32[]{:S(2)}) %collective-permute-start.10) | collective-permute-done | bytes 1048608 | tf_op jit(solution)/shard_map/ppermute | solution.py:961
  403.1 3.7 shard_map.253
  408.5 4.5 %shard_map.261 = (f32[512,2048]{1,0:T(8,128)}, f32[2048,512]{1,0:T(8,128)}) custom-call(s32[1,5]{1,0:T(1,128)S(1)} %bitcast.94, bf16[2048,512]{1,0:T(8,128)(2,1)S(1)} %shard_map.260.refs_1_, bf16[2048,512]{1,0:T(8,128)(2,1)S(1)} %collective-permute-done.35.refs_2_), custom_call_target="tpu_custom_call" | custom-call | bytes 12582932 | tf_op jit(solution)/shard_map/pallas_call | solution.py:188
  (176 shorter events, 106.9 us)
Async XLA Ops:
  7.2 84.1 %all-gather.3.cloned.1.call-start = ((), (), s32[]{:S(2)}) async-start(), calls=%async_computation | async-start | bytes 2228224 | tf_op jit(solution)/shard_map/all_gather | solution.py:1142
  8.4 9.8 %collective-permute-start.2 = (bf16[128,512]{1,0:T(8,128)(2,1)S(1)}, bf16[128,512]{1,0:T(8,128)(2,1)S(1)}, u32[]{:S(2)}, u32[]{:S(2)}) collective-permute-start(bf16[128,512]{1,0:T(8,128)(2,1)S(1)} %select_bitcast_fusion.1), channel_id=1, source_target_pairs={{0,16},{16,0},{1,17},{17,1},{2,18},{18,2},{3,19},{19,3},{4,20},{20... | collective-permute-start | bytes 393224 | tf_op jit(solution)/shard_map/ppermute | solution.py:961
  17.3 26.4 %collective-permute-start.1 = (bf16[1024,512]{1,0:T(8,128)(2,1)}, bf16[1024,512]{1,0:T(8,128)(2,1)}, u32[]{:S(2)}, u32[]{:S(2)}) collective-permute-start(bf16[1024,512]{1,0:T(8,128)(2,1)} %shard_map.231), channel_id=1, source_target_pairs={{0,16},{16,0},{1,17},{17,1},{2,18},{18,2},{3,19},{19,3},{4,20},{20... | collective-permute-start | bytes 3145736 | tf_op jit(solution)/shard_map/ppermute | solution.py:961
  32.6 11.1 %collective-permute-start.5 = (bf16[512,512]{1,0:T(8,128)(2,1)S(1)}, bf16[512,512]{1,0:T(8,128)(2,1)S(1)}, u32[]{:S(2)}, u32[]{:S(2)}) collective-permute-start(bf16[512,512]{1,0:T(8,128)(2,1)S(1)} %shard_map.233.refs_1_.refs_3_), channel_id=1, source_target_pairs={{0,2},{1,5},{2,0},{3,7},{4,6},{5,1},{6,4},{7,3},{8,10},{9,13},{10,... | collective-permute-start | bytes 1572872 | tf_op jit(solution)/shard_map/ppermute | solution.py:961
  44.3 14.0 %collective-permute-start.6 = (bf16[1024,512]{1,0:T(8,128)(2,1)S(1)}, bf16[1024,512]{1,0:T(8,128)(2,1)S(1)}, u32[]{:S(2)}, u32[]{:S(2)}) collective-permute-start(bf16[1024,512]{1,0:T(8,128)(2,1)S(1)} %shard_map.234.refs_6_.refs_5_.refs_7_), channel_id=1, source_target_pairs={{0,1},{1,0},{2,3},{3,2},{4,5},{5,4},{6,7},{7,6},{8,9},{9,8},{10,11... | collective-permute-start | bytes 3145736 | tf_op jit(solution)/shard_map/ppermute | solution.py:961
  49.5 37.6 %collective-permute-start.8 = (bf16[1536,512]{1,0:T(8,128)(2,1)}, bf16[1536,512]{1,0:T(8,128)(2,1)}, u32[]{:S(2)}, u32[]{:S(2)}) collective-permute-start(bf16[1536,512]{1,0:T(8,128)(2,1)} %shard_map.236), channel_id=1, source_target_pairs={{0,16},{16,0},{1,17},{17,1},{2,18},{18,2},{3,19},{19,3},{4,20},{20... | collective-permute-start | bytes 4718600 | tf_op jit(solution)/shard_map/ppermute | solution.py:961
  153.4 24.0 %collective-permute-start.12 = (bf16[1,1024,512]{2,1,0:T(8,128)(2,1)}, bf16[1,1024,512]{2,1,0:T(8,128)(2,1)}, u32[]{:S(2)}, u32[]{:S(2)}) collective-permute-start(bf16[1,1024,512]{2,1,0:T(8,128)(2,1)} %get-tuple-element.100), channel_id=1, source_target_pairs={{0,2},{1,5},{2,0},{3,7},{4,6},{5,1},{6,4},{7,3},{8,10},{9,13},{10,... | collective-permute-start | bytes 3145736 | tf_op jit(solution)/shard_map/ppermute | solution.py:961
  177.3 37.4 %collective-permute-start.14 = (bf16[1,1664,512]{2,1,0:T(8,128)(2,1)}, bf16[1,1664,512]{2,1,0:T(8,128)(2,1)}, u32[]{:S(2)}, u32[]{:S(2)}) collective-permute-start(bf16[1,1664,512]{2,1,0:T(8,128)(2,1)} %bitcast.117), channel_id=1, source_target_pairs={{0,1},{1,0},{2,3},{3,2},{4,5},{5,4},{6,7},{7,6},{8,9},{9,8},{10,11... | collective-permute-start | bytes 5111816 | tf_op jit(solution)/shard_map/ppermute | solution.py:961
  180.4 31.3 %collective-permute-start.13 = (bf16[1,512,512]{2,1,0:T(8,128)(2,1)}, bf16[1,512,512]{2,1,0:T(8,128)(2,1)}, u32[]{:S(2)}, u32[]{:S(2)}) collective-permute-start(bf16[1,512,512]{2,1,0:T(8,128)(2,1)} %get-tuple-element.120), channel_id=1, source_target_pairs={{0,4},{1,9},{2,6},{3,11},{4,0},{5,13},{6,2},{7,15},{8,12},{9,1},{1... | collective-permute-start | bytes 1572872 | tf_op jit(solution)/shard_map/ppermute | solution.py:961
  211.7 35.1 %collective-permute-start.26 = (bf16[1,2048,512]{2,1,0:T(8,128)(2,1)}, bf16[1,2048,512]{2,1,0:T(8,128)(2,1)}, u32[]{:S(2)}, u32[]{:S(2)}) collective-permute-start(bf16[1,2048,512]{2,1,0:T(8,128)(2,1)} %bitcast.114), channel_id=1, source_target_pairs={{0,1},{1,0},{2,3},{3,2},{4,5},{5,4},{6,7},{7,6},{8,9},{9,8},{10,11... | collective-permute-start | bytes 6291464 | tf_op jit(solution)/shard_map/ppermute | solution.py:961
  239.4 15.1 %collective-permute-start.18 = (bf16[1,832,512]{2,1,0:T(8,128)(2,1)}, bf16[1,832,512]{2,1,0:T(8,128)(2,1)}, u32[]{:S(2)}, u32[]{:S(2)}) collective-permute-start(bf16[1,832,512]{2,1,0:T(8,128)(2,1)} %get-tuple-element.130), channel_id=1, source_target_pairs={{0,2},{1,5},{2,0},{3,7},{4,6},{5,1},{6,4},{7,3},{8,10},{9,13},{10,... | collective-permute-start | bytes 2555912 | tf_op jit(solution)/shard_map/ppermute | solution.py:961
  246.1 14.6 %collective-permute-start.17 = (bf16[1,832,512]{2,1,0:T(8,128)(2,1)}, bf16[1,832,512]{2,1,0:T(8,128)(2,1)}, u32[]{:S(2)}, u32[]{:S(2)}) collective-permute-start(bf16[1,832,512]{2,1,0:T(8,128)(2,1)} %get-tuple-element.129), channel_id=1, source_target_pairs={{0,2},{1,5},{2,0},{3,7},{4,6},{5,1},{6,4},{7,3},{8,10},{9,13},{10,... | collective-permute-start | bytes 2555912 | tf_op jit(solution)/shard_map/ppermute | solution.py:961
  249.8 39.4 %collective-permute-start.27 = (bf16[1,1024,512]{2,1,0:T(8,128)(2,1)}, bf16[1,1024,512]{2,1,0:T(8,128)(2,1)}, u32[]{:S(2)}, u32[]{:S(2)}) collective-permute-start(bf16[1,1024,512]{2,1,0:T(8,128)(2,1)} %get-tuple-element.143), channel_id=1, source_target_pairs={{0,2},{1,5},{2,0},{3,7},{4,6},{5,1},{6,4},{7,3},{8,10},{9,13},{10,... | collective-permute-start | bytes 3145736 | tf_op jit(solution)/shard_map/ppermute | solution.py:961
  252.1 71.3 %collective-permute-start.15 = (bf16[1024,512]{1,0:T(8,128)(2,1)S(1)}, bf16[1024,512]{1,0:T(8,128)(2,1)S(1)}, u32[]{:S(2)}, u32[]{:S(2)}) collective-permute-start(bf16[1024,512]{1,0:T(8,128)(2,1)S(1)} %get-tuple-element.169), channel_id=1, source_target_pairs={{0,16},{16,0},{1,17},{17,1},{2,18},{18,2},{3,19},{19,3},{4,20},{20... | collective-permute-start | bytes 3145736 | tf_op jit(solution)/shard_map/ppermute | solution.py:961
  262.6 59.3 %collective-permute-start.19 = (bf16[2,416,512]{2,1,0:T(8,128)(2,1)S(1)}, bf16[2,416,512]{2,1,0:T(8,128)(2,1)S(1)}, u32[]{:S(2)}, u32[]{:S(2)}) collective-permute-start(bf16[2,416,512]{2,1,0:T(8,128)(2,1)S(1)} %get-tuple-element.132), channel_id=1, source_target_pairs={{0,4},{1,9},{2,6},{3,11},{4,0},{5,13},{6,2},{7,15},{8,12},{9,1},{1... | collective-permute-start | bytes 2555912 | tf_op jit(solution)/shard_map/ppermute | solution.py:961
  290.7 29.6 %collective-permute-start.28 = (bf16[1,512,512]{2,1,0:T(8,128)(2,1)S(1)}, bf16[1,512,512]{2,1,0:T(8,128)(2,1)S(1)}, u32[]{:S(2)}, u32[]{:S(2)}) collective-permute-start(bf16[1,512,512]{2,1,0:T(8,128)(2,1)S(1)} %get-tuple-element.145), channel_id=1, source_target_pairs={{0,4},{1,9},{2,6},{3,11},{4,0},{5,13},{6,2},{7,15},{8,12},{9,1},{1... | collective-permute-start | bytes 1572872 | tf_op jit(solution)/shard_map/ppermute | solution.py:961
  290.8 32.6 %collective-permute-start.30 = (bf16[1,256,512]{2,1,0:T(8,128)(2,1)S(1)}, bf16[1,256,512]{2,1,0:T(8,128)(2,1)S(1)}, u32[]{:S(2)}, u32[]{:S(2)}) collective-permute-start(bf16[1,256,512]{2,1,0:T(8,128)(2,1)S(1)} %get-tuple-element.148), channel_id=1, source_target_pairs={{0,8},{1,3},{2,10},{3,1},{4,12},{5,7},{6,14},{7,5},{8,0},{9,11},{1... | collective-permute-start | bytes 786440 | tf_op jit(solution)/shard_map/ppermute | solution.py:961
  340.3 17.3 %collective-permute-start.33 = (bf16[512,512]{1,0:T(8,128)(2,1)S(1)}, bf16[512,512]{1,0:T(8,128)(2,1)S(1)}, u32[]{:S(2)}, u32[]{:S(2)}) collective-permute-start(bf16[512,512]{1,0:T(8,128)(2,1)S(1)} %shard_map.258.refs_1_), channel_id=1, source_target_pairs={{0,4},{1,9},{2,6},{3,11},{4,0},{5,13},{6,2},{7,15},{8,12},{9,1},{1... | collective-permute-start | bytes 1572872 | tf_op jit(solution)/shard_map/ppermute | solution.py:961
  358.3 24.5 %collective-permute-start.34 = (bf16[1024,512]{1,0:T(8,128)(2,1)S(1)}, bf16[1024,512]{1,0:T(8,128)(2,1)S(1)}, u32[]{:S(2)}, u32[]{:S(2)}) collective-permute-start(bf16[1024,512]{1,0:T(8,128)(2,1)S(1)} %shard_map.259.refs_1_), channel_id=1, source_target_pairs={{0,2},{1,5},{2,0},{3,7},{4,6},{5,1},{6,4},{7,3},{8,10},{9,13},{10,... | collective-permute-start | bytes 3145736 | tf_op jit(solution)/shard_map/ppermute | solution.py:961
  358.3 19.6 %collective-permute-start.23 = (bf16[416,512]{1,0:T(8,128)(2,1)S(1)}, bf16[416,512]{1,0:T(8,128)(2,1)S(1)}, u32[]{:S(2)}, u32[]{:S(2)}) collective-permute-start(bf16[416,512]{1,0:T(8,128)(2,1)S(1)} %shard_map.250.refs_1_.refs_3_), channel_id=1, source_target_pairs={{0,4},{1,9},{2,6},{3,11},{4,0},{5,13},{6,2},{7,15},{8,12},{9,1},{1... | collective-permute-start | bytes 1277960 | tf_op jit(solution)/shard_map/ppermute | solution.py:961
  378.5 13.3 %collective-permute-start.24 = (bf16[832,512]{1,0:T(8,128)(2,1)S(1)}, bf16[832,512]{1,0:T(8,128)(2,1)S(1)}, u32[]{:S(2)}, u32[]{:S(2)}) collective-permute-start(bf16[832,512]{1,0:T(8,128)(2,1)S(1)} %shard_map.251.refs_1_.refs_3_), channel_id=1, source_target_pairs={{0,2},{1,5},{2,0},{3,7},{4,6},{5,1},{6,4},{7,3},{8,10},{9,13},{10,... | collective-permute-start | bytes 2555912 | tf_op jit(solution)/shard_map/ppermute | solution.py:961
  381.9 14.8 %collective-permute-start.10 = (bf16[1024,512]{1,0:T(8,128)(2,1)S(1)}, bf16[1024,512]{1,0:T(8,128)(2,1)S(1)}, u32[]{:S(2)}, u32[]{:S(2)}) collective-permute-start(bf16[1024,512]{1,0:T(8,128)(2,1)S(1)} %get-tuple-element.171), channel_id=1, source_target_pairs={{0,16},{16,0},{1,17},{17,1},{2,18},{18,2},{3,19},{19,3},{4,20},{20... | collective-permute-start | bytes 3145736 | tf_op jit(solution)/shard_map/ppermute | solution.py:961
  383.4 25.1 %collective-permute-start.35 = (bf16[2048,512]{1,0:T(8,128)(2,1)S(1)}, bf16[2048,512]{1,0:T(8,128)(2,1)S(1)}, u32[]{:S(2)}, u32[]{:S(2)}) collective-permute-start(bf16[2048,512]{1,0:T(8,128)(2,1)S(1)} %shard_map.260.refs_1_), channel_id=1, source_target_pairs={{0,1},{1,0},{2,3},{3,2},{4,5},{5,4},{6,7},{7,6},{8,9},{9,8},{10,11... | collective-permute-start | bytes 6291464 | tf_op jit(solution)/shard_map/ppermute | solution.py:961
  392.4 10.6 %collective-permute-start.25 = (bf16[1664,512]{1,0:T(8,128)(2,1)S(1)}, bf16[1664,512]{1,0:T(8,128)(2,1)S(1)}, u32[]{:S(2)}, u32[]{:S(2)}) collective-permute-start(bf16[1664,512]{1,0:T(8,128)(2,1)S(1)} %shard_map.252.refs_1_), channel_id=1, source_target_pairs={{0,1},{1,0},{2,3},{3,2},{4,5},{5,4},{6,7},{7,6},{8,9},{9,8},{10,11... | collective-permute-start | bytes 5111816 | tf_op jit(solution)/shard_map/ppermute | solution.py:961
  (49 other events, 485.8 us)
Sparse Core Ops, SparseCore 0:
  43.8 47.4 all-gather.2

commit v3 on v2

--- a/solution.py
+++ b/solution.py
@@ -142,7 +142,7 @@
 LARGE = 256 << 10
 
 
-def kernel_call(body, outs, operands, scalars=0, scratch=(), out_specs=None, flops=0, after=(), direct=False):
+def kernel_call(body, outs, operands, scalars=0, scratch=(), out_specs=None, flops=0, after=(), direct=False, weight=20, room_for=52):
     size = sum(bytes_of(x) for x in (*operands, *outs))
     held = size + (sum(bytes_of(x) for x in scratch) if direct else 0)
     count, many, extra = len(operands), len(outs), len(scratch)
@@ -191,8 +191,8 @@
         in_specs=in_specs,
         out_specs=tuple(specs),
         scratch_shapes=list(scratch) + room + sems,
-        compiler_params=pltpu.CompilerParams(vmem_limit_bytes=held + (3 << 20) if direct else 62 << 20),
-        cost_estimate=pl.CostEstimate(flops=flops, bytes_accessed=size, transcendentals=0),
+        compiler_params=pltpu.CompilerParams(vmem_limit_bytes=held + (3 << 20) if direct else room_for << 20),
+        cost_estimate=pl.CostEstimate(flops=weight * (flops or 2 * FLOP_UNIT), bytes_accessed=weight * size, transcendentals=0),
     )(*(x.value if isinstance(x, Raw) else x for x in operands), *after)
 
 
@@ -272,6 +272,7 @@
         scalars=3,
         out_specs=(SMEM, VMEM, VMEM, VMEM),
         direct=True,
+        weight=0,
     )
 
 
@@ -384,6 +385,16 @@
         sent[rows, :] = value
 
 
+def put_side(flags, side, mine, theirs, rows, value):
+    @pl.when(flags[0, 0] == side)
+    def _():
+        mine[rows, :] = value
+
+    @pl.when(flags[0, 0] != side)
+    def _():
+        theirs[rows, :] = value
+
+
 def rows_at(start, count=D):
     return slice(start, start + count)
 
@@ -479,7 +490,7 @@
         active[at, cols], slope[at, cols] = gelu_parts(hidden)
 
 
-def encoder_ff_kernel(z1, expand, contract, cross, small, inner, z2, memory, states, active):
+def encoder_ff_kernel(flags, z1, expand, contract, cross, small, inner, z2, mine, theirs, states, active):
     def block(at):
         unit, _ = normalized(z1[at, :])
         value = scaled(unit, small, 0)
@@ -492,16 +503,16 @@
         z2[at, :] = total
         unit, _ = normalized(total)
         out = scaled(unit, small, 1)
-        memory[at, :] = out.astype(BF)
+        put_side(flags, 0, mine, theirs, at, out.astype(BF))
         got = nn(out.astype(BF), cross[...])
         states[at, :D] = got[:, :D].astype(BF)
         states[at, D:] = (got[:, D:] + small[6:7, :]).astype(BF)
 
     each_block(block)
-    leave(inner, z2, memory)
-
-
-def ff_back(flags, dzb, value_b, active, inner, expand, contract, kept, sent, bias_rows):
+    leave(inner, z2)
+
+
+def ff_back(flags, dzb, value_b, active, inner, contract, kept, sent, bias_rows):
     def block(at):
         for j in range(FF // D):
             cols = rows_at(j * D)
@@ -518,7 +529,7 @@
 
 def decoder_ff_kernel(
     flags, z2, expand, contract, small, cotangent,
-    decoded, kept, sent, bias_grads, bias_rows, dz2,
+    mine, theirs, kept, sent, bias_grads, bias_rows, dz2,
     active, inner, value_b, dz, dzb,
 ):
     bias_grads[...] = jnp.zeros_like(bias_grads)
@@ -531,7 +542,7 @@
         expand_block(value.astype(BF), expand, small, active, inner, at)
         total = value + nn(active[at, :], contract[...]) + small[5:6, :]
         unit, scale = normalized(total)
-        decoded[at, :] = scaled(unit, small, 2).astype(BF)
+        put_side(flags, 1, mine, theirs, at, scaled(unit, small, 2).astype(BF))
         wanted = cotangent[pl.ds(pl.multiple_of(offset + at.start, BLOCK), BLOCK), :].astype(F32)
         bias_grads[0:1, :] += column_sum(wanted * unit)
         bias_grads[1:2, :] += column_sum(wanted)
@@ -541,9 +552,8 @@
         dzb[at, :] = back.astype(BF)
 
     each_block(block)
-    leave(decoded)
-    ff_back(flags, dzb, value_b, active, inner, expand, contract, kept, sent, bias_rows)
-    leave(kept, sent)
+    leave(mine, theirs)
+    ff_back(flags, dzb, value_b, active, inner, contract, kept, sent, bias_rows)
 
     def last(at):
         back = dz[at, :] + nt(inner[at, :], expand[...])
@@ -557,11 +567,11 @@
 
 def encoder_ff_back_kernel(
     flags, z2, dstates, z1, hidden, own_cross, own_expand, own_contract, rest, half, last_half, small,
-    cross_grads, kept, sent, bias_grads, bias_rows, dz1,
-    cross, expand, contract, active, inner, value_b, memory_b, dz, dzb, sems,
+    kept, sent, bias_grads, bias_rows, inner, dz,
+    cross, contract, active, value_b, memory_b, dzb, sems,
 ):
     own = (own_cross, own_expand, own_contract, rest, half, last_half)
-    cross, expand, contract = fetch_rest(0, flags, *own, cross, expand, contract, sems)
+    cross, _, contract = fetch_rest(0, flags, *own, cross, None, contract, sems)
     bias_grads[...] = jnp.zeros_like(bias_grads)
 
     def block(at):
@@ -582,25 +592,17 @@
             active[at, cols], inner[at, cols] = gelu_parts(hidden[at, cols])
 
     each_block(block)
-    ff_back(flags, dzb, value_b, active, inner, expand, contract, kept, sent, bias_rows)
+    leave(dz)
+    ff_back(flags, dzb, value_b, active, inner, contract, kept, sent, bias_rows)
+    leave(inner)
     for c in range(2):
-        cross_grads[rows_at(c * D), :] = tn(memory_b[...], dstates[:, rows_at(c * D)]).astype(BF)
-    leave(kept, sent, cross_grads)
-
-    def last(at):
-        back = dz[at, :] + nt(inner[at, :], expand[...])
-        unit, scale = normalized(z1[at, :])
-        bias_grads[4:5, :] += column_sum(back * unit)
-        bias_grads[5:6, :] += column_sum(back)
-        dz1[at, :] = normalized_back(back * small[7:8, :], unit, scale)
-
-    each_block(last)
+        put(flags, c, kept, sent, rows_at(FF), tn(memory_b[...], dstates[:, rows_at(c * D)]).astype(BF))
 
 
 def encoder_ff_back(flags, dstates, z1, z2, hidden, weights, small, after=()):
     outs = (
-        shaped(2 * D, D, BF), shaped(FF, D, BF), shaped(FF, D, BF),
-        shaped(8, D, F32), shaped(8, D, F32), shaped(T, D, F32),
+        shaped(FF + D, D, BF), shaped(FF + D, D, BF),
+        shaped(8, D, F32), shaped(8, D, F32), shaped(T, FF, BF), shaped(T, D, F32),
     )
     return kernel_call(
         encoder_ff_back_kernel,
@@ -609,17 +611,45 @@
         scalars=1,
         scratch=[
             pltpu.VMEM((D, 2 * D), BF),
-            pltpu.VMEM((D, FF), BF),
             pltpu.VMEM((FF, D), BF),
-            pltpu.VMEM((T, FF), BF),
             pltpu.VMEM((T, FF), BF),
             pltpu.VMEM((T, D), BF),
             pltpu.VMEM((T, D), BF),
-            pltpu.VMEM((T, D), F32),
             pltpu.VMEM((T, D), BF),
             pltpu.SemaphoreType.DMA((3,)),
         ],
-        flops=22 * FLOP_UNIT,
+        flops=18 * FLOP_UNIT,
+        after=after,
+    )
+
+
+def encoder_ff_last_kernel(
+    flags, inner, dz, z1, own_cross, own_expand, own_contract, rest, half, last_half, small,
+    bias_grads, dz1,
+    expand, sems,
+):
+    own = (own_cross, own_expand, own_contract, rest, half, last_half)
+    _, expand, _ = fetch_rest(0, flags, *own, None, expand, None, sems)
+    bias_grads[...] = jnp.zeros_like(bias_grads)
+
+    def last(at):
+        back = dz[at, :] + nt(inner[at, :], expand[...])
+        unit, scale = normalized(z1[at, :])
+        bias_grads[4:5, :] += column_sum(back * unit)
+        bias_grads[5:6, :] += column_sum(back)
+        dz1[at, :] = normalized_back(back * small[7:8, :], unit, scale)
+
+    each_block(last)
+
+
+def encoder_ff_last(flags, inner, dz, z1, weights, small, after=()):
+    return kernel_call(
+        encoder_ff_last_kernel,
+        (shaped(8, D, F32), shaped(T, D, F32)),
+        (flags, inner, dz, z1, *map(Raw, weights), small),
+        scalars=1,
+        scratch=[pltpu.VMEM((D, FF), BF), pltpu.SemaphoreType.DMA((3,))],
+        flops=4 * FLOP_UNIT,
         after=after,
     )
 
@@ -641,8 +671,8 @@
 
 
 def decoder_cross_back_kernel(
-    table, bias, dz2, z1, queries, states, mixed, stats, weight, small,
-    grads, bias_grads, dstates, dz1,
+    table, flags, bias, dz2, z1, queries, states, mixed, stats, weight, small,
+    kept, sent, bias_grads, dstates, dz1,
     value_b, dzb, out, dq,
 ):
     bias_grads[...] = jnp.zeros_like(bias_grads)
@@ -658,9 +688,9 @@
     each_block(before)
     attend_back(table, bias, queries, *thirds(states), stats, out, dq, *thirds(dstates))
     leave(dstates)
-    grads[:D, :] = tn(value_b[...], dq[...]).astype(BF)
-    grads[D:, :] = tn(mixed[...], dzb[...]).astype(BF)
-    leave(grads)
+    put(flags, 0, kept, sent, rows_at(FF), tn(value_b[...], dq[...]).astype(BF))
+    put(flags, 1, kept, sent, rows_at(FF), tn(mixed[...], dzb[...]).astype(BF))
+    leave(kept, sent)
 
     def after(at):
         back = dz2[at, :] + nt(dq[at, :], weight[:, :D])
@@ -672,7 +702,7 @@
     each_block(after)
 
 
-def self_back(table, bias, flags, dz, x, joined, mixed, stats, weight_in, weight_out, cross, kept, sent, acc, dzb, out, djoined):
+def self_back(table, bias, flags, dz, x, joined, mixed, stats, weight_in, weight_out, kept, sent, acc, dzb, out, djoined):
     acc[...] = jnp.zeros_like(acc)
 
     def before(at):
@@ -683,17 +713,15 @@
 
     each_block(before)
     attend_back(table, bias, *thirds(joined), stats, out, *thirds(djoined))
-    for half in range(2):
-        put(flags, half, kept, sent, rows_at(0), cross[rows_at(half * D), :])
     for c in range(3):
         value = tn(x[...], djoined[:, rows_at(c * D)]).astype(BF)
-        put(flags, c // 2, kept, sent, rows_at(D + c % 2 * D), value)
-    put(flags, 1, kept, sent, rows_at(2 * D), tn(mixed[...], dzb[...]).astype(BF))
+        put(flags, c // 2, kept, sent, rows_at(c % 2 * D), value)
+    put(flags, 1, kept, sent, rows_at(D), tn(mixed[...], dzb[...]).astype(BF))
 
 
 def put_small(flags, kept, sent, rows):
-    count = kept.shape[0] - 3 * D
-    at = rows_at(3 * D, count)
+    count = kept.shape[0] - 2 * D
+    at = rows_at(2 * D, count)
     filled = jnp.concatenate(rows + [jnp.zeros((count - 13, D), F32)], axis=0).astype(BF)
     put(flags, 0, kept, sent, at, filled)
     put(flags, 1, kept, sent, at, jnp.zeros((count, D), BF))
@@ -701,12 +729,12 @@
 
 def decoder_self_back_kernel(
     table, flags, dz, own_in, own_out, half, rest, joined, bias, stats, x, mixed, glance, places,
-    cross, ff_bias, ff_rows, cross_bias,
+    ff_bias, ff_rows, cross_bias,
     kept, sent, target_grad, source_grad,
     weight_in, weight_out, acc, dzb, out, djoined, dcopied, sems,
 ):
     weight_in, weight_out = fetch_self(1, flags, own_in, own_out, half, rest, weight_in, weight_out, sems)
-    self_back(table, bias, flags, dz, x, joined, mixed, stats, weight_in, weight_out, cross, kept, sent, acc, dzb, out, djoined)
+    self_back(table, bias, flags, dz, x, joined, mixed, stats, weight_in, weight_out, kept, sent, acc, dzb, out, djoined)
     put_small(
         flags, kept, sent,
         [
@@ -737,16 +765,16 @@
 
 
 def half_rows(count):
-    return 3 * D + 8 * count
-
-
-def decoder_self_back(table, flags, bias, dz, x, joined, mixed, stats, glance, places, weights, cross, ff_bias, ff_rows, cross_bias, count, after=()):
+    return 2 * D + 8 * count
+
+
+def decoder_self_back(table, flags, bias, dz, x, joined, mixed, stats, glance, places, weights, ff_bias, ff_rows, cross_bias, count, after=()):
     half = half_rows(count)
     outs = (shaped(half, D, BF), shaped(half, D, BF), shaped(T, D, BF), shaped(T, D, BF))
     return kernel_call(
         decoder_self_back_kernel,
         outs,
-        (table, flags, dz, *map(Raw, weights), joined, bias, stats, x, mixed, glance, places, cross, ff_bias, ff_rows, cross_bias),
+        (table, flags, dz, *map(Raw, weights), joined, bias, stats, x, mixed, glance, places, ff_bias, ff_rows, cross_bias),
         scalars=2,
         scratch=[
             pltpu.VMEM((D, 3 * D), BF), pltpu.VMEM((D, D), BF),
@@ -759,9 +787,9 @@
 
 
 def encoder_self_back_kernel(
-    table, flags, dz, rows, got, own_in, own_out, half, rest, joined, bias, stats, mixed, copies_grad, small,
-    cross, ff_bias, ff_rows,
-    kept, sent, source_grad,
+    table, flags, dz, rows, got_0, got_1, own_in, own_out, half, rest, joined, bias, stats, mixed, copies_grad, small,
+    ff_bias, ff_rows, last_bias, target_grad,
+    kept, sent, mine, theirs,
     source, weight_in, weight_out, acc, x, dzb, out, djoined, sems,
 ):
     @pl.when(flags[0, 0] == 0)
@@ -770,7 +798,7 @@
 
     @pl.when(flags[0, 0] != 0)
     def _():
-        start((got, source, sems.at[2]))
+        start(*row_parts((got_0, got_1), source, sems.at[2]))
 
     source = Landing(source, sems.at[2])
     weight_in, weight_out = fetch_self(0, flags, own_in, own_out, half, rest, weight_in, weight_out, sems)
@@ -780,33 +808,35 @@
         x[at, :] = scaled(unit, small, 2).astype(BF)
 
     each_block(first)
-    self_back(table, bias, flags, dz, x, joined, mixed, stats, weight_in, weight_out, cross, kept, sent, acc, dzb, out, djoined)
+    self_back(table, bias, flags, dz, x, joined, mixed, stats, weight_in, weight_out, kept, sent, acc, dzb, out, djoined)
 
     def after(at):
         back = dz[at, :] + nt(djoined[at, :], weight_in[...])
         unit, scale = normalized(source[at, :].astype(F32))
         acc[1:2, :] += column_sum(back * unit)
         acc[2:3, :] += column_sum(back)
-        source_grad[at, :] = (normalized_back(back * small[9:10, :], unit, scale) + copies_grad[at, :].astype(F32)).astype(BF)
+        value = normalized_back(back * small[9:10, :], unit, scale) + copies_grad[at, :].astype(F32)
+        put_side(flags, 0, mine, theirs, at, value.astype(BF))
+        put_side(flags, 1, mine, theirs, at, target_grad[at, :])
 
     each_block(after)
     put_small(
         flags, kept, sent,
         [
             ff_rows[0:4, :], acc[0:1, :], ff_bias[3:4, :], ff_bias[0:1, :],
-            ff_bias[4:5, :], ff_bias[1:2, :], acc[1:2, :],
-            ff_bias[5:6, :], ff_bias[2:3, :], acc[2:3, :],
+            last_bias[4:5, :], ff_bias[1:2, :], acc[1:2, :],
+            last_bias[5:6, :], ff_bias[2:3, :], acc[2:3, :],
         ],
     )
 
 
-def encoder_self_back(table, flags, bias, dz, rows, got, joined, mixed, stats, copies_grad, weights, small, cross, ff_bias, ff_rows, count, after=()):
+def encoder_self_back(table, flags, bias, dz, rows, got, joined, mixed, stats, copies_grad, weights, small, ff_bias, ff_rows, last_bias, target_grad, count, after=()):
     half = half_rows(count)
-    outs = (shaped(half, D, BF), shaped(half, D, BF), shaped(T, D, BF))
+    outs = (shaped(half, D, BF), shaped(half, D, BF), shaped(T, D, BF), shaped(T, D, BF))
     return kernel_call(
         encoder_self_back_kernel,
         outs,
-        (table, flags, dz, Raw(rows), Raw(got), *map(Raw, weights), joined, bias, stats, mixed, copies_grad, small, cross, ff_bias, ff_rows),
+        (table, flags, dz, Raw(rows), *map(Raw, got), *map(Raw, weights), joined, bias, stats, mixed, copies_grad, small, ff_bias, ff_rows, last_bias, target_grad),
         scalars=2,
         scratch=[
             pltpu.VMEM((T, D), BF), pltpu.VMEM((D, 3 * D), BF), pltpu.VMEM((D, D), BF),
@@ -844,40 +874,47 @@
     own = flags[0, 0] == layer
 
     def other(low, high):
-        start(
-            *((rest.at[rows_at((2 + j) * D), :], expand.at[:, rows_at(j * D)], sems.at[1]) for j in range(2)),
-            *((low.at[rows_at(j * D), :], expand.at[:, rows_at((2 + j) * D)], sems.at[1]) for j in range(2)),
-            (low.at[rows_at(2 * D), :], contract.at[rows_at(0), :], sems.at[2]),
-            (high, contract.at[rows_at(D, 3 * D), :], sems.at[2]),
-            *((rest.at[rows_at(j * D), :], cross.at[:, rows_at(j * D)], sems.at[0]) for j in range(2)),
-        )
-
-    pl.when(own)(
-        lambda: start((own_expand, expand, sems.at[1]), (own_contract, contract, sems.at[2]), (own_cross, cross, sems.at[0]))
-    )
+        copies = [(rest.at[rows_at((2 + j) * D), :], expand.at[:, rows_at(j * D)], 1) for j in range(2)] if expand is not None else []
+        copies += [(low.at[rows_at(j * D), :], expand.at[:, rows_at((2 + j) * D)], 1) for j in range(2)] if expand is not None else []
+        if contract is not None:
+            copies.append((low.at[rows_at(2 * D), :], contract.at[rows_at(0), :], 2))
+            copies.append((high, contract.at[rows_at(D, 3 * D), :], 2))
+        if cross is not None:
+            copies += [(rest.at[rows_at(j * D), :], cross.at[:, rows_at(j * D)], 0) for j in range(2)]
+        start(*((source, target, sems.at[i]) for source, target, i in copies))
+
+    pairs = ((own_expand, expand, 1), (own_contract, contract, 2), (own_cross, cross, 0))
+    pl.when(own)(lambda: start(*((source, target, sems.at[i]) for source, target, i in pairs if target is not None)))
     pl.when(jnp.logical_not(own) & (flags[0, 1] == 0))(lambda: other(half, last))
     pl.when(jnp.logical_not(own) & (flags[0, 1] != 0))(lambda: other(last, half))
-    return Landing(cross, sems.at[0]), Landing(expand, sems.at[1]), Landing(contract, sems.at[2])
+    return tuple(ref if ref is None else Landing(ref, sems.at[i]) for i, ref in enumerate((cross, expand, contract)))
+
+
+PARTS = ((0, 384), (384, 640))
+
+
+def row_parts(parts, to, sem):
+    return [(part, to.at[rows_at(at, size), :], sem) for part, (at, size) in zip(parts, PARTS)]
 
 
 def fetch_rows(flags, rows, got, source, target, sems):
     @pl.when(flags[0, 0] == 0)
     def _():
-        start((rows.at[rows_at(0, T), :], source, sems.at[0]), (got, target, sems.at[1]))
+        start((rows.at[rows_at(0, T), :], source, sems.at[0]), *row_parts(got, target, sems.at[1]))
 
     @pl.when(flags[0, 0] != 0)
     def _():
-        start((got, source, sems.at[0]), (rows.at[rows_at(T, T), :], target, sems.at[1]))
+        start(*row_parts(got, source, sems.at[0]), (rows.at[rows_at(T, T), :], target, sems.at[1]))
 
     return Landing(source, sems.at[0]), Landing(target, sems.at[1])
 
 
 def first_kernel(
-    table, flags, rows, got, own_in, own_out, half, rest, bias, glance, places, small, small_other,
+    table, flags, rows, got_0, got_1, own_in, own_out, half, rest, bias, glance, places, small, small_other,
     e_small, d_small, e_joined, e_mixed, e_stats, e_z, x, d_joined, d_mixed, d_stats, d_z,
     source, target, e_in, e_out, d_in, d_out, wide, copied, sems,
 ):
-    source, target = fetch_rows(flags, rows, got, source, target, sems.at[pl.ds(0, 2)])
+    source, target = fetch_rows(flags, rows, (got_0, got_1), source, target, sems.at[pl.ds(0, 2)])
     e_in, e_out = fetch_self(0, flags, own_in, own_out, half, rest, e_in, e_out, sems.at[pl.ds(2, 2)])
     d_in, d_out = fetch_self(1, flags, own_in, own_out, half, rest, d_in, d_out, sems.at[pl.ds(4, 2)])
 
@@ -902,7 +939,7 @@
     return kernel_call(
         first_kernel,
         outs,
-        (table, flags, Raw(rows), Raw(got), *map(Raw, weights), bias, glance, places, small, small_other),
+        (table, flags, Raw(rows), *map(Raw, got), *map(Raw, weights), bias, glance, places, small, small_other),
         scalars=2,
         scratch=[
             pltpu.VMEM((T, D), BF), pltpu.VMEM((T, D), BF),
@@ -910,26 +947,27 @@
             pltpu.VMEM((T, D), F32), pltpu.VMEM((T, D), BF), pltpu.SemaphoreType.DMA((6,)),
         ],
         flops=24 * FLOP_UNIT,
+        weight=0,
     )
 
 
 def middle_kernel(
     table, flags, e_z1, own_cross, own_expand, own_contract, rest, half, last, bias, d_z1, cotangent, e_small, d_small,
-    hidden, e_z2, memory, decoded, kept, sent, ff_bias, ff_rows, cross_grads, cross_bias, dstates, dz1,
+    hidden, e_z2, mine, theirs, kept, sent, ff_bias, ff_rows, cross_bias, dstates, dz1,
     e_cross, e_expand, e_contract, d_cross, d_expand, d_contract,
     active, states, queries, mixed, stats, d_z2, wide, inner, value_b, dzb, dz2, sems,
 ):
     own = (own_cross, own_expand, own_contract, rest, half, last)
     e_cross, e_expand, e_contract = fetch_rest(0, flags, *own, e_cross, e_expand, e_contract, sems.at[pl.ds(0, 3)])
     d_cross, d_expand, d_contract = fetch_rest(1, flags, *own, d_cross, d_expand, d_contract, sems.at[pl.ds(3, 3)])
-    encoder_ff_kernel(e_z1, e_expand, e_contract, e_cross, e_small, hidden, e_z2, memory, states, active)
+    encoder_ff_kernel(flags, e_z1, e_expand, e_contract, e_cross, e_small, hidden, e_z2, mine, theirs, states, active)
     decoder_cross_kernel(table, bias, d_z1, states, d_cross, d_small, queries, mixed, stats, d_z2, wide)
     decoder_ff_kernel(
-        flags, d_z2, d_expand, d_contract, d_small, cotangent, decoded, kept, sent, ff_bias, ff_rows, dz2,
+        flags, d_z2, d_expand, d_contract, d_small, cotangent, mine, theirs, kept, sent, ff_bias, ff_rows, dz2,
         active, inner, value_b, wide, dzb,
     )
     decoder_cross_back_kernel(
-        table, bias, dz2, d_z1, queries, states, mixed, stats, d_cross, d_small, cross_grads, cross_bias, dstates, dz1,
+        table, flags, bias, dz2, d_z1, queries, states, mixed, stats, d_cross, d_small, kept, sent, cross_bias, dstates, dz1,
         value_b, dzb, active.at[:, rows_at(0)], active.at[:, rows_at(D)],
     )
 
@@ -937,8 +975,8 @@
 def middle(table, flags, bias, e_z1, d_z1, weights, cotangent, e_small, d_small):
     low, high = shaped(T, D, BF), shaped(T, D, F32)
     outs = (
-        shaped(T, FF, BF), high, low, low, shaped(FF, D, BF), shaped(FF, D, BF),
-        shaped(8, D, F32), shaped(8, D, F32), shaped(2 * D, D, BF), shaped(8, D, F32), shaped(T, 2 * D, BF), high,
+        shaped(T, FF, BF), high, low, low, shaped(FF + D, D, BF), shaped(FF + D, D, BF),
+        shaped(8, D, F32), shaped(8, D, F32), shaped(8, D, F32), shaped(T, 2 * D, BF), high,
     )
     weight_room = [pltpu.VMEM((D, 2 * D), BF), pltpu.VMEM((D, FF), BF), pltpu.VMEM((FF, D), BF)]
     return kernel_call(
@@ -953,6 +991,7 @@
             pltpu.VMEM((T, D), BF), pltpu.VMEM((T, D), BF), pltpu.VMEM((T, D), F32), pltpu.SemaphoreType.DMA((6,)),
         ],
         flops=54 * FLOP_UNIT,
+        room_for=62,
     )
 
 
@@ -969,15 +1008,16 @@
     return (first.astype(F32) + second.astype(F32)).astype(BF)
 
 
-def gate(value, after):
+def gate(values, after):
     anywhere = pl.BlockSpec(memory_space=pl.ANY)
     return pl.pallas_call(
         lambda *refs: None,
-        out_shape=jax.ShapeDtypeStruct(value.shape, value.dtype),
-        in_specs=[anywhere] * (1 + len(after)),
-        out_specs=anywhere,
-        input_output_aliases={0: 0},
-    )(value, *after)
+        out_shape=tuple(jax.ShapeDtypeStruct(value.shape, value.dtype) for value in values),
+        in_specs=[anywhere] * (len(values) + len(after)),
+        out_specs=(anywhere,) * len(values),
+        input_output_aliases={i: i for i in range(len(values))},
+        cost_estimate=pl.CostEstimate(flops=0, bytes_accessed=0, transcendentals=0),
+    )(*values, *after)
 
 
 def halve_kernel(step, pairs, flags, *refs):
@@ -1014,12 +1054,16 @@
         keep[...], send[...] = sums[1], sums[0]
 
 
+def add_kernel(first, second, out):
+    out[...] = added(first[...], second[...])
+
+
 class Steps:
     def __init__(self):
         count = lax.axis_size("dp")
         bits = list(range(1, (count - 1).bit_length()))
-        cut = max(1, len(bits) // 3)
-        orders = (bits, bits[cut:] + bits[:cut])
+        cut = (len(bits) + 1) // 3
+        orders = (bits, bits[cut : 2 * cut] + bits[:cut] + bits[2 * cut :])
         index = lax.axis_index("dp")
         core = index & 1
         self.partners = [lambda i: i ^ 1]
@@ -1044,23 +1088,34 @@
             functools.partial(halve_kernel, step + 1, len(pairs)), (shape, shape), (self.flags, *operands), scalars=1, after=after, direct=True
         )
 
-    def double(self, step, own, got, after=()):
+    def double(self, step, own, got, after=(), weight=20):
         out = (shaped(2 * own.shape[0], D, BF),)
-        return kernel_call(functools.partial(double_kernel, step), out, (self.flags, own, got), scalars=1, after=after, direct=True)[0]
-
-    def half_gathered(self, value, after):
+        return kernel_call(functools.partial(double_kernel, step), out, (self.flags, own, got), scalars=1, after=after, direct=True, weight=weight)[0]
+
+    def half_gathered(self, value, afters):
         parts = []
         for step in range(self.last, 0, -1):
-            value = self.double(step, value, self.swap(value, step), after=after if step == 1 else ())
+            after = afters[step - 1] if step <= len(afters) else ()
+            value = self.double(step, value, self.swap(value, step), after=after, weight=0)
             parts.append(value)
         return parts
 
-    def across(self, *pairs, after=()):
+    def doubled(self, pairs, after, spill, outs):
         shape = shaped(*pairs[0][0].shape[1:], BF)
         operands = [x for pair in pairs for x in pair]
-        return kernel_call(
+        kept, sent = kernel_call(
             functools.partial(across_kernel, len(pairs)), (shape, shape), (self.flags, *operands), scalars=1, after=after, direct=True
         )
+        got = swapped_pipe(sent)
+        after = yield kept
+        (value,) = kernel_call(add_kernel, (shape,), (kept, got), after=after, direct=True)
+        for step in range(self.last, 0, -1):
+            got = self.swap(value, step)
+            after = yield value
+            value = self.double(step, value, got, after=after)
+        got = self.swap(value, 0)
+        after = yield value
+        yield tuple(kernel_call(spill, outs, (self.flags, value, got), scalars=1, after=after, direct=True))
 
 
 def by_core(flags, first, second, body):
@@ -1068,24 +1123,23 @@
     pl.when(flags[0, 1] != 0)(lambda: body(second, first))
 
 
-def spill_ff_kernel(flags, own, other, expand, contract):
+def spill_ff_kernel(flags, own, other, expand, contract, cross):
     def fill(low, high):
         for j in range(FF // D):
             expand[:, rows_at(j * D)] = low[rows_at(j * D), :].astype(F32)
             contract[rows_at(j * D), :] = high[rows_at(j * D), :].astype(F32)
+        cross[:, rows_at(0)] = low[rows_at(FF), :].astype(F32)
+        cross[:, rows_at(D)] = high[rows_at(FF), :].astype(F32)
 
     by_core(flags, own, other, fill)
 
 
-def spill_rest_kernel(flags, own, other, joined, out, cross, expand_bias, branch, gain, shift):
+def spill_rest_kernel(flags, own, other, joined, out, expand_bias, branch, gain, shift):
     def fill(low, high):
-        spots = (
-            (low, 0, cross, 0), (low, 1, joined, 0), (low, 2, joined, 1),
-            (high, 0, cross, 1), (high, 1, joined, 2), (high, 2, out, 0),
-        )
+        spots = ((low, 0, joined, 0), (low, 1, joined, 1), (high, 0, joined, 2), (high, 1, out, 0))
         for ref, block, to, column in spots:
             to[:, rows_at(column * D)] = ref[rows_at(block * D), :].astype(F32)
-        value = low[rows_at(3 * D, 16), :].astype(F32)
+        value = low[rows_at(2 * D, 16), :].astype(F32)
         for j in range(FF // D):
             expand_bias[0:1, rows_at(j * D)] = value[j : j + 1, :]
         branch[...] = value[4:7, :]
@@ -1120,8 +1174,6 @@
 
     rows = embeddings[0]
     small = jnp.concatenate([expand_bias.reshape(4, D), branch_bias[0], norm_gain[0], norm_shift[0]], 0)
-    small_other = swapped_pipe(small)
-    got = swapped_pipe(gate(lax.dynamic_slice_in_dim(rows, (1 - pipe) * T, T, 0), (small_other,)))
     size = 4 * D // count
 
     def piece(place, blocks_of):
@@ -1134,106 +1186,124 @@
 
     self_piece = piece(steps.place, [(self_in, 0), (self_in, 1), (self_in, 2), (self_out, 0)])
     rest_piece = piece(lax.axis_index("dp"), [(cross_weight, 0), (cross_weight, 1), (expand, 0), (expand, 1)])
-    self_parts = steps.half_gathered(swapped_pipe(self_piece), (got,))
-    self_half = self_parts[-1]
-    (last_piece,) = kernel_call(last_kernel, (shaped(3 * D, D, BF),), (flags, expand, contract), scalars=1, after=(self_parts[-2],), direct=True)
-    self_rest = steps.swap(self_half, 0)
-    last_half = swapped_pipe(last_piece)
-    rest = lax.all_gather(swapped_pipe(rest_piece), "dp").reshape(4 * D, D)
-
     table, bias, glance, places = row_layout(
         flags, lengths, hamming, priority.reshape(2 * T // WIN, WIN), copy_index.reshape(2 * T // WIN, WIN)
     )
+    self_piece = swapped_pipe(self_piece)
+    small_other = swapped_pipe(small)
+    theirs = [lax.dynamic_slice_in_dim(rows, (1 - pipe) * T + at, size, 0) for at, size in PARTS]
+    got = [swapped_pipe(part) for part in gate(theirs, (self_piece, small_other))]
+    self_parts = steps.half_gathered(self_piece, ((bias,), (got[1],), (got[0],)))
+    self_half = self_parts[-1]
+    self_rest = steps.swap(self_half, 0)
+    (last_piece,) = kernel_call(last_kernel, (shaped(3 * D, D, BF),), (flags, expand, contract), scalars=1, after=(self_parts[-2],), direct=True, weight=0)
+    last_half = swapped_pipe(last_piece)
+    (rest_piece,) = gate((swapped_pipe(rest_piece),), (self_parts[-2],))
+    rest = lax.all_gather(rest_piece, "dp").reshape(4 * D, D)
+
     self_weights = (self_in, self_out, self_half, self_rest)
     (
         e_small, d_small, e_joined, e_mixed, e_stats, e_z1, x, d_joined, d_mixed, d_stats, d_z1,
     ) = first(table, flags, bias, glance, places, rows, got, self_weights, small, small_other)
-    last_half = gate(last_half, (d_z1,))
+    (last_half,) = gate((last_half,), (d_z1,))
     last_rest = steps.swap(last_half, 0)
     rest_weights = (cross_weight, expand, contract, rest, last_half, last_rest)
     (
-        hidden, e_z2, memory, decoded, *dec_ff, d_ff_bias, d_ff_rows, d_cross, d_cross_bias, dstates, dz1,
+        hidden, e_z2, layer_mine, layer_theirs, *dec_ff, d_ff_bias, d_ff_rows, d_cross_bias, dstates, dz1,
     ) = middle(table, flags, bias, e_z1, d_z1, rest_weights, cotangent, e_small, d_small)
 
-    def rows_swap(first, second):
-        return swapped_pipe(jnp.where(leading, second, first).astype(BF))
-
-    def rows_out(first, second, other):
-        own, other = jnp.where(leading, first, second).astype(F32), other.astype(F32)
+    def rows_out(own, other):
+        own, other = own.astype(F32), other.astype(F32)
         return jnp.where(leading, jnp.concatenate([own, other], 0), jnp.concatenate([other, own], 0))[None]
 
     def opened(pair):
         return [part[None] for part in pair]
 
-    layer_other = rows_swap(memory, decoded)
+    layer_other = swapped_pipe(layer_theirs)
     dec_kept, dec_sent = opened(dec_ff)
     dec_got = steps.swap(dec_sent, 0)
+    *dec_self, target_grad, copies_grad = decoder_self_back(
+        table, flags, bias, dz1, x, d_joined, d_mixed, d_stats, glance, places, self_weights,
+        d_ff_bias, d_ff_rows, d_cross_bias, count,
+    )
+    dself_kept, dself_sent = opened(dec_self)
+    dself_got = steps.swap(dself_sent, 0)
+    (dec_got,) = gate((dec_got,), (target_grad,))
     dec_kept, dec_sent = steps.halve(0, (dec_kept, dec_got))
     dec_got = steps.swap(dec_sent, 1)
-    *dec_self, target_grad, copies_grad = decoder_self_back(
-        table, flags, bias, dz1, x, d_joined, d_mixed, d_stats, glance, places, self_weights,
-        d_cross, d_ff_bias, d_ff_rows, d_cross_bias, count, after=(dec_kept,),
-    )
-    dself_kept, dself_sent = opened(dec_self)
-    dself_got = steps.swap(dself_sent, 0)
+    *enc_ff, e_ff_bias, e_ff_rows, inner, dz = encoder_ff_back(
+        flags, dstates, e_z1, e_z2, hidden, rest_weights, e_small, after=(dec_kept,)
+    )
+    enc_kept, enc_sent = opened(enc_ff)
+    enc_got = steps.swap(enc_sent, 0)
+    dec_got, dself_got = gate((dec_got, dself_got), (dz,))
     dec_kept, dec_sent = steps.halve(1, (dec_kept, dec_got))
     dec_got = steps.swap(dec_sent, 2)
-    e_cross, *enc_ff, e_ff_bias, e_ff_rows, e_dz1 = encoder_ff_back(
-        flags, dstates, e_z1, e_z2, hidden, rest_weights, e_small, after=(dec_kept, target_grad)
-    )
-    enc_kept, enc_sent = opened(enc_ff)
-    enc_got = steps.swap(enc_sent, 0)
     dself_kept, dself_sent = steps.halve(0, (dself_kept, dself_got))
     dself_got = steps.swap(dself_sent, 1)
+    last_bias, e_dz1 = encoder_ff_last(flags, inner, dz, e_z1, rest_weights, e_small, after=(dec_kept, dself_kept))
+    enc_got, dec_got = gate((enc_got, dec_got), (e_dz1,))
     dec_kept, dec_sent = steps.halve(2, (dec_kept, dec_got))
     dec_got = steps.swap(dec_sent, 3)
-    *enc_self, source_grad = encoder_self_back(
+    enc_kept, enc_sent = steps.halve(0, (enc_kept, enc_got))
+    enc_got = steps.swap(enc_sent, 1)
+    *enc_self, grad_mine, grad_theirs = encoder_self_back(
         table, flags, bias, e_dz1, rows, got, e_joined, e_mixed, e_stats, copies_grad, self_weights, e_small,
-        e_cross, e_ff_bias, e_ff_rows, count, after=(dec_kept, dself_kept),
-    )
-    grad_other = rows_swap(source_grad, target_grad)
+        e_ff_bias, e_ff_rows, last_bias, target_grad, count, after=(enc_kept, dec_kept),
+    )
+
+    grad_other = swapped_pipe(grad_theirs)
     self_kept, self_sent = opened(enc_self)
     self_got = steps.swap(self_sent, 0)
-    enc_kept, enc_sent = steps.halve(0, (enc_kept, enc_got), after=(source_grad,))
-    enc_got = steps.swap(enc_sent, 1)
-    self_kept, self_sent = steps.halve(0, (self_kept, self_got))
-    self_got = steps.swap(self_sent, 1)
-    for step in range(3, steps.last):
-        dec_kept, dec_sent = steps.halve(step, (dec_kept, dec_got))
-        dec_got = steps.swap(dec_sent, step + 1)
-    mark = (self_kept,)
-    ff_step, self_step = 1, 1
-    self_pairs = [(self_kept, self_got), (dself_kept, dself_got)]
-    enc_pair = (enc_kept, enc_got)
-    while ff_step < steps.last:
-        kept, sent = steps.halve(ff_step, enc_pair, after=mark)
-        ff_step += 1
-        enc_pair = (kept, steps.swap(sent, ff_step))
-        if self_step < steps.last:
-            kept, sent = steps.halve(self_step, *self_pairs)
-            self_step += 1
-            self_pairs = [(kept, steps.swap(sent, self_step))]
-            mark = (kept,)
-    keep, send = steps.across(enc_pair, (dec_kept, dec_got), after=mark + (grad_other,))
-    ff_got = swapped_pipe(send)
-    keep_self, send_self = steps.across(*self_pairs)
-    self_got = swapped_pipe(send_self)
-    ff = added(keep, ff_got)
-    ff_got = steps.swap(ff, steps.last)
-    rest_sum = added(keep_self, self_got)
-    self_got = steps.swap(rest_sum, steps.last)
-    for step in range(steps.last, 0, -1):
-        ff = steps.double(step, ff, ff_got, after=(rest_sum,))
-        ff_got = steps.swap(ff, step - 1)
-        rest_sum = steps.double(step, rest_sum, self_got)
-        self_got = steps.swap(rest_sum, step - 1)
-
-    layer_out = rows_out(memory, decoded, layer_other)
-    embedding_grad = rows_out(source_grad, target_grad, grad_other)
-    outs = (shaped(D, FF, F32), shaped(FF, D, F32))
-    expand_grad, contract_grad = kernel_call(spill_ff_kernel, outs, (flags, ff, ff_got), scalars=1, direct=True)
-    outs = (shaped(D, 3 * D, F32), shaped(D, D, F32), shaped(D, 2 * D, F32), shaped(1, FF, F32)) + (shaped(3, D, F32),) * 3
-    in_grad, out_grad, cross_grad, *small_grads = kernel_call(spill_rest_kernel, outs, (flags, rest_sum, self_got), scalars=1, direct=True)
+    enc_got, dec_got, dself_got = gate((enc_got, dec_got, dself_got), (grad_mine,))
+
+    def ff_sum():
+        enc_pair, dec_pair = (enc_kept, enc_got), (dec_kept, dec_got)
+        after = yield
+        for step in range(1, steps.last):
+            kept, sent = steps.halve(step, enc_pair, after=after)
+            enc_pair = (kept, steps.swap(sent, step + 1))
+            if step + 2 < steps.last:
+                kept, sent = steps.halve(step + 2, dec_pair, after=(kept,))
+                dec_pair = (kept, steps.swap(sent, step + 3))
+            after = yield kept
+        outs = (shaped(D, FF, F32), shaped(FF, D, F32), shaped(D, 2 * D, F32))
+        yield from steps.doubled((enc_pair, dec_pair), after, spill_ff_kernel, outs)
+
+    def self_sum():
+        pairs = [(self_kept, self_got)]
+        after = yield
+        for step in range(steps.last):
+            kept, sent = steps.halve(step, *pairs, after=after)
+            pairs = [(kept, steps.swap(sent, step + 1))]
+            if step == 0:
+                pairs.append((dself_kept, dself_got))
+            after = yield kept
+        outs = (shaped(D, 3 * D, F32), shaped(D, D, F32), shaped(1, FF, F32)) + (shaped(3, D, F32),) * 3
+        yield from steps.doubled(pairs, after, spill_rest_kernel, outs)
+
+    chains = [ff_sum(), self_sum()]
+    results = [None, None]
+    mark = dself_got
+    for chain in chains:
+        next(chain)
+    live = [0, 1]
+    turn = 0
+    while live:
+        if turn == 5:
+            layer = gate((layer_mine, layer_other), (mark,))
+            layer_out, embedding_grad = rows_out(*layer), rows_out(*gate((grad_mine, grad_other), (mark,)))
+        for i in list(live):
+            extra = (layer_out, embedding_grad) if turn == 7 else ()
+            value = chains[i].send((mark, *extra))
+            if isinstance(value, tuple):
+                results[i] = value
+                live.remove(i)
+                value = value[0]
+            mark = value
+        turn += 1
+    expand_grad, contract_grad, cross_grad = results[0]
+    in_grad, out_grad, *small_grads = results[1]
     return (
         layer_out,
         embedding_grad,

time: 429 us -> 407 us (0.949)
  waiting for transfers between devices: 148 us -> 102 us
  local copies, waits for them, and re-layouts: 20 us -> 32.5 us
  starting transfers between devices: 44.9 us -> 52 us
  Pallas kernels: 180 us -> 185 us
    ppermute x36 -> x37, waiting for transfers between devices: 148 us -> 102 us  [swapped(): return lax.ppermute(value, axis, [(i, partner(i)) for i in range(count)])]
    unnamed x78 -> x134, local copies, waits for them, and re-layouts: 17.6 us -> 28.5 us
    ppermute x36 -> x37, starting transfers between devices: 44.9 us -> 52 us  [swapped(): return lax.ppermute(value, axis, [(i, partner(i)) for i in range(count)])]
    concatenate x4, other arithmetic: 2.27 us -> 7.48 us  [rows_out(): jnp.concatenate([own, other], 0)]
    pallas_call x30 -> x33, Pallas kernels: 180 us -> 185 us  [kernel_call(): pl.pallas_call(run, out_shape=tuple(outs), in_specs=in_specs, out_specs=t...]
  transfers between devices with their start and end apart: 37 -> 38, of which waited for: 21 -> 20; matrix products, arithmetic and copies ran while one was open for 4% -> 4% of each run, Pallas kernels for 29% -> 32%
where the time goes in v3:
time: 407 us; the launch traced here: 400 us
  Pallas kernels  185 us (45%)
  waiting for transfers between devices  102 us (25%)
  starting transfers between devices  52 us (13%)
  local copies, waits for them, and re-layouts  32.5 us (8%)
  between operations  14.9 us (4%)
  other arithmetic  12.8 us (3%)
    pallas_call x33, Pallas kernels, kernel_call(): pl.pallas_call(run, out_shape=tuple(outs), in_specs=in_specs, out_specs=t...  185 us
    ppermute x37, waiting for transfers between devices, swapped(): return lax.ppermute(value, axis, [(i, partner(i)) for i in range(count)])  102 us
    ppermute x37, starting transfers between devices, swapped(): return lax.ppermute(value, axis, [(i, partner(i)) for i in range(count)])  52 us
    unnamed x134, local copies, waits for them, and re-layouts  28.5 us
  transfers between devices with their start and end apart: 38, of which 20 were waited for; matrix products, arithmetic and copies ran while one was open for 4% of the time, Pallas kernels for 32%

profile of v3, /device:TPU:1, one launch (start us, length us, event | category | flops | bytes accessed | tf_op | source)
XLA Modules:
  0.0 399.8 jit_solution(10889023012261991166)
XLA Ops:
  23.2 4.3 %collective-permute-done.4.refs_2_ = bf16[128,512]{1,0:T(8,128)(2,1)S(1)} collective-permute-done((bf16[128,512]{1,0:T(8,128)(2,1)}, bf16[128,512]{1,0:T(8,128)(2,1)S(1)}, u32[]{:S(2)}, u32[]{:S(2)}) %collective-permute-start.4) | collective-permute-done | bytes 131104 | tf_op jit(solution)/shard_map/ppermute | solution.py:1000
  36.7 5.9 %collective-permute-done.3.refs_3_.refs_4_.refs_5_ = bf16[640,512]{1,0:T(8,128)(2,1)S(1)} collective-permute-done((bf16[640,512]{1,0:T(8,128)(2,1)}, bf16[640,512]{1,0:T(8,128)(2,1)S(1)}, u32[]{:S(2)}, u32[]{:S(2)}) %collective-permute-start.3) | collective-permute-done | bytes 655392 | tf_op jit(solution)/shard_map/ppermute | solution.py:1000
  56.9 3.6 collective-permute-start.7
  63.8 21.0 %shard_map.235 = (f32[16,512]{1,0:T(8,128)S(1)}, f32[16,512]{1,0:T(8,128)S(1)}, bf16[1024,1536]{1,0:T(8,128)(2,1)}, bf16[1024,512]{1,0:T(8,128)(2,1)}, f32[72,2,...) custom-call(s32[1,128]{1,0:T(1,128)S(1)} %get-tuple-element.99.refs_, ...), custom_call_target="tpu_custom_call" | custom-call | tf_op jit(solution)/shard_map/pallas_call | solution.py:188
  88.2 3.5 collective-permute-done.10.refs_8_.refs_10_.refs_9_
  92.8 52.4 %shard_map.239 = (bf16[1024,2048]{1,0:T(8,128)(2,1)}, f32[1024,512]{1,0:T(8,128)}, bf16[1024,512]{1,0:T(8,128)(2,1)}, bf16[1024,512]{1,0:T(8,128)(2,1)}, bf16[25...) custom-call(s32[1,128]{1,0:T(1,128)} %copy-done.36, ...), custom_call_target="tpu_custom_call" | custom-call | flops 579820584960 | bytes 717957504 | tf_op jit(solution)/shard_map/pallas_call | solution.py:188
  150.0 20.6 %shard_map.240 = (bf16[1152,512]{1,0:T(8,128)(2,1)}, bf16[1152,512]{1,0:T(8,128)(2,1)}, bf16[1024,512]{1,0:T(8,128)(2,1)}, bf16[1024,512]{1,0:T(8,128)(2,1)}) custom-call(s32[1,128]{1,0:T(1,128)S(1)} %copy-done.37, s32[1,5]{1,0:T(1,128)S(1)} %bitcast.78, f32[1024,512]{1,0:T(8,128)} %get-tuple-element.116.refs_2_, bf16[512,1536]{1,0:T(8,128)(2,1)} %bitcast.115, ...), custom_call_target="tpu_custom_call" | custom-call | flops 193273528320 | bytes 368322944 | tf_op jit(solution)/shard_map/pallas_call | solution.py:188
  172.5 3.4 shard_map.242
  179.6 23.3 %shard_map.243 = (bf16[2560,512]{1,0:T(8,128)(2,1)}, bf16[2560,512]{1,0:T(8,128)(2,1)}, f32[8,512]{1,0:T(8,128)S(1)}, f32[8,512]{1,0:T(8,128)S(1)}, bf16[1024,2048]{1,0:T(8,128)(2,1)}, /*index=5*/f32[1024,512]{1,0:T(8,128)}) custom-call(s32[1,5]{1,0:T(1,128)S(1)} %bitcast.80, f32[1024,512]{1,0:T(8,128)} %get-tuple-element.111.refs_1_, ...), custom_call_target="tpu_custom_call" | custom-call | flops 193273528320 | bytes 651428224 | tf_op jit(solution)/shard_map/pallas_call | solution.py:188
  210.8 8.9 %shard_map.247 = (f32[8,512]{1,0:T(8,128)S(1)}, f32[1024,512]{1,0:T(8,128)}) custom-call(s32[1,5]{1,0:T(1,128)S(1)} %bitcast.83, bf16[1024,2048]{1,0:T(8,128)(2,1)} %get-tuple-element.126.refs_1_, f32[1024,512]{1,0:T(8,128)} %get-tuple-element.127.refs_2_, f32[1024,512]{1,0:T(8,128)} %get-tuple-element.105.refs_2_.refs_3_, bf16[512,1024]{1,0:T(8,128)(2,1)} %bitcast.69, ...), custom_call_target="tpu_custom_call" | custom-call | flops 42949672960 | bytes 420413824 | tf_op jit(solution)/shard_map/pallas_call | solution.py:188
  219.7 5.7 %collective-permute-done.16.refs_1_ = bf16[1,640,512]{2,1,0:T(8,128)(2,1)S(1)} collective-permute-done((bf16[1,640,512]{2,1,0:T(8,128)(2,1)S(1)}, bf16[1,640,512]{2,1,0:T(8,128)(2,1)S(1)}, u32[]{:S(2)}, u32[]{:S(2)}) %collective-permute-start.16) | collective-permute-done | bytes 655392 | tf_op jit(solution)/shard_map/ppermute | solution.py:1000
  230.7 4.3 %collective-permute-start.19 = (bf16[1,320,512]{2,1,0:T(8,128)(2,1)}, bf16[1,320,512]{2,1,0:T(8,128)(2,1)}, u32[]{:S(2)}, u32[]{:S(2)}) collective-permute-start(bf16[1,320,512]{2,1,0:T(8,128)(2,1)} %get-tuple-element.153), channel_id=1, source_target_pairs={{0,8},{1,9},{2,10},{3,11},{4,12},{5,13},{6,14},{7,15},{8,0},{9,1},... | collective-permute-start | bytes 983048 | tf_op jit(solution)/shard_map/ppermute | solution.py:1000
  238.2 22.2 %shard_map.251 = (bf16[1152,512]{1,0:T(8,128)(2,1)}, bf16[1152,512]{1,0:T(8,128)(2,1)}, bf16[1024,512]{1,0:T(8,128)(2,1)}, bf16[1024,512]{1,0:T(8,128)(2,1)}) custom-call(s32[1,128]{1,0:T(1,128)S(1)} %copy-done.38, s32[1,5]{1,0:T(1,128)S(1)} %bitcast.86, f32[1024,512]{1,0:T(8,128)} %get-tuple-element.135.refs_2_, bf16[2048,512]{1,0:T(8,128)(2,1)} %bitcast.113, ...), custom_call_target="tpu_custom_call" | custom-call | flops 193273528320 | bytes 431892864 | tf_op jit(solution)/shard_map/pallas_call | solution.py:188
  267.9 9.3 %collective-permute-done.22.refs_2_ = bf16[1,640,512]{2,1,0:T(8,128)(2,1)S(1)} collective-permute-done((bf16[1,640,512]{2,1,0:T(8,128)(2,1)S(1)}, bf16[1,640,512]{2,1,0:T(8,128)(2,1)S(1)}, u32[]{:S(2)}, u32[]{:S(2)}) %collective-permute-start.22) | collective-permute-done | bytes 655392 | tf_op jit(solution)/shard_map/ppermute | solution.py:1000
  277.9 3.2 collective-permute-start.24
  284.0 10.2 %collective-permute-done.24.refs_2_ = bf16[1,320,512]{2,1,0:T(8,128)(2,1)S(1)} collective-permute-done((bf16[1,320,512]{2,1,0:T(8,128)(2,1)S(1)}, bf16[1,320,512]{2,1,0:T(8,128)(2,1)S(1)}, u32[]{:S(2)}, u32[]{:S(2)}) %collective-permute-start.24) | collective-permute-done | bytes 327712 | tf_op jit(solution)/shard_map/ppermute | solution.py:1000
  297.4 4.6 %collective-permute-done.26.refs_1_ = bf16[320,512]{1,0:T(8,128)(2,1)S(1)} collective-permute-done((bf16[320,512]{1,0:T(8,128)(2,1)S(1)}, bf16[320,512]{1,0:T(8,128)(2,1)S(1)}, u32[]{:S(2)}, u32[]{:S(2)}) %collective-permute-start.26) | collective-permute-done | bytes 327712 | tf_op jit(solution)/shard_map/ppermute | solution.py:1000
  302.2 16.2 %collective-permute-done.25.refs_2_ = bf16[2,144,512]{2,1,0:T(8,128)(2,1)S(1)} collective-permute-done((bf16[2,144,512]{2,1,0:T(8,128)(2,1)S(1)}, bf16[2,144,512]{2,1,0:T(8,128)(2,1)S(1)}, u32[]{:S(2)}, u32[]{:S(2)}) %collective-permute-start.25) | collective-permute-done | bytes 294944 | tf_op jit(solution)/shard_map/ppermute | solution.py:1000
  319.9 5.6 %collective-permute-done.28.refs_2_ = bf16[320,512]{1,0:T(8,128)(2,1)S(1)} collective-permute-done((bf16[320,512]{1,0:T(8,128)(2,1)S(1)}, bf16[320,512]{1,0:T(8,128)(2,1)S(1)}, u32[]{:S(2)}, u32[]{:S(2)}) %collective-permute-start.28) | collective-permute-done | bytes 327712 | tf_op jit(solution)/shard_map/ppermute | solution.py:1000
  337.7 18.1 %collective-permute-done.33.refs_2_ = bf16[1280,512]{1,0:T(8,128)(2,1)S(1)} collective-permute-done((bf16[1280,512]{1,0:T(8,128)(2,1)S(1)}, bf16[1280,512]{1,0:T(8,128)(2,1)S(1)}, u32[]{:S(2)}, u32[]{:S(2)}) %collective-permute-start.33) | collective-permute-done | bytes 1310752 | tf_op jit(solution)/shard_map/ppermute | solution.py:1000
  356.6 7.3 %collective-permute-start.35 = (bf16[2560,512]{1,0:T(8,128)(2,1)S(1)}, bf16[2560,512]{1,0:T(8,128)(2,1)S(1)}, u32[]{:S(2)}, u32[]{:S(2)}) collective-permute-start(bf16[2560,512]{1,0:T(8,128)(2,1)S(1)} %shard_map.267.refs_3_.refs_1_), channel_id=1, source_target_pairs={{0,1},{1,0},{2,3},{3,2},{4,5},{5,4},{6,7},{7,6},{8,9},{9,8},{10,11... | collective-permute-start | bytes 7864328 | tf_op jit(solution)/shard_map/ppermute | solution.py:1000
  366.4 5.0 %collective-permute-done.32.refs_2_ = bf16[288,512]{1,0:T(8,128)(2,1)S(1)} collective-permute-done((bf16[288,512]{1,0:T(8,128)(2,1)S(1)}, bf16[288,512]{1,0:T(8,128)(2,1)S(1)}, u32[]{:S(2)}, u32[]{:S(2)}) %collective-permute-start.32) | collective-permute-done | bytes 294944 | tf_op jit(solution)/shard_map/ppermute | solution.py:1000
  372.0 5.2 %shard_map.269 = (f32[512,2048]{1,0:T(8,128)}, f32[2048,512]{1,0:T(8,128)}, f32[512,1024]{1,0:T(8,128)}) custom-call(s32[1,5]{1,0:T(1,128)S(1)} %bitcast.99, bf16[2560,512]{1,0:T(8,128)(2,1)S(1)} %shard_map.267.refs_3_.refs_1_, bf16[2560,512]{1,0:T(8,128)(2,1)S(1)} %collective-permute-done.35.refs_2_, bf16[576,512]{1,0:T(8,128)(2,1)S(1)} %shard_map.268.refs_3_.refs_1_, ...), custom_call_target="tpu_custom_call" | custom-call | flops 21474836480 | bytes 314573184 | tf_op jit(solution)/shard_map/pallas_call | solution.py:188
  377.2 3.8 collective-permute-done.34.refs_2_
  (243 shorter events, 117.3 us)
Async XLA Ops:
  7.2 84.6 %all-gather.3.cloned.1.call-start = ((), (), s32[]{:S(2)}) async-start(), calls=%async_computation | async-start | bytes 2228224 | tf_op jit(solution)/shard_map/all_gather | solution.py:1202
  20.5 22.1 %collective-permute-start.3 = (bf16[640,512]{1,0:T(8,128)(2,1)}, bf16[640,512]{1,0:T(8,128)(2,1)S(1)}, u32[]{:S(2)}, u32[]{:S(2)}) collective-permute-start(bf16[640,512]{1,0:T(8,128)(2,1)} %get-tuple-element.101), channel_id=1, source_target_pairs={{0,16},{16,0},{1,17},{17,1},{2,18},{18,2},{3,19},{19,3},{4,20},{20... | collective-permute-start | bytes 1966088 | tf_op jit(solution)/shard_map/ppermute | solution.py:1000
  33.4 12.0 %collective-permute-start.8 = (bf16[128,512]{1,0:T(8,128)(2,1)S(1)}, bf16[128,512]{1,0:T(8,128)(2,1)S(1)}, u32[]{:S(2)}, u32[]{:S(2)}) collective-permute-start(bf16[128,512]{1,0:T(8,128)(2,1)S(1)} %select_bitcast_fusion), channel_id=1, source_target_pairs={{0,16},{16,0},{1,17},{17,1},{2,18},{18,2},{3,19},{19,3},{4,20},{20... | collective-permute-start | bytes 393224 | tf_op jit(solution)/shard_map/ppermute | solution.py:1000
  46.1 10.1 %collective-permute-start.6 = (bf16[512,512]{1,0:T(8,128)(2,1)}, bf16[512,512]{1,0:T(8,128)(2,1)S(1)}, u32[]{:S(2)}, u32[]{:S(2)}) collective-permute-start(bf16[512,512]{1,0:T(8,128)(2,1)} %copy-done), channel_id=1, source_target_pairs={{0,2},{1,5},{2,0},{3,7},{4,6},{5,1},{6,4},{7,3},{8,10},{9,13},{10,... | collective-permute-start | bytes 1572872 | tf_op jit(solution)/shard_map/ppermute | solution.py:1000
  51.2 34.3 %collective-permute-start.9 = (bf16[1536,512]{1,0:T(8,128)(2,1)S(1)}, bf16[1536,512]{1,0:T(8,128)(2,1)}, u32[]{:S(2)}, u32[]{:S(2)}) collective-permute-start(bf16[1536,512]{1,0:T(8,128)(2,1)S(1)} %shard_map.237), channel_id=1, source_target_pairs={{0,16},{16,0},{1,17},{17,1},{2,18},{18,2},{3,19},{19,3},{4,20},{20... | collective-permute-start | bytes 4718600 | tf_op jit(solution)/shard_map/ppermute | solution.py:1000
  145.3 181.7 %collective-permute-start.11 = (bf16[1024,512]{1,0:T(8,128)(2,1)}, bf16[1024,512]{1,0:T(8,128)(2,1)}, u32[]{:S(2)}, u32[]{:S(2)}) collective-permute-start(bf16[1024,512]{1,0:T(8,128)(2,1)} %get-tuple-element.110), channel_id=1, source_target_pairs={{0,16},{16,0},{1,17},{17,1},{2,18},{18,2},{3,19},{19,3},{4,20},{20... | collective-permute-start | bytes 3145736 | tf_op jit(solution)/shard_map/ppermute | solution.py:1000
  147.3 23.4 %collective-permute-start.12 = (bf16[1,2560,512]{2,1,0:T(8,128)(2,1)}, bf16[1,2560,512]{2,1,0:T(8,128)(2,1)}, u32[]{:S(2)}, u32[]{:S(2)}) collective-permute-start(bf16[1,2560,512]{2,1,0:T(8,128)(2,1)} %bitcast.119), channel_id=1, source_target_pairs={{0,1},{1,0},{2,3},{3,2},{4,5},{5,4},{6,7},{7,6},{8,9},{9,8},{10,11... | collective-permute-start | bytes 7864328 | tf_op jit(solution)/shard_map/ppermute | solution.py:1000
  170.6 32.4 %collective-permute-start.14 = (bf16[1,1152,512]{2,1,0:T(8,128)(2,1)}, bf16[1,1152,512]{2,1,0:T(8,128)(2,1)}, u32[]{:S(2)}, u32[]{:S(2)}) collective-permute-start(bf16[1,1152,512]{2,1,0:T(8,128)(2,1)} %bitcast.121), channel_id=1, source_target_pairs={{0,1},{1,0},{2,3},{3,2},{4,5},{5,4},{6,7},{7,6},{8,9},{9,8},{10,11... | collective-permute-start | bytes 3538952 | tf_op jit(solution)/shard_map/ppermute | solution.py:1000
  177.0 26.0 %collective-permute-start.13 = (bf16[1,1280,512]{2,1,0:T(8,128)(2,1)}, bf16[1,1280,512]{2,1,0:T(8,128)(2,1)}, u32[]{:S(2)}, u32[]{:S(2)}) collective-permute-start(bf16[1,1280,512]{2,1,0:T(8,128)(2,1)} %get-tuple-element.128), channel_id=1, source_target_pairs={{0,2},{1,5},{2,0},{3,7},{4,6},{5,1},{6,4},{7,3},{8,10},{9,13},{10,... | collective-permute-start | bytes 3932168 | tf_op jit(solution)/shard_map/ppermute | solution.py:1000
  202.9 22.5 %collective-permute-start.15 = (bf16[1,2560,512]{2,1,0:T(8,128)(2,1)}, bf16[1,2560,512]{2,1,0:T(8,128)(2,1)S(1)}, u32[]{:S(2)}, u32[]{:S(2)}) collective-permute-start(bf16[1,2560,512]{2,1,0:T(8,128)(2,1)} %bitcast.118), channel_id=1, source_target_pairs={{0,1},{1,0},{2,3},{3,2},{4,5},{5,4},{6,7},{7,6},{8,9},{9,8},{10,11... | collective-permute-start | bytes 7864328 | tf_op jit(solution)/shard_map/ppermute | solution.py:1000
  208.7 52.2 %collective-permute-start.20 = (bf16[1,576,512]{2,1,0:T(8,128)(2,1)}, bf16[1,576,512]{2,1,0:T(8,128)(2,1)}, u32[]{:S(2)}, u32[]{:S(2)}) collective-permute-start(bf16[1,576,512]{2,1,0:T(8,128)(2,1)} %get-tuple-element.154), channel_id=1, source_target_pairs={{0,2},{1,5},{2,0},{3,7},{4,6},{5,1},{6,4},{7,3},{8,10},{9,13},{10,... | collective-permute-start | bytes 1769480 | tf_op jit(solution)/shard_map/ppermute | solution.py:1000
  209.6 15.8 %collective-permute-start.16 = (bf16[1,640,512]{2,1,0:T(8,128)(2,1)S(1)}, bf16[1,640,512]{2,1,0:T(8,128)(2,1)S(1)}, u32[]{:S(2)}, u32[]{:S(2)}) collective-permute-start(bf16[1,640,512]{2,1,0:T(8,128)(2,1)S(1)} %get-tuple-element.145), channel_id=1, source_target_pairs={{0,4},{1,3},{2,6},{3,1},{4,0},{5,7},{6,2},{7,5},{8,12},{9,11},{10,... | collective-permute-start | bytes 1966088 | tf_op jit(solution)/shard_map/ppermute | solution.py:1000
  230.7 31.1 %collective-permute-start.19 = (bf16[1,320,512]{2,1,0:T(8,128)(2,1)}, bf16[1,320,512]{2,1,0:T(8,128)(2,1)}, u32[]{:S(2)}, u32[]{:S(2)}) collective-permute-start(bf16[1,320,512]{2,1,0:T(8,128)(2,1)} %get-tuple-element.153), channel_id=1, source_target_pairs={{0,8},{1,9},{2,10},{3,11},{4,12},{5,13},{6,14},{7,15},{8,0},{9,1},... | collective-permute-start | bytes 983048 | tf_op jit(solution)/shard_map/ppermute | solution.py:1000
  238.1 23.7 %collective-permute-start.18 = (bf16[1,1280,512]{2,1,0:T(8,128)(2,1)}, bf16[1,1280,512]{2,1,0:T(8,128)(2,1)}, u32[]{:S(2)}, u32[]{:S(2)}) collective-permute-start(bf16[1,1280,512]{2,1,0:T(8,128)(2,1)} %get-tuple-element.152), channel_id=1, source_target_pairs={{0,2},{1,5},{2,0},{3,7},{4,6},{5,1},{6,4},{7,3},{8,10},{9,13},{10,... | collective-permute-start | bytes 3932168 | tf_op jit(solution)/shard_map/ppermute | solution.py:1000
  260.4 70.0 %collective-permute-start.29 = (bf16[1024,512]{1,0:T(8,128)(2,1)}, bf16[1024,512]{1,0:T(8,128)(2,1)}, u32[]{:S(2)}, u32[]{:S(2)}) collective-permute-start(bf16[1024,512]{1,0:T(8,128)(2,1)} %get-tuple-element.175), channel_id=1, source_target_pairs={{0,16},{16,0},{1,17},{17,1},{2,18},{18,2},{3,19},{19,3},{4,20},{20... | collective-permute-start | bytes 3145736 | tf_op jit(solution)/shard_map/ppermute | solution.py:1000
  263.6 13.6 %collective-permute-start.22 = (bf16[1,640,512]{2,1,0:T(8,128)(2,1)S(1)}, bf16[1,640,512]{2,1,0:T(8,128)(2,1)S(1)}, u32[]{:S(2)}, u32[]{:S(2)}) collective-permute-start(bf16[1,640,512]{2,1,0:T(8,128)(2,1)S(1)} %get-tuple-element.161), channel_id=1, source_target_pairs={{0,4},{1,3},{2,6},{3,1},{4,0},{5,7},{6,2},{7,5},{8,12},{9,11},{10,... | collective-permute-start | bytes 1966088 | tf_op jit(solution)/shard_map/ppermute | solution.py:1000
  266.1 15.0 %collective-permute-start.21 = (bf16[1,576,512]{2,1,0:T(8,128)(2,1)S(1)}, bf16[1,576,512]{2,1,0:T(8,128)(2,1)S(1)}, u32[]{:S(2)}, u32[]{:S(2)}) collective-permute-start(bf16[1,576,512]{2,1,0:T(8,128)(2,1)S(1)} %get-tuple-element.160), channel_id=1, source_target_pairs={{0,2},{1,5},{2,0},{3,7},{4,6},{5,1},{6,4},{7,3},{8,10},{9,13},{10,... | collective-permute-start | bytes 1769480 | tf_op jit(solution)/shard_map/ppermute | solution.py:1000
  277.9 16.3 %collective-permute-start.24 = (bf16[1,320,512]{2,1,0:T(8,128)(2,1)S(1)}, bf16[1,320,512]{2,1,0:T(8,128)(2,1)S(1)}, u32[]{:S(2)}, u32[]{:S(2)}) collective-permute-start(bf16[1,320,512]{2,1,0:T(8,128)(2,1)S(1)} %get-tuple-element.165), channel_id=1, source_target_pairs={{0,8},{1,9},{2,10},{3,11},{4,12},{5,13},{6,14},{7,15},{8,0},{9,1},... | collective-permute-start | bytes 983048 | tf_op jit(solution)/shard_map/ppermute | solution.py:1000
  282.5 14.1 %collective-permute-start.23 = (bf16[2,288,512]{2,1,0:T(8,128)(2,1)S(1)}, bf16[2,288,512]{2,1,0:T(8,128)(2,1)S(1)}, u32[]{:S(2)}, u32[]{:S(2)}) collective-permute-start(bf16[2,288,512]{2,1,0:T(8,128)(2,1)S(1)} %get-tuple-element.164), channel_id=1, source_target_pairs={{0,4},{1,3},{2,6},{3,1},{4,0},{5,7},{6,2},{7,5},{8,12},{9,11},{10,... | collective-permute-start | bytes 1769480 | tf_op jit(solution)/shard_map/ppermute | solution.py:1000
  297.3 21.1 %collective-permute-start.25 = (bf16[2,144,512]{2,1,0:T(8,128)(2,1)S(1)}, bf16[2,144,512]{2,1,0:T(8,128)(2,1)S(1)}, u32[]{:S(2)}, u32[]{:S(2)}) collective-permute-start(bf16[2,144,512]{2,1,0:T(8,128)(2,1)S(1)} %get-tuple-element.169), channel_id=1, source_target_pairs={{0,8},{1,9},{2,10},{3,11},{4,12},{5,13},{6,14},{7,15},{8,0},{9,1},... | collective-permute-start | bytes 884744 | tf_op jit(solution)/shard_map/ppermute | solution.py:1000
  302.1 23.3 %collective-permute-start.28 = (bf16[320,512]{1,0:T(8,128)(2,1)S(1)}, bf16[320,512]{1,0:T(8,128)(2,1)S(1)}, u32[]{:S(2)}, u32[]{:S(2)}) collective-permute-start(bf16[320,512]{1,0:T(8,128)(2,1)S(1)} %shard_map.259.refs_3_.refs_1_), channel_id=1, source_target_pairs={{0,8},{1,9},{2,10},{3,11},{4,12},{5,13},{6,14},{7,15},{8,0},{9,1},... | collective-permute-start | bytes 983048 | tf_op jit(solution)/shard_map/ppermute | solution.py:1000
  326.9 10.3 %collective-permute-start.30 = (bf16[144,512]{1,0:T(8,128)(2,1)S(1)}, bf16[144,512]{1,0:T(8,128)(2,1)S(1)}, u32[]{:S(2)}, u32[]{:S(2)}) collective-permute-start(bf16[144,512]{1,0:T(8,128)(2,1)S(1)} %shard_map.262.refs_2_.refs_3_.refs_1_), channel_id=1, source_target_pairs={{0,8},{1,9},{2,10},{3,11},{4,12},{5,13},{6,14},{7,15},{8,0},{9,1},... | collective-permute-start | bytes 442376 | tf_op jit(solution)/shard_map/ppermute | solution.py:1000
  336.5 19.4 %collective-permute-start.33 = (bf16[1280,512]{1,0:T(8,128)(2,1)S(1)}, bf16[1280,512]{1,0:T(8,128)(2,1)S(1)}, u32[]{:S(2)}, u32[]{:S(2)}) collective-permute-start(bf16[1280,512]{1,0:T(8,128)(2,1)S(1)} %shard_map.265.refs_3_.refs_1_), channel_id=1, source_target_pairs={{0,2},{1,5},{2,0},{3,7},{4,6},{5,1},{6,4},{7,3},{8,10},{9,13},{10,... | collective-permute-start | bytes 3932168 | tf_op jit(solution)/shard_map/ppermute | solution.py:1000
  356.6 15.4 %collective-permute-start.35 = (bf16[2560,512]{1,0:T(8,128)(2,1)S(1)}, bf16[2560,512]{1,0:T(8,128)(2,1)S(1)}, u32[]{:S(2)}, u32[]{:S(2)}) collective-permute-start(bf16[2560,512]{1,0:T(8,128)(2,1)S(1)} %shard_map.267.refs_3_.refs_1_), channel_id=1, source_target_pairs={{0,1},{1,0},{2,3},{3,2},{4,5},{5,4},{6,7},{7,6},{8,9},{9,8},{10,11... | collective-permute-start | bytes 7864328 | tf_op jit(solution)/shard_map/ppermute | solution.py:1000
  (78 other events, 740.4 us)
Sparse Core Ops, SparseCore 0:
  46.2 45.5 all-gather.2

commit v4 on v3

--- a/solution.py
+++ b/solution.py
@@ -98,6 +98,13 @@
 
 
 LEAVING = {}
+WAITING = []
+
+
+def arrive():
+    for copy in WAITING:
+        copy.start()
+    WAITING.clear()
 
 
 def leave(*refs):
@@ -142,7 +149,7 @@
 LARGE = 256 << 10
 
 
-def kernel_call(body, outs, operands, scalars=0, scratch=(), out_specs=None, flops=0, after=(), direct=False, weight=20, room_for=52):
+def kernel_call(body, outs, operands, scalars=0, scratch=(), out_specs=None, flops=0, after=(), direct=False, weight=20, room_for=52, hold=False):
     size = sum(bytes_of(x) for x in (*operands, *outs))
     held = size + (sum(bytes_of(x) for x in scratch) if direct else 0)
     count, many, extra = len(operands), len(outs), len(scratch)
@@ -164,9 +171,11 @@
         for i, c in enumerate(comes):
             if c:
                 copy = pltpu.make_async_copy(ins[i], buffers[slot], rest[-1].at[slot])
-                copy.start()
+                WAITING.append(copy)
                 ins[i] = Held(buffers[slot], copy)
                 slot += 1
+        if not hold:
+            arrive()
         LEAVING.clear()
         for i, g in enumerate(goes):
             if g:
@@ -175,6 +184,7 @@
                 LEAVING[id(results[i])] = (copy, False)
                 slot += 1
         body(*ins, *results, *own)
+        assert not WAITING
         for value in ins:
             ready(value)
         for i, g in enumerate(goes):
@@ -254,14 +264,15 @@
         return carry
 
     lax.fori_loop(0, count + 1, window, 0)
-    table[0, 2 + count] = 0
-    bias[count + 1] = jnp.full((WIN, WIN), NEG, F32)
+    for extra in range(1, WIDE_GROUP):
+        table[0, 1 + count + extra] = 0
+        bias[count + extra] = jnp.full((WIN, WIN), NEG, F32)
 
 
 def row_layout(flags, lengths, hamming, priority, copies):
     outs = (
         shaped(1, 128, jnp.int32),
-        jax.ShapeDtypeStruct((SENTS + 1, WIN, WIN), F32),
+        jax.ShapeDtypeStruct((WINDOWS, WIN, WIN), F32),
         shaped(T, WIN, F32),
         shaped(T, WIN, jnp.int32),
     )
@@ -292,14 +303,16 @@
 
 PAIRS = [slice(i * 128, i * 128 + 128) for i in range(HEADS // 2)]
 GROUP = 2
-
-
-def grouped(table, body):
+WIDE_GROUP = 4
+WINDOWS = SENTS + WIDE_GROUP - 1
+
+
+def grouped(table, body, many=GROUP):
     def step(index, carry):
-        body([index * GROUP + i for i in range(GROUP)])
+        body([index * many + i for i in range(many)])
         return carry
 
-    lax.fori_loop(0, (table[0, 0] + GROUP - 1) // GROUP, step, 0)
+    lax.fori_loop(0, (table[0, 0] + many - 1) // many, step, 0)
 
 
 def spread(table, windows):
@@ -336,7 +349,7 @@
             stats[w * 4 + pair, 1:2, :] = i
 
     mixed[...] = jnp.zeros_like(mixed)
-    grouped(table, body)
+    grouped(table, body, WIDE_GROUP)
 
 
 def attend_back(table, bias, queries, keys, values, stats, grad, grad_q, grad_k, grad_v):
@@ -368,7 +381,7 @@
     grouped(table, body)
 
 
-STATS = jax.ShapeDtypeStruct(((SENTS + 1) * 4, 2, 2 * WIN), F32)
+STATS = jax.ShapeDtypeStruct((WINDOWS * 4, 2, 2 * WIN), F32)
 
 
 def thirds(ref):
@@ -572,6 +585,7 @@
 ):
     own = (own_cross, own_expand, own_contract, rest, half, last_half)
     cross, _, contract = fetch_rest(0, flags, *own, cross, None, contract, sems)
+    arrive()
     bias_grads[...] = jnp.zeros_like(bias_grads)
 
     def block(at):
@@ -620,6 +634,7 @@
         ],
         flops=18 * FLOP_UNIT,
         after=after,
+        hold=True,
     )
 
 
@@ -630,6 +645,7 @@
 ):
     own = (own_cross, own_expand, own_contract, rest, half, last_half)
     _, expand, _ = fetch_rest(0, flags, *own, None, expand, None, sems)
+    arrive()
     bias_grads[...] = jnp.zeros_like(bias_grads)
 
     def last(at):
@@ -651,6 +667,7 @@
         scratch=[pltpu.VMEM((D, FF), BF), pltpu.SemaphoreType.DMA((3,))],
         flops=4 * FLOP_UNIT,
         after=after,
+        hold=True,
     )
 
 
@@ -734,6 +751,7 @@
     weight_in, weight_out, acc, dzb, out, djoined, dcopied, sems,
 ):
     weight_in, weight_out = fetch_self(1, flags, own_in, own_out, half, rest, weight_in, weight_out, sems)
+    arrive()
     self_back(table, bias, flags, dz, x, joined, mixed, stats, weight_in, weight_out, kept, sent, acc, dzb, out, djoined)
     put_small(
         flags, kept, sent,
@@ -783,6 +801,7 @@
         ],
         flops=18 * FLOP_UNIT,
         after=after,
+        hold=True,
     )
 
 
@@ -802,6 +821,7 @@
 
     source = Landing(source, sems.at[2])
     weight_in, weight_out = fetch_self(0, flags, own_in, own_out, half, rest, weight_in, weight_out, sems)
+    arrive()
 
     def first(at):
         unit, _ = normalized(source[at, :].astype(F32))
@@ -845,6 +865,7 @@
         ],
         flops=18 * FLOP_UNIT,
         after=after,
+        hold=True,
     )
 
 
@@ -883,7 +904,7 @@
             copies += [(rest.at[rows_at(j * D), :], cross.at[:, rows_at(j * D)], 0) for j in range(2)]
         start(*((source, target, sems.at[i]) for source, target, i in copies))
 
-    pairs = ((own_expand, expand, 1), (own_contract, contract, 2), (own_cross, cross, 0))
+    pairs = ((own_cross, cross, 0), (own_expand, expand, 1), (own_contract, contract, 2))
     pl.when(own)(lambda: start(*((source, target, sems.at[i]) for source, target, i in pairs if target is not None)))
     pl.when(jnp.logical_not(own) & (flags[0, 1] == 0))(lambda: other(half, last))
     pl.when(jnp.logical_not(own) & (flags[0, 1] != 0))(lambda: other(last, half))
@@ -916,6 +937,7 @@
 ):
     source, target = fetch_rows(flags, rows, (got_0, got_1), source, target, sems.at[pl.ds(0, 2)])
     e_in, e_out = fetch_self(0, flags, own_in, own_out, half, rest, e_in, e_out, sems.at[pl.ds(2, 2)])
+    arrive()
     d_in, d_out = fetch_self(1, flags, own_in, own_out, half, rest, d_in, d_out, sems.at[pl.ds(4, 2)])
 
     @pl.when(flags[0, 0] == 0)
@@ -948,6 +970,7 @@
         ],
         flops=24 * FLOP_UNIT,
         weight=0,
+        hold=True,
     )
 
 
@@ -959,6 +982,7 @@
 ):
     own = (own_cross, own_expand, own_contract, rest, half, last)
     e_cross, e_expand, e_contract = fetch_rest(0, flags, *own, e_cross, e_expand, e_contract, sems.at[pl.ds(0, 3)])
+    arrive()
     d_cross, d_expand, d_contract = fetch_rest(1, flags, *own, d_cross, d_expand, d_contract, sems.at[pl.ds(3, 3)])
     encoder_ff_kernel(flags, e_z1, e_expand, e_contract, e_cross, e_small, hidden, e_z2, mine, theirs, states, active)
     decoder_cross_kernel(table, bias, d_z1, states, d_cross, d_small, queries, mixed, stats, d_z2, wide)
@@ -992,6 +1016,7 @@
         ],
         flops=54 * FLOP_UNIT,
         room_for=62,
+        hold=True,
     )
 
 
@@ -1054,8 +1079,20 @@
         keep[...], send[...] = sums[1], sums[0]
 
 
-def add_kernel(first, second, out):
-    out[...] = added(first[...], second[...])
+def add_kernel(*refs):
+    total = refs[0][...].astype(F32)
+    for ref in refs[1:-1]:
+        total = total + ref[...].astype(F32)
+    refs[-1][...] = total.astype(BF)
+
+
+def corner_kernel(step, flags, kept, got, *outs):
+    half = kept.shape[1] // 2
+    side, bit = flags[0, 0], flags[0, 1 + step]
+    quarters = ((side, bit), (side, 1 - bit), (1 - side, bit), (1 - side, 1 - bit))
+    for out, (layer, part) in zip(outs, quarters):
+        at = (pl.ds(layer, 1), pl.ds(pl.multiple_of(part * half, 16), half), slice(None))
+        out[...] = added(kept[at], got[at])[0]
 
 
 class Steps:
@@ -1100,15 +1137,26 @@
             parts.append(value)
         return parts
 
-    def doubled(self, pairs, after, spill, outs):
+    def crossed(self, pairs, after):
         shape = shaped(*pairs[0][0].shape[1:], BF)
         operands = [x for pair in pairs for x in pair]
         kept, sent = kernel_call(
             functools.partial(across_kernel, len(pairs)), (shape, shape), (self.flags, *operands), scalars=1, after=after, direct=True
         )
-        got = swapped_pipe(sent)
-        after = yield kept
-        (value,) = kernel_call(add_kernel, (shape,), (kept, got), after=after, direct=True)
+        return kept, swapped_pipe(sent)
+
+    def cornered(self, kept, got, after):
+        shape = shaped(kept.shape[1] // 2, D, BF)
+        own, *sent = kernel_call(
+            functools.partial(corner_kernel, self.last), (shape,) * 4, (self.flags, kept, got), scalars=1, after=after, direct=True
+        )
+        partner = self.partners[self.last]
+        pairs = [(p * self.count + i, (1 - p) * self.count + partner(i)) for p in range(2) for i in range(self.count)]
+        return own, self.swap(sent[0], self.last), swapped_pipe(sent[1]), lax.ppermute(sent[2], ("pipe", "dp"), pairs)
+
+    def doubled(self, parts, spill, outs):
+        after = yield parts[0]
+        (value,) = kernel_call(add_kernel, (shaped(*parts[0].shape, BF),), parts, after=after, direct=True)
         for step in range(self.last, 0, -1):
             got = self.swap(value, step)
             after = yield value
@@ -1192,13 +1240,13 @@
     self_piece = swapped_pipe(self_piece)
     small_other = swapped_pipe(small)
     theirs = [lax.dynamic_slice_in_dim(rows, (1 - pipe) * T + at, size, 0) for at, size in PARTS]
-    got = [swapped_pipe(part) for part in gate(theirs, (self_piece, small_other))]
-    self_parts = steps.half_gathered(self_piece, ((bias,), (got[1],), (got[0],)))
+    got = [swapped_pipe(part) for part in gate(theirs, (self_piece,))]
+    self_parts = steps.half_gathered(self_piece, ((), (got[1], bias), (got[0],)))
     self_half = self_parts[-1]
     self_rest = steps.swap(self_half, 0)
-    (last_piece,) = kernel_call(last_kernel, (shaped(3 * D, D, BF),), (flags, expand, contract), scalars=1, after=(self_parts[-2],), direct=True, weight=0)
+    (last_piece,) = kernel_call(last_kernel, (shaped(3 * D, D, BF),), (flags, expand, contract), scalars=1, after=(self_parts[-2], small_other), direct=True, weight=0)
     last_half = swapped_pipe(last_piece)
-    (rest_piece,) = gate((swapped_pipe(rest_piece),), (self_parts[-2],))
+    (rest_piece,) = gate((swapped_pipe(rest_piece),), (self_parts[0],))
     rest = lax.all_gather(rest_piece, "dp").reshape(4 * D, D)
 
     self_weights = (self_in, self_out, self_half, self_rest)
@@ -1268,19 +1316,19 @@
                 dec_pair = (kept, steps.swap(sent, step + 3))
             after = yield kept
         outs = (shaped(D, FF, F32), shaped(FF, D, F32), shaped(D, 2 * D, F32))
-        yield from steps.doubled((enc_pair, dec_pair), after, spill_ff_kernel, outs)
+        yield from steps.doubled(steps.crossed((enc_pair, dec_pair), after), spill_ff_kernel, outs)
 
     def self_sum():
         pairs = [(self_kept, self_got)]
         after = yield
-        for step in range(steps.last):
+        for step in range(steps.last - 1):
             kept, sent = steps.halve(step, *pairs, after=after)
             pairs = [(kept, steps.swap(sent, step + 1))]
             if step == 0:
                 pairs.append((dself_kept, dself_got))
             after = yield kept
         outs = (shaped(D, 3 * D, F32), shaped(D, D, F32), shaped(1, FF, F32)) + (shaped(3, D, F32),) * 3
-        yield from steps.doubled(pairs, after, spill_rest_kernel, outs)
+        yield from steps.doubled(steps.cornered(*pairs[0], after), spill_rest_kernel, outs)
 
     chains = [ff_sum(), self_sum()]
     results = [None, None]

time: 407 us -> 391 us (0.961)
  Pallas kernels: 185 us -> 178 us
  starting transfers between devices: 52 us -> 46.5 us
    ppermute x37, waiting for transfers between devices: 102 us -> 88.1 us  [swapped(): return lax.ppermute(value, axis, [(i, partner(i)) for i in range(count)])]
    ppermute x0 -> x1, waiting for transfers between devices: none -> 12.9 us  [cornered(): lax.ppermute(sent[2], ('pipe', 'dp'), pairs)]
    pallas_call x33 -> x32, Pallas kernels: 185 us -> 178 us  [kernel_call(): pl.pallas_call(run, out_shape=tuple(outs), in_specs=in_specs, out_specs=t...]
    ppermute x37, starting transfers between devices: 52 us -> 46.4 us  [swapped(): return lax.ppermute(value, axis, [(i, partner(i)) for i in range(count)])]
    unnamed x134 -> x136, local copies, waits for them, and re-layouts: 28.5 us -> 26.8 us
  transfers between devices with their start and end apart: 38 -> 39, of which waited for: 20 -> 20; matrix products, arithmetic and copies ran while one was open for 4% -> 4% of each run, Pallas kernels for 32% -> 32%
where the time goes in v4:
time: 391 us; the launch traced here: 384 us
  Pallas kernels  178 us (46%)
  waiting for transfers between devices  101 us (26%)
  starting transfers between devices  46.5 us (12%)
  local copies, waits for them, and re-layouts  30.7 us (8%)
  between operations  15 us (4%)
  other arithmetic  12.2 us (3%)
    pallas_call x32, Pallas kernels, kernel_call(): pl.pallas_call(run, out_shape=tuple(outs), in_specs=in_specs, out_specs=t...  178 us
    ppermute x37, waiting for transfers between devices, swapped(): return lax.ppermute(value, axis, [(i, partner(i)) for i in range(count)])  88.1 us
    ppermute x37, starting transfers between devices, swapped(): return lax.ppermute(value, axis, [(i, partner(i)) for i in range(count)])  46.4 us
    unnamed x136, local copies, waits for them, and re-layouts  26.8 us
    ppermute x1, waiting for transfers between devices, cornered(): lax.ppermute(sent[2], ('pipe', 'dp'), pairs)  12.9 us
  transfers between devices with their start and end apart: 39, of which 20 were waited for; matrix products, arithmetic and copies ran while one was open for 4% of the time, Pallas kernels for 32%

profile of v4, /device:TPU:1, one launch (start us, length us, event | category | flops | bytes accessed | tf_op | source)
XLA Modules:
  0.0 383.5 jit_solution(5814029906435345384)
XLA Ops:
  32.6 3.1 shard_map.230
  35.7 6.4 %collective-permute-done.2.refs_3_.refs_4_.refs_5_ = bf16[640,512]{1,0:T(8,128)(2,1)S(1)} collective-permute-done((bf16[640,512]{1,0:T(8,128)(2,1)}, bf16[640,512]{1,0:T(8,128)(2,1)S(1)}, u32[]{:S(2)}, u32[]{:S(2)}) %collective-permute-start.2) | collective-permute-done | bytes 655392 | tf_op jit(solution)/shard_map/ppermute | solution.py:1025
  49.2 5.4 %collective-permute-done.5.refs_2_ = bf16[512,512]{1,0:T(8,128)(2,1)S(1)} collective-permute-done((bf16[512,512]{1,0:T(8,128)(2,1)S(1)}, bf16[512,512]{1,0:T(8,128)(2,1)S(1)}, u32[]{:S(2)}, u32[]{:S(2)}) %collective-permute-start.5) | collective-permute-done | bytes 524320 | tf_op jit(solution)/shard_map/ppermute | solution.py:1025
  61.1 18.8 %shard_map.235 = (f32[16,512]{1,0:T(8,128)S(1)}, f32[16,512]{1,0:T(8,128)S(1)}, bf16[1024,1536]{1,0:T(8,128)(2,1)}, bf16[1024,512]{1,0:T(8,128)(2,1)}, f32[80,2,...) custom-call(s32[1,128]{1,0:T(1,128)S(1)} %get-tuple-element.99.refs_, ...), custom_call_target="tpu_custom_call" | custom-call | tf_op jit(solution)/shard_map/pallas_call | solution.py:198
  81.1 5.0 %collective-permute-start.10 = (bf16[1536,512]{1,0:T(8,128)(2,1)}, bf16[1536,512]{1,0:T(8,128)(2,1)S(1)}, u32[]{:S(2)}, u32[]{:S(2)}) collective-permute-start(bf16[1536,512]{1,0:T(8,128)(2,1)} %shard_map.238.refs_7_.refs_9_.refs_8_), channel_id=1, source_target_pairs={{0,1},{1,0},{2,3},{3,2},{4,5},{5,4},{6,7},{7,6},{8,9},{9,8},{10,11... | collective-permute-start | bytes 4718600 | tf_op jit(solution)/shard_map/ppermute | solution.py:1025
  86.1 3.2 collective-permute-done.10.refs_8_.refs_10_.refs_9_
  90.6 51.5 %shard_map.239 = (bf16[1024,2048]{1,0:T(8,128)(2,1)}, f32[1024,512]{1,0:T(8,128)}, bf16[1024,512]{1,0:T(8,128)(2,1)}, bf16[1024,512]{1,0:T(8,128)(2,1)}, bf16[25...) custom-call(s32[1,128]{1,0:T(1,128)} %copy-done.33, ...), custom_call_target="tpu_custom_call" | custom-call | flops 579820584960 | bytes 720578944 | tf_op jit(solution)/shard_map/pallas_call | solution.py:198
  145.9 19.4 %shard_map.240 = (bf16[1152,512]{1,0:T(8,128)(2,1)}, bf16[1152,512]{1,0:T(8,128)(2,1)}, bf16[1024,512]{1,0:T(8,128)(2,1)}, bf16[1024,512]{1,0:T(8,128)(2,1)}) custom-call(s32[1,128]{1,0:T(1,128)S(1)} %copy-done.34, s32[1,5]{1,0:T(1,128)S(1)} %bitcast.78, f32[1024,512]{1,0:T(8,128)} %get-tuple-element.116.refs_2_, bf16[512,1536]{1,0:T(8,128)(2,1)} %bitcast.114, ...), custom_call_target="tpu_custom_call" | custom-call | flops 193273528320 | bytes 371272064 | tf_op jit(solution)/shard_map/pallas_call | solution.py:198
  167.5 3.4 shard_map.242
  172.0 3.7 collective-permute-start.13
  175.7 24.1 %shard_map.243 = (bf16[2560,512]{1,0:T(8,128)(2,1)}, bf16[2560,512]{1,0:T(8,128)(2,1)}, f32[8,512]{1,0:T(8,128)S(1)}, f32[8,512]{1,0:T(8,128)S(1)}, bf16[1024,2048]{1,0:T(8,128)(2,1)}, /*index=5*/f32[1024,512]{1,0:T(8,128)}) custom-call(s32[1,5]{1,0:T(1,128)S(1)} %bitcast.80, f32[1024,512]{1,0:T(8,128)} %get-tuple-element.111.refs_1_, ...), custom_call_target="tpu_custom_call" | custom-call | flops 193273528320 | bytes 651428224 | tf_op jit(solution)/shard_map/pallas_call | solution.py:198
  202.9 2.6 shard_map.246
  207.2 8.9 %shard_map.247 = (f32[8,512]{1,0:T(8,128)S(1)}, f32[1024,512]{1,0:T(8,128)}) custom-call(s32[1,5]{1,0:T(1,128)S(1)} %bitcast.83, bf16[1024,2048]{1,0:T(8,128)(2,1)} %get-tuple-element.126.refs_1_, f32[1024,512]{1,0:T(8,128)} %get-tuple-element.127.refs_2_, f32[1024,512]{1,0:T(8,128)} %get-tuple-element.105.refs_2_.refs_3_, bf16[512,1024]{1,0:T(8,128)(2,1)} %bitcast.69, ...), custom_call_target="tpu_custom_call" | custom-call | flops 42949672960 | bytes 420413824 | tf_op jit(solution)/shard_map/pallas_call | solution.py:198
  216.1 5.7 %collective-permute-done.16.refs_1_ = bf16[1,640,512]{2,1,0:T(8,128)(2,1)S(1)} collective-permute-done((bf16[1,640,512]{2,1,0:T(8,128)(2,1)S(1)}, bf16[1,640,512]{2,1,0:T(8,128)(2,1)S(1)}, u32[]{:S(2)}, u32[]{:S(2)}) %collective-permute-start.16) | collective-permute-done | bytes 655392 | tf_op jit(solution)/shard_map/ppermute | solution.py:1025
  232.6 20.2 %shard_map.251 = (bf16[1152,512]{1,0:T(8,128)(2,1)}, bf16[1152,512]{1,0:T(8,128)(2,1)}, bf16[1024,512]{1,0:T(8,128)(2,1)}, bf16[1024,512]{1,0:T(8,128)(2,1)}) custom-call(s32[1,128]{1,0:T(1,128)S(1)} %copy-done.35, s32[1,5]{1,0:T(1,128)S(1)} %bitcast.86, f32[1024,512]{1,0:T(8,128)} %get-tuple-element.135.refs_2_, bf16[2048,512]{1,0:T(8,128)(2,1)} %bitcast.112, ...), custom_call_target="tpu_custom_call" | custom-call | flops 193273528320 | bytes 434841984 | tf_op jit(solution)/shard_map/pallas_call | solution.py:198
  260.5 12.2 %collective-permute-done.22.refs_2_ = bf16[1,640,512]{2,1,0:T(8,128)(2,1)S(1)} collective-permute-done((bf16[1,640,512]{2,1,0:T(8,128)(2,1)S(1)}, bf16[1,640,512]{2,1,0:T(8,128)(2,1)S(1)}, u32[]{:S(2)}, u32[]{:S(2)}) %collective-permute-start.22) | collective-permute-done | bytes 655392 | tf_op jit(solution)/shard_map/ppermute | solution.py:1025
  276.6 13.6 %collective-permute-done.24.refs_2_ = bf16[1,320,512]{2,1,0:T(8,128)(2,1)S(1)} collective-permute-done((bf16[1,320,512]{2,1,0:T(8,128)(2,1)S(1)}, bf16[1,320,512]{2,1,0:T(8,128)(2,1)S(1)}, u32[]{:S(2)}, u32[]{:S(2)}) %collective-permute-start.24) | collective-permute-done | bytes 327712 | tf_op jit(solution)/shard_map/ppermute | solution.py:1025
  293.9 6.4 %collective-permute-done.28.refs_1_ = bf16[320,512]{1,0:T(8,128)(2,1)S(1)} collective-permute-done((bf16[320,512]{1,0:T(8,128)(2,1)S(1)}, bf16[320,512]{1,0:T(8,128)(2,1)S(1)}, u32[]{:S(2)}, u32[]{:S(2)}) %collective-permute-start.28) | collective-permute-done | bytes 327712 | tf_op jit(solution)/shard_map/ppermute | solution.py:1025
  303.4 12.9 %collective-permute-done.27.refs_3_ = bf16[144,512]{1,0:T(8,128)(2,1)S(1)} collective-permute-done((bf16[144,512]{1,0:T(8,128)(2,1)S(1)}, bf16[144,512]{1,0:T(8,128)(2,1)S(1)}, u32[]{:S(2)}, u32[]{:S(2)}) %collective-permute-start.27) | collective-permute-done | bytes 147488 | tf_op jit(solution)/shard_map/ppermute | solution.py:1155
  316.5 8.6 %collective-permute-done.30.refs_2_ = bf16[320,512]{1,0:T(8,128)(2,1)S(1)} collective-permute-done((bf16[320,512]{1,0:T(8,128)(2,1)S(1)}, bf16[320,512]{1,0:T(8,128)(2,1)S(1)}, u32[]{:S(2)}, u32[]{:S(2)}) %collective-permute-start.30) | collective-permute-done | bytes 327712 | tf_op jit(solution)/shard_map/ppermute | solution.py:1025
  330.3 2.8 bitcast_convert_fusion.2
  340.4 14.6 %collective-permute-done.35.refs_2_ = bf16[1280,512]{1,0:T(8,128)(2,1)S(1)} collective-permute-done((bf16[1280,512]{1,0:T(8,128)(2,1)S(1)}, bf16[1280,512]{1,0:T(8,128)(2,1)S(1)}, u32[]{:S(2)}, u32[]{:S(2)}) %collective-permute-start.35) | collective-permute-done | bytes 1310752 | tf_op jit(solution)/shard_map/ppermute | solution.py:1025
  364.4 5.2 %shard_map.269 = (f32[512,2048]{1,0:T(8,128)}, f32[2048,512]{1,0:T(8,128)}, f32[512,1024]{1,0:T(8,128)}) custom-call(s32[1,5]{1,0:T(1,128)S(1)} %bitcast.99, bf16[2560,512]{1,0:T(8,128)(2,1)S(1)} %shard_map.267.refs_3_.refs_1_, bf16[2560,512]{1,0:T(8,128)(2,1)S(1)} %collective-permute-done.37.refs_2_, bf16[1152,512]{1,0:T(8,128)(2,1)S(1)} %shard_map.268.refs_3_.refs_1_, ...), custom_call_target="tpu_custom_call" | custom-call | flops 21474836480 | bytes 314573184 | tf_op jit(solution)/shard_map/pallas_call | solution.py:198
  371.8 2.8 shard_map.270
  (246 shorter events, 107.9 us)
Async XLA Ops:
  7.2 82.2 %all-gather.3.cloned.1.call-start = ((), (), s32[]{:S(2)}) async-start(), calls=%async_computation | async-start | bytes 2228224 | tf_op jit(solution)/shard_map/all_gather | solution.py:1250
  28.4 13.7 %collective-permute-start.2 = (bf16[640,512]{1,0:T(8,128)(2,1)}, bf16[640,512]{1,0:T(8,128)(2,1)S(1)}, u32[]{:S(2)}, u32[]{:S(2)}) collective-permute-start(bf16[640,512]{1,0:T(8,128)(2,1)} %get-tuple-element.101), channel_id=1, source_target_pairs={{0,16},{16,0},{1,17},{17,1},{2,18},{18,2},{3,19},{19,3},{4,20},{20... | collective-permute-start | bytes 1966088 | tf_op jit(solution)/shard_map/ppermute | solution.py:1025
  31.0 14.2 %collective-permute-start.7 = (f32[13,512]{1,0:T(8,128)S(1)}, f32[13,512]{1,0:T(8,128)S(1)}, u32[]{:S(2)}, u32[]{:S(2)}) collective-permute-start(f32[13,512]{1,0:T(8,128)S(1)} %pad_maximum_fusion.refs_12_), channel_id=1, source_target_pairs={{0,16},{16,0},{1,17},{17,1},{2,18},{18,2},{3,19},{19,3},{4,20},{20... | collective-permute-start | bytes 79880 | tf_op jit(solution)/shard_map/ppermute | solution.py:1025
  49.2 32.0 %collective-permute-start.9 = (bf16[1536,512]{1,0:T(8,128)(2,1)S(1)}, bf16[1536,512]{1,0:T(8,128)(2,1)}, u32[]{:S(2)}, u32[]{:S(2)}) collective-permute-start(bf16[1536,512]{1,0:T(8,128)(2,1)S(1)} %shard_map.237), channel_id=1, source_target_pairs={{0,16},{16,0},{1,17},{17,1},{2,18},{18,2},{3,19},{19,3},{4,20},{20... | collective-permute-start | bytes 4718600 | tf_op jit(solution)/shard_map/ppermute | solution.py:1025
  142.1 188.2 %collective-permute-start.11 = (bf16[1024,512]{1,0:T(8,128)(2,1)}, bf16[1024,512]{1,0:T(8,128)(2,1)}, u32[]{:S(2)}, u32[]{:S(2)}) collective-permute-start(bf16[1024,512]{1,0:T(8,128)(2,1)} %get-tuple-element.110), channel_id=1, source_target_pairs={{0,16},{16,0},{1,17},{17,1},{2,18},{18,2},{3,19},{19,3},{4,20},{20... | collective-permute-start | bytes 3145736 | tf_op jit(solution)/shard_map/ppermute | solution.py:1025
  143.1 22.6 %collective-permute-start.12 = (bf16[1,2560,512]{2,1,0:T(8,128)(2,1)}, bf16[1,2560,512]{2,1,0:T(8,128)(2,1)}, u32[]{:S(2)}, u32[]{:S(2)}) collective-permute-start(bf16[1,2560,512]{2,1,0:T(8,128)(2,1)} %bitcast.118), channel_id=1, source_target_pairs={{0,1},{1,0},{2,3},{3,2},{4,5},{5,4},{6,7},{7,6},{8,9},{9,8},{10,11... | collective-permute-start | bytes 7864328 | tf_op jit(solution)/shard_map/ppermute | solution.py:1025
  165.4 34.5 %collective-permute-start.14 = (bf16[1,1152,512]{2,1,0:T(8,128)(2,1)}, bf16[1,1152,512]{2,1,0:T(8,128)(2,1)}, u32[]{:S(2)}, u32[]{:S(2)}) collective-permute-start(bf16[1,1152,512]{2,1,0:T(8,128)(2,1)} %bitcast.120), channel_id=1, source_target_pairs={{0,1},{1,0},{2,3},{3,2},{4,5},{5,4},{6,7},{7,6},{8,9},{9,8},{10,11... | collective-permute-start | bytes 3538952 | tf_op jit(solution)/shard_map/ppermute | solution.py:1025
  172.0 27.9 %collective-permute-start.13 = (bf16[1,1280,512]{2,1,0:T(8,128)(2,1)}, bf16[1,1280,512]{2,1,0:T(8,128)(2,1)}, u32[]{:S(2)}, u32[]{:S(2)}) collective-permute-start(bf16[1,1280,512]{2,1,0:T(8,128)(2,1)} %get-tuple-element.128), channel_id=1, source_target_pairs={{0,2},{1,5},{2,0},{3,7},{4,6},{5,1},{6,4},{7,3},{8,10},{9,13},{10,... | collective-permute-start | bytes 3932168 | tf_op jit(solution)/shard_map/ppermute | solution.py:1025
  199.7 22.0 %collective-permute-start.15 = (bf16[1,2560,512]{2,1,0:T(8,128)(2,1)}, bf16[1,2560,512]{2,1,0:T(8,128)(2,1)S(1)}, u32[]{:S(2)}, u32[]{:S(2)}) collective-permute-start(bf16[1,2560,512]{2,1,0:T(8,128)(2,1)} %bitcast.117), channel_id=1, source_target_pairs={{0,1},{1,0},{2,3},{3,2},{4,5},{5,4},{6,7},{7,6},{8,9},{9,8},{10,11... | collective-permute-start | bytes 7864328 | tf_op jit(solution)/shard_map/ppermute | solution.py:1025
  205.5 49.3 %collective-permute-start.20 = (bf16[1,576,512]{2,1,0:T(8,128)(2,1)}, bf16[1,576,512]{2,1,0:T(8,128)(2,1)}, u32[]{:S(2)}, u32[]{:S(2)}) collective-permute-start(bf16[1,576,512]{2,1,0:T(8,128)(2,1)} %get-tuple-element.154), channel_id=1, source_target_pairs={{0,2},{1,5},{2,0},{3,7},{4,6},{5,1},{6,4},{7,3},{8,10},{9,13},{10,... | collective-permute-start | bytes 1769480 | tf_op jit(solution)/shard_map/ppermute | solution.py:1025
  205.7 16.1 %collective-permute-start.16 = (bf16[1,640,512]{2,1,0:T(8,128)(2,1)S(1)}, bf16[1,640,512]{2,1,0:T(8,128)(2,1)S(1)}, u32[]{:S(2)}, u32[]{:S(2)}) collective-permute-start(bf16[1,640,512]{2,1,0:T(8,128)(2,1)S(1)} %get-tuple-element.145), channel_id=1, source_target_pairs={{0,4},{1,3},{2,6},{3,1},{4,0},{5,7},{6,2},{7,5},{8,12},{9,11},{10,... | collective-permute-start | bytes 1966088 | tf_op jit(solution)/shard_map/ppermute | solution.py:1025
  227.0 29.6 %collective-permute-start.19 = (bf16[1,320,512]{2,1,0:T(8,128)(2,1)}, bf16[1,320,512]{2,1,0:T(8,128)(2,1)}, u32[]{:S(2)}, u32[]{:S(2)}) collective-permute-start(bf16[1,320,512]{2,1,0:T(8,128)(2,1)} %get-tuple-element.153), channel_id=1, source_target_pairs={{0,8},{1,9},{2,10},{3,11},{4,12},{5,13},{6,14},{7,15},{8,0},{9,1},... | collective-permute-start | bytes 983048 | tf_op jit(solution)/shard_map/ppermute | solution.py:1025
  231.8 24.9 %collective-permute-start.18 = (bf16[1,1280,512]{2,1,0:T(8,128)(2,1)}, bf16[1,1280,512]{2,1,0:T(8,128)(2,1)}, u32[]{:S(2)}, u32[]{:S(2)}) collective-permute-start(bf16[1,1280,512]{2,1,0:T(8,128)(2,1)} %get-tuple-element.152), channel_id=1, source_target_pairs={{0,2},{1,5},{2,0},{3,7},{4,6},{5,1},{6,4},{7,3},{8,10},{9,13},{10,... | collective-permute-start | bytes 3932168 | tf_op jit(solution)/shard_map/ppermute | solution.py:1025
  252.8 80.4 %collective-permute-start.31 = (bf16[1024,512]{1,0:T(8,128)(2,1)}, bf16[1024,512]{1,0:T(8,128)(2,1)}, u32[]{:S(2)}, u32[]{:S(2)}) collective-permute-start(bf16[1024,512]{1,0:T(8,128)(2,1)} %get-tuple-element.175), channel_id=1, source_target_pairs={{0,16},{16,0},{1,17},{17,1},{2,18},{18,2},{3,19},{19,3},{4,20},{20... | collective-permute-start | bytes 3145736 | tf_op jit(solution)/shard_map/ppermute | solution.py:1025
  258.4 14.3 %collective-permute-start.22 = (bf16[1,640,512]{2,1,0:T(8,128)(2,1)S(1)}, bf16[1,640,512]{2,1,0:T(8,128)(2,1)S(1)}, u32[]{:S(2)}, u32[]{:S(2)}) collective-permute-start(bf16[1,640,512]{2,1,0:T(8,128)(2,1)S(1)} %get-tuple-element.161), channel_id=1, source_target_pairs={{0,4},{1,3},{2,6},{3,1},{4,0},{5,7},{6,2},{7,5},{8,12},{9,11},{10,... | collective-permute-start | bytes 1966088 | tf_op jit(solution)/shard_map/ppermute | solution.py:1025
  260.2 15.0 %collective-permute-start.21 = (bf16[1,576,512]{2,1,0:T(8,128)(2,1)S(1)}, bf16[1,576,512]{2,1,0:T(8,128)(2,1)S(1)}, u32[]{:S(2)}, u32[]{:S(2)}) collective-permute-start(bf16[1,576,512]{2,1,0:T(8,128)(2,1)S(1)} %get-tuple-element.160), channel_id=1, source_target_pairs={{0,2},{1,5},{2,0},{3,7},{4,6},{5,1},{6,4},{7,3},{8,10},{9,13},{10,... | collective-permute-start | bytes 1769480 | tf_op jit(solution)/shard_map/ppermute | solution.py:1025
  273.4 16.9 %collective-permute-start.24 = (bf16[1,320,512]{2,1,0:T(8,128)(2,1)S(1)}, bf16[1,320,512]{2,1,0:T(8,128)(2,1)S(1)}, u32[]{:S(2)}, u32[]{:S(2)}) collective-permute-start(bf16[1,320,512]{2,1,0:T(8,128)(2,1)S(1)} %get-tuple-element.165), channel_id=1, source_target_pairs={{0,8},{1,9},{2,10},{3,11},{4,12},{5,13},{6,14},{7,15},{8,0},{9,1},... | collective-permute-start | bytes 983048 | tf_op jit(solution)/shard_map/ppermute | solution.py:1025
  276.5 15.8 %collective-permute-start.23 = (bf16[2,288,512]{2,1,0:T(8,128)(2,1)S(1)}, bf16[2,288,512]{2,1,0:T(8,128)(2,1)S(1)}, u32[]{:S(2)}, u32[]{:S(2)}) collective-permute-start(bf16[2,288,512]{2,1,0:T(8,128)(2,1)S(1)} %get-tuple-element.164), channel_id=1, source_target_pairs={{0,4},{1,3},{2,6},{3,1},{4,0},{5,7},{6,2},{7,5},{8,12},{9,11},{10,... | collective-permute-start | bytes 1769480 | tf_op jit(solution)/shard_map/ppermute | solution.py:1025
  300.3 16.1 %collective-permute-start.27 = (bf16[144,512]{1,0:T(8,128)(2,1)S(1)}, bf16[144,512]{1,0:T(8,128)(2,1)S(1)}, u32[]{:S(2)}, u32[]{:S(2)}) collective-permute-start(bf16[144,512]{1,0:T(8,128)(2,1)S(1)} %get-tuple-element.171), channel_id=1, source_target_pairs={{0,24},{1,25},{2,26},{3,27},{4,28},{5,29},{6,30},{7,31},{8,16},{9,... | collective-permute-start | bytes 442376 | tf_op jit(solution)/shard_map/ppermute | solution.py:1155
  300.4 24.7 %collective-permute-start.30 = (bf16[320,512]{1,0:T(8,128)(2,1)S(1)}, bf16[320,512]{1,0:T(8,128)(2,1)S(1)}, u32[]{:S(2)}, u32[]{:S(2)}) collective-permute-start(bf16[320,512]{1,0:T(8,128)(2,1)S(1)} %shard_map.259.refs_4_.refs_1_), channel_id=1, source_target_pairs={{0,8},{1,9},{2,10},{3,11},{4,12},{5,13},{6,14},{7,15},{8,0},{9,1},... | collective-permute-start | bytes 983048 | tf_op jit(solution)/shard_map/ppermute | solution.py:1025
  316.4 11.8 %collective-permute-start.29 = (bf16[144,512]{1,0:T(8,128)(2,1)S(1)}, bf16[144,512]{1,0:T(8,128)(2,1)S(1)}, u32[]{:S(2)}, u32[]{:S(2)}) collective-permute-start(bf16[144,512]{1,0:T(8,128)(2,1)S(1)} %shard_map.260.refs_3_.refs_1_), channel_id=1, source_target_pairs={{0,8},{1,9},{2,10},{3,11},{4,12},{5,13},{6,14},{7,15},{8,0},{9,1},... | collective-permute-start | bytes 442376 | tf_op jit(solution)/shard_map/ppermute | solution.py:1025
  325.7 11.8 %collective-permute-start.33 = (bf16[640,512]{1,0:T(8,128)(2,1)S(1)}, bf16[640,512]{1,0:T(8,128)(2,1)S(1)}, u32[]{:S(2)}, u32[]{:S(2)}) collective-permute-start(bf16[640,512]{1,0:T(8,128)(2,1)S(1)} %shard_map.261.refs_3_.refs_1_), channel_id=1, source_target_pairs={{0,4},{1,3},{2,6},{3,1},{4,0},{5,7},{6,2},{7,5},{8,12},{9,11},{10,... | collective-permute-start | bytes 1966088 | tf_op jit(solution)/shard_map/ppermute | solution.py:1025
  338.2 16.8 %collective-permute-start.35 = (bf16[1280,512]{1,0:T(8,128)(2,1)S(1)}, bf16[1280,512]{1,0:T(8,128)(2,1)S(1)}, u32[]{:S(2)}, u32[]{:S(2)}) collective-permute-start(bf16[1280,512]{1,0:T(8,128)(2,1)S(1)} %shard_map.265.refs_3_.refs_1_), channel_id=1, source_target_pairs={{0,2},{1,5},{2,0},{3,7},{4,6},{5,1},{6,4},{7,3},{8,10},{9,13},{10,... | collective-permute-start | bytes 3932168 | tf_op jit(solution)/shard_map/ppermute | solution.py:1025
  339.3 22.1 %collective-permute-start.34 = (bf16[576,512]{1,0:T(8,128)(2,1)S(1)}, bf16[576,512]{1,0:T(8,128)(2,1)S(1)}, u32[]{:S(2)}, u32[]{:S(2)}) collective-permute-start(bf16[576,512]{1,0:T(8,128)(2,1)S(1)} %shard_map.266.refs_3_.refs_1_), channel_id=1, source_target_pairs={{0,2},{1,5},{2,0},{3,7},{4,6},{5,1},{6,4},{7,3},{8,10},{9,13},{10,... | collective-permute-start | bytes 1769480 | tf_op jit(solution)/shard_map/ppermute | solution.py:1025
  (80 other events, 850.8 us)
Sparse Core Ops, SparseCore 0:
  28.5 45.1 all-gather.2
